TPU v7x, 32 devices: a whole 2x2x4 slice. The times are simulated.
32 devices in a mesh: cell: 16 (over z, y, core), seq: 2 (over x).
Axes of the slice: x: 2, y: 2, z: 4, core: 2. Of those that a mesh axis runs over, the one named last changes fastest.
Arguments:
- tokens: bfloat16 [16, 1024, 1280], P('cell', 'seq'), may hold values from -6 to 6
- out_grad: bfloat16 [16, 1024, 1280], P('cell', 'seq'), may hold values from -6 to 6
- query_counts: int32 [16], P('cell'), may hold values from 50 to 2000
- first_gain: bfloat16 [1280], P('seq'), may hold values from 0.25 to 1.75
- first_bias: bfloat16 [1280], P('seq'), may hold values from -1 to 1
- query_weight: bfloat16 [1280, 1280], P('seq'), may hold values from -0.15625 to 0.15625
- query_bias: bfloat16 [1280], P('seq'), may hold values from -1 to 1
- key_weight: bfloat16 [1280, 1280], P('seq'), may hold values from -0.15625 to 0.15625
- value_weight: bfloat16 [1280, 1280], P('seq'), may hold values from -0.15625 to 0.15625
- value_bias: bfloat16 [1280], P('seq'), may hold values from -1 to 1
- output_weight: bfloat16 [1280, 1280], P('seq'), may hold values from -2.5 to 2.5
- output_bias: bfloat16 [1280], P('seq'), may hold values from -1 to 1
- second_gain: bfloat16 [1280], P('seq'), may hold values from 0.25 to 1.75
- second_bias: bfloat16 [1280], P('seq'), may hold values from -1 to 1
- up_weight: bfloat16 [1280, 5120], P('seq'), may hold values from -0.15625 to 0.15625
- up_bias: bfloat16 [5120], P('seq'), may hold values from -1 to 1
- down_weight: bfloat16 [5120, 1280], P('seq'), may hold values from -0.078125 to 0.078125
- down_bias: bfloat16 [1280], P('seq'), may hold values from -1 to 1
Outputs:
- result: bfloat16 [16, 1024, 1280], P('cell', 'seq')
- input_grad: bfloat16 [16, 1024, 1280], P('cell', 'seq')
- grad_first_gain: float32 [1280], P('seq')
- grad_first_bias: float32 [1280], P('seq')
- grad_query_weight: float32 [1280, 1280], P('seq')
- grad_query_bias: float32 [1280], P('seq')
- grad_key_weight: float32 [1280, 1280], P('seq')
- grad_value_weight: float32 [1280, 1280], P('seq')
- grad_value_bias: float32 [1280], P('seq')
- grad_output_weight: float32 [1280, 1280], P('seq')
- grad_output_bias: float32 [1280], P('seq')
- grad_second_gain: float32 [1280], P('seq')
- grad_second_bias: float32 [1280], P('seq')
- grad_up_weight: float32 [1280, 5120], P('seq')
- grad_up_bias: float32 [5120], P('seq')
- grad_down_weight: float32 [5120, 1280], P('seq')
- grad_down_bias: float32 [1280], P('seq')
All inputs are finite; a program needn't handle non-finite values.
Results may differ from a plain program's by a relative error of at most 0.019.
Values may be sent and summed in bfloat16 or wider, within the bound.
A program may use at most 320 MiB of HBM per device.

v0:
```python
import jax
import jax.numpy as jnp
from jax import lax
from jax.sharding import PartitionSpec as P

HEADS = 20
HDIM = 64


def from_behind(value, axis, steps):
    count = lax.axis_size(axis)
    pairs = [(source, (source + steps) % count) for source in range(count)]
    return lax.ppermute(value, axis, pairs)


def for_sending(x):
    return jax.tree.map(lambda a: a.astype(jnp.bfloat16) if a.dtype == jnp.float32 else a, x)


def matmul(left, right):
    return jnp.dot(left, right, preferred_element_type=jnp.float32)


def matmul_right_t(left, right):
    return jnp.einsum("to,io->ti", left, right, preferred_element_type=jnp.float32)


def weight_grad(left, right):
    return jnp.einsum("ti,to->io", left, right, preferred_element_type=jnp.float32)


def standardize(values):
    average = jnp.mean(values, axis=-1, keepdims=True)
    centred = values - average
    inverse = lax.rsqrt(jnp.mean(centred * centred, axis=-1, keepdims=True) + 1e-05)
    return (centred * inverse, inverse)


def standardize_back(grad_normed, standard, inverse, gain_vec):
    scaled = grad_normed * gain_vec
    return inverse * (
        scaled
        - jnp.mean(scaled, axis=-1, keepdims=True)
        - standard * jnp.mean(scaled * standard, axis=-1, keepdims=True)
    )


def gelu_value(up_proj):
    return 0.5 * up_proj * (1.0 + lax.erf(up_proj * 0.7071067811865476))


def gelu_slope(up_proj):
    return (
        0.5 * (1.0 + lax.erf(up_proj * 0.7071067811865476))
        + up_proj * jnp.exp(-0.5 * up_proj * up_proj) * 0.3989422804014327
    )


def score_block(queries, key_rows):
    return (
        jnp.einsum("cqhd,ckhd->chqk", queries, key_rows, preferred_element_type=jnp.float32) * 0.125
    )


def column_sum(values):
    return jnp.sum(values.astype(jnp.float32), axis=0)


def per_device(
    tokens,
    out_grad,
    query_counts,
    first_gain,
    first_bias,
    query_weight,
    query_bias,
    key_weight,
    value_weight,
    value_bias,
    output_weight,
    output_bias,
    second_gain,
    second_bias,
    up_weight,
    up_bias,
    down_weight,
    down_bias,
):
    (
        first_gain,
        first_bias,
        query_weight,
        query_bias,
        key_weight,
        value_weight,
        value_bias,
        output_weight,
        output_bias,
        second_gain,
        second_bias,
        up_weight,
        up_bias,
        down_weight,
        down_bias,
    ) = (
        lax.all_gather(first_gain, "seq", axis=0, tiled=True),
        lax.all_gather(first_bias, "seq", axis=0, tiled=True),
        lax.all_gather(query_weight, "seq", axis=0, tiled=True),
        lax.all_gather(query_bias, "seq", axis=0, tiled=True),
        lax.all_gather(key_weight, "seq", axis=0, tiled=True),
        lax.all_gather(value_weight, "seq", axis=0, tiled=True),
        lax.all_gather(value_bias, "seq", axis=0, tiled=True),
        lax.all_gather(output_weight, "seq", axis=0, tiled=True),
        lax.all_gather(output_bias, "seq", axis=0, tiled=True),
        lax.all_gather(second_gain, "seq", axis=0, tiled=True),
        lax.all_gather(second_bias, "seq", axis=0, tiled=True),
        lax.all_gather(up_weight, "seq", axis=0, tiled=True),
        lax.all_gather(up_bias, "seq", axis=0, tiled=True),
        lax.all_gather(down_weight, "seq", axis=0, tiled=True),
        lax.all_gather(down_bias, "seq", axis=0, tiled=True),
    )
    f32 = jnp.float32
    bf16 = jnp.bfloat16
    gain_first = first_gain.astype(f32)
    gain_second = second_gain.astype(f32)
    cell_count, seg_len, model_width = tokens.shape
    row_count = cell_count * seg_len
    head_shape = (cell_count, seg_len, HEADS, HDIM)
    cycle_size = lax.axis_size("seq")
    flat_input = tokens.reshape(row_count, model_width).astype(f32)
    standard_one, inverse_one = standardize(flat_input)
    normed_one = (standard_one * gain_first + first_bias.astype(f32)).astype(bf16)
    query_heads = (
        (matmul(normed_one, query_weight) + query_bias.astype(f32)).astype(bf16).reshape(head_shape)
    )
    key_heads = matmul(normed_one, key_weight).astype(bf16).reshape(head_shape)
    value_heads = (
        (matmul(normed_one, value_weight) + value_bias.astype(f32)).astype(bf16).reshape(head_shape)
    )
    running_max = jnp.full((cell_count, HEADS, seg_len), -1e30, f32)
    running_sum = jnp.zeros((cell_count, HEADS, seg_len), f32)
    weighted = jnp.zeros((cell_count, HEADS, seg_len, HDIM), f32)
    travel = (key_heads, value_heads)
    for step in range(cycle_size):
        if step > 0:
            travel = from_behind((travel[0], travel[1]), "seq", 1)
        scores = score_block(query_heads, travel[0])
        new_max = jnp.maximum(running_max, jnp.max(scores, axis=-1))
        rescale = jnp.exp(running_max - new_max)
        exp_scores = jnp.exp(scores - new_max[..., None])
        running_sum = running_sum * rescale + jnp.sum(exp_scores, axis=-1)
        weighted = weighted * rescale[..., None] + jnp.einsum(
            "chqk,ckhd->chqd", exp_scores.astype(bf16), travel[1], preferred_element_type=f32
        )
        running_max = new_max
    attended = weighted / running_sum[..., None]
    log_total = running_max + jnp.log(running_sum)
    mixed = attended.transpose(0, 2, 1, 3).reshape(row_count, model_width).astype(bf16)
    middle = flat_input + matmul(mixed, output_weight) + output_bias.astype(f32)
    standard_two, inverse_two = standardize(middle)
    normed_two = (standard_two * gain_second + second_bias.astype(f32)).astype(bf16)
    up_proj = matmul(normed_two, up_weight) + up_bias.astype(f32)
    hidden = gelu_value(up_proj).astype(bf16)
    result = middle + matmul(hidden, down_weight) + down_bias.astype(f32)
    result_out = result.astype(bf16).reshape(cell_count, seg_len, model_width)
    weight_cell = jnp.sqrt(query_counts.astype(f32) / 1000.0)
    grad_result = (out_grad.astype(f32) * weight_cell[:, None, None]).reshape(
        row_count, model_width
    )
    grad_ffn_out = grad_result.astype(bf16)
    grad_down_weight = weight_grad(hidden, grad_ffn_out)
    grad_down_bias = column_sum(grad_ffn_out)
    grad_up = (matmul_right_t(grad_ffn_out, down_weight) * gelu_slope(up_proj)).astype(bf16)
    grad_up_weight = weight_grad(normed_two, grad_up)
    grad_up_bias = column_sum(grad_up)
    grad_normed_two = matmul_right_t(grad_up, up_weight)
    grad_second_gain = jnp.sum(grad_normed_two * standard_two, axis=0)
    grad_second_bias = jnp.sum(grad_normed_two, axis=0)
    grad_middle = grad_result + standardize_back(
        grad_normed_two, standard_two, inverse_two, gain_second
    )
    grad_attn_out = grad_middle.astype(bf16)
    grad_output_weight = weight_grad(mixed, grad_attn_out)
    grad_output_bias = column_sum(grad_attn_out)
    grad_mixed = matmul_right_t(grad_attn_out, output_weight).astype(bf16).reshape(head_shape)
    row_delta = jnp.sum(grad_mixed.astype(f32).transpose(0, 2, 1, 3) * attended, axis=-1)
    grad_query_acc = jnp.zeros(head_shape, f32)
    moving = (jnp.zeros(head_shape, f32), jnp.zeros(head_shape, f32))
    travel = (key_heads, value_heads)
    for step in range(cycle_size):
        if step > 0:
            travel = from_behind((travel[0], travel[1]), "seq", 1)
        block_keys, block_values = travel
        scores = score_block(query_heads, block_keys)
        prob_block = jnp.exp(scores - log_total[..., None])
        part_values = jnp.einsum(
            "chqk,cqhd->ckhd", prob_block.astype(bf16), grad_mixed, preferred_element_type=f32
        )
        grad_probs = jnp.einsum(
            "cqhd,ckhd->chqk", grad_mixed, block_values, preferred_element_type=f32
        )
        grad_scores = (prob_block * (grad_probs - row_delta[..., None])).astype(bf16)
        grad_query_acc = (
            grad_query_acc
            + jnp.einsum("chqk,ckhd->cqhd", grad_scores, block_keys, preferred_element_type=f32)
            * 0.125
        )
        part_keys = (
            jnp.einsum("chqk,cqhd->ckhd", grad_scores, query_heads, preferred_element_type=f32)
            * 0.125
        )
        moving = from_behind(
            (for_sending(moving[0] + part_keys), for_sending(moving[1] + part_values)), "seq", 1
        )
    grad_queries = grad_query_acc.astype(bf16).reshape(row_count, model_width)
    grad_keys = moving[0].astype(bf16).reshape(row_count, model_width)
    grad_values = moving[1].astype(bf16).reshape(row_count, model_width)
    grad_query_weight = weight_grad(normed_one, grad_queries)
    grad_query_bias = column_sum(grad_queries)
    grad_key_weight = weight_grad(normed_one, grad_keys)
    grad_value_weight = weight_grad(normed_one, grad_values)
    grad_value_bias = column_sum(grad_values)
    grad_normed_one = (
        matmul_right_t(grad_queries, query_weight)
        + matmul_right_t(grad_keys, key_weight)
        + matmul_right_t(grad_values, value_weight)
    )
    grad_first_gain = jnp.sum(grad_normed_one * standard_one, axis=0)
    grad_first_bias = jnp.sum(grad_normed_one, axis=0)
    grad_input = grad_middle + standardize_back(
        grad_normed_one, standard_one, inverse_one, gain_first
    )
    input_grad = grad_input.astype(bf16).reshape(cell_count, seg_len, model_width)
    shared_all = (
        lax.psum_scatter(
            grad_first_gain.astype(jnp.bfloat16), "seq", scatter_dimension=0, tiled=True
        ).astype(jnp.float32),
        lax.psum_scatter(
            grad_first_bias.astype(jnp.bfloat16), "seq", scatter_dimension=0, tiled=True
        ).astype(jnp.float32),
        lax.psum_scatter(
            grad_query_weight.astype(jnp.bfloat16), "seq", scatter_dimension=0, tiled=True
        ).astype(jnp.float32),
        lax.psum_scatter(
            grad_query_bias.astype(jnp.bfloat16), "seq", scatter_dimension=0, tiled=True
        ).astype(jnp.float32),
        lax.psum_scatter(
            grad_key_weight.astype(jnp.bfloat16), "seq", scatter_dimension=0, tiled=True
        ).astype(jnp.float32),
        lax.psum_scatter(
            grad_value_weight.astype(jnp.bfloat16), "seq", scatter_dimension=0, tiled=True
        ).astype(jnp.float32),
        lax.psum_scatter(
            grad_value_bias.astype(jnp.bfloat16), "seq", scatter_dimension=0, tiled=True
        ).astype(jnp.float32),
        lax.psum_scatter(
            grad_output_weight.astype(jnp.bfloat16), "seq", scatter_dimension=0, tiled=True
        ).astype(jnp.float32),
        lax.psum_scatter(
            grad_output_bias.astype(jnp.bfloat16), "seq", scatter_dimension=0, tiled=True
        ).astype(jnp.float32),
        lax.psum_scatter(
            grad_second_gain.astype(jnp.bfloat16), "seq", scatter_dimension=0, tiled=True
        ).astype(jnp.float32),
        lax.psum_scatter(
            grad_second_bias.astype(jnp.bfloat16), "seq", scatter_dimension=0, tiled=True
        ).astype(jnp.float32),
        lax.psum_scatter(
            grad_up_weight.astype(jnp.bfloat16), "seq", scatter_dimension=0, tiled=True
        ).astype(jnp.float32),
        lax.psum_scatter(
            grad_up_bias.astype(jnp.bfloat16), "seq", scatter_dimension=0, tiled=True
        ).astype(jnp.float32),
        lax.psum_scatter(
            grad_down_weight.astype(jnp.bfloat16), "seq", scatter_dimension=0, tiled=True
        ).astype(jnp.float32),
        lax.psum_scatter(
            grad_down_bias.astype(jnp.bfloat16), "seq", scatter_dimension=0, tiled=True
        ).astype(jnp.float32),
    )
    (
        grad_first_gain,
        grad_first_bias,
        grad_query_weight,
        grad_query_bias,
        grad_key_weight,
        grad_value_weight,
        grad_value_bias,
        grad_output_weight,
        grad_output_bias,
        grad_second_gain,
        grad_second_bias,
        grad_up_weight,
        grad_up_bias,
        grad_down_weight,
        grad_down_bias,
    ) = shared_all
    (
        grad_first_gain,
        grad_first_bias,
        grad_query_weight,
        grad_query_bias,
        grad_key_weight,
        grad_value_weight,
        grad_value_bias,
        grad_output_weight,
        grad_output_bias,
        grad_second_gain,
        grad_second_bias,
        grad_up_weight,
        grad_up_bias,
        grad_down_weight,
        grad_down_bias,
    ) = (
        lax.psum(grad_first_gain.astype(jnp.bfloat16), "cell").astype(jnp.float32),
        lax.psum(grad_first_bias.astype(jnp.bfloat16), "cell").astype(jnp.float32),
        lax.psum(grad_query_weight.astype(jnp.bfloat16), "cell").astype(jnp.float32),
        lax.psum(grad_query_bias.astype(jnp.bfloat16), "cell").astype(jnp.float32),
        lax.psum(grad_key_weight.astype(jnp.bfloat16), "cell").astype(jnp.float32),
        lax.psum(grad_value_weight.astype(jnp.bfloat16), "cell").astype(jnp.float32),
        lax.psum(grad_value_bias.astype(jnp.bfloat16), "cell").astype(jnp.float32),
        lax.psum(grad_output_weight.astype(jnp.bfloat16), "cell").astype(jnp.float32),
        lax.psum(grad_output_bias.astype(jnp.bfloat16), "cell").astype(jnp.float32),
        lax.psum(grad_second_gain.astype(jnp.bfloat16), "cell").astype(jnp.float32),
        lax.psum(grad_second_bias.astype(jnp.bfloat16), "cell").astype(jnp.float32),
        lax.psum(grad_up_weight.astype(jnp.bfloat16), "cell").astype(jnp.float32),
        lax.psum(grad_up_bias.astype(jnp.bfloat16), "cell").astype(jnp.float32),
        lax.psum(grad_down_weight.astype(jnp.bfloat16), "cell").astype(jnp.float32),
        lax.psum(grad_down_bias.astype(jnp.bfloat16), "cell").astype(jnp.float32),
    )
    return (
        result_out,
        input_grad,
        grad_first_gain,
        grad_first_bias,
        grad_query_weight,
        grad_query_bias,
        grad_key_weight,
        grad_value_weight,
        grad_value_bias,
        grad_output_weight,
        grad_output_bias,
        grad_second_gain,
        grad_second_bias,
        grad_up_weight,
        grad_up_bias,
        grad_down_weight,
        grad_down_bias,
    )


def solution(mesh):
    placed = (
        P("cell", "seq", None),
        P("cell", "seq", None),
        P("cell"),
        P("seq"),
        P("seq"),
        P("seq", None),
        P("seq"),
        P("seq", None),
        P("seq", None),
        P("seq"),
        P("seq", None),
        P("seq"),
        P("seq"),
        P("seq"),
        P("seq", None),
        P("seq"),
        P("seq", None),
        P("seq"),
    )
    return jax.shard_map(
        per_device,
        mesh=mesh,
        in_specs=placed,
        out_specs=(
            P("cell", "seq", None),
            P("cell", "seq", None),
            P("seq"),
            P("seq"),
            P("seq", None),
            P("seq"),
            P("seq", None),
            P("seq", None),
            P("seq"),
            P("seq", None),
            P("seq"),
            P("seq"),
            P("seq"),
            P("seq", None),
            P("seq"),
            P("seq", None),
            P("seq"),
        ),
        check_vma=False,
    )
```

profile of v0, /device:TPU:0, one launch (start us, length us, event | category | flops | bytes accessed | tf_op | source)
XLA Modules:
  0.0 1622.7 jit_solution(10952334343229256608)
XLA Ops:
  49.8 9.4 all-gather.16.cloned.1.call-done
  66.0 41.2 %all-gather.18.cloned.1.call-done = bf16[1280,1280]{1,0:T(8,128)(2,1)} async-done(((bf16[640,1280]{1,0:T(8,128)(2,1)}), bf16[1280,1280]{1,0:T(8,128)(2,1)}) %all-gather.18.cloned.1.call-update) | async-done | bytes 3276816 | tf_op jit(solution)/shard_map/all_gather | solution.py:110
  115.0 65.8 %all-gather.20.cloned.1.call-done = bf16[1280,1280]{1,0:T(8,128)(2,1)} async-done(((bf16[640,1280]{1,0:T(8,128)(2,1)}), bf16[1280,1280]{1,0:T(8,128)(2,1)}) %all-gather.20.cloned.1.call-update) | async-done | bytes 3276816 | tf_op jit(solution)/shard_map/all_gather | solution.py:111
  193.1 11.7 multiply_reduce_fusion
  206.8 10.8 fusion
  217.7 9.3 fusion.18
  227.0 19.0 %collective-permute-done.1 = bf16[1,512,20,64]{1,3,2,0:T(8,128)(2,1)} collective-permute-done((bf16[1,512,20,64]{1,3,2,0:T(8,128)(2,1)}, bf16[1,512,20,64]{1,3,2,0:T(8,128)(2,1)}, u32[]{:S(2)}, u32[]{:S(2)}) %collective-permute-start.1) | collective-permute-done | bytes 1310752 | tf_op jit(solution)/shard_map/ppermute | solution.py:13
  246.0 11.0 bitcast_convert_fusion.1
  263.4 150.8 %all-gather.24.cloned.1.call-done = bf16[1280,5120]{1,0:T(8,128)(2,1)} async-done(((bf16[640,5120]{1,0:T(8,128)(2,1)}), bf16[1280,5120]{1,0:T(8,128)(2,1)}) %all-gather.24.cloned.1.call-update) | async-done | bytes 13107216 | tf_op jit(solution)/shard_map/all_gather | solution.py:117
  414.2 16.4 %multiply_convert_fusion.2 = (bf16[512,5120]{1,0:T(8,128)(2,1)}, f32[512,5120]{1,0:T(8,128)}) fusion(f32[5120]{0:T(1024)S(1)} %bitcast.191, bf16[1280,5120]{1,0:T(8,128)(2,1)} %all-gather.24.cloned.1.call-done, f32[512,1280]{1,0:T(8,128)} %copy-done.1, f32[1280]{0:T(1024)S(1)} %reshape.442, f32[1280]{0:T(1024)S(1)} %reshape.441, f32[512]{0:T(512)S(1)} %add_rsqrt_fusion, ...), kind=kOutput, calls=%fused_computation.29 | convolution fusion | flops 6729891840 | bytes 31492096 | tf_op jit(solution)/shard_map/dot_general | solution.py:21
  430.6 143.3 %all-gather.26.cloned.1.call-done = bf16[5120,1280]{1,0:T(8,128)(2,1)} async-done(((bf16[2560,1280]{1,0:T(8,128)(2,1)}), bf16[5120,1280]{1,0:T(8,128)(2,1)}) %all-gather.26.cloned.1.call-update) | async-done | bytes 13107216 | tf_op jit(solution)/shard_map/all_gather | solution.py:119
  574.0 16.4 %fusion.93 = (bf16[5120]{0:T(1024)(128)(2,1)}, bf16[512,5120]{1,0:T(8,128)(2,1)}) fusion(f32[512,5120]{1,0:T(8,128)} %get-tuple-element.67, f32[5120]{0:T(1024)S(1)} %bitcast.192, bf16[5120,1280]{1,0:T(8,128)(2,1)} %all-gather.26.cloned.1.call-done, bf16[1,512,1280]{2,1,0:T(8,128)(2,1)S(1)} %copy-done.18, f32[]{:T(128)} %bitcast.13), kind=kOutput, calls=%fused_computation.141 | convolution fusion | flops 6744304640 | bytes 30177284 | tf_op jit(solution)/shard_map/to,io->ti/dot_general | solution.py:25
  590.4 15.7 multiply_reduce_fusion.2
  629.0 12.3 multiply_convert_fusion.1
  647.3 12.6 multiply_convert_fusion
  671.5 7.2 fusion.62
  679.1 59.1 %collective-permute-done.2 = bf16[1,512,20,64]{1,3,2,0:T(8,128)(2,1)S(1)} collective-permute-done((bf16[1,512,20,64]{1,3,2,0:T(8,128)(2,1)S(1)}, bf16[1,512,20,64]{1,3,2,0:T(8,128)(2,1)S(1)}, u32[]{:S(2)}, u32[]{:S(2)}) %collective-permute-start.2) | collective-permute-done | bytes 1310752 | tf_op jit(solution)/shard_map/ppermute | solution.py:13
  738.2 7.3 fusion.55
  745.7 29.6 %collective-permute-done.3 = bf16[1,512,20,64]{1,3,2,0:T(8,128)(2,1)S(1)} collective-permute-done((bf16[1,512,20,64]{1,3,2,0:T(8,128)(2,1)S(1)}, bf16[1,512,20,64]{1,3,2,0:T(8,128)(2,1)S(1)}, u32[]{:S(2)}, u32[]{:S(2)}) %collective-permute-start.3) | collective-permute-done | bytes 1310752 | tf_op jit(solution)/shard_map/ppermute | solution.py:13
  780.5 10.1 fusion.63
  790.6 58.5 %collective-permute-done.4 = bf16[1,512,20,64]{1,3,2,0:T(8,128)(2,1)S(1)} collective-permute-done((bf16[1,512,20,64]{1,3,2,0:T(8,128)(2,1)S(1)}, bf16[1,512,20,64]{1,3,2,0:T(8,128)(2,1)S(1)}, u32[]{:S(2)}, u32[]{:S(2)}) %collective-permute-start.4) | collective-permute-done | bytes 1310752 | tf_op jit(solution)/shard_map/ppermute | solution.py:13
  849.1 9.4 fusion.54
  858.7 26.9 %collective-permute-done.5 = bf16[1,512,20,64]{1,3,2,0:T(8,128)(2,1)S(1)} collective-permute-done((bf16[1,512,20,64]{1,3,2,0:T(8,128)(2,1)S(1)}, bf16[1,512,20,64]{1,3,2,0:T(8,128)(2,1)S(1)}, u32[]{:S(2)}, u32[]{:S(2)}) %collective-permute-start.5) | collective-permute-done | bytes 1310752 | tf_op jit(solution)/shard_map/ppermute | solution.py:13
  892.4 12.8 convolution_convert_fusion.1
  905.3 12.1 convolution_convert_fusion
  917.6 18.0 %reduce-scatter.11.cloned.1.call-done = bf16[640,1280]{1,0:T(8,128)(2,1)} async-done(((bf16[1280,1280]{1,0:T(8,128)(2,1)}), bf16[640,1280]{1,0:T(8,128)(2,1)}) %reduce-scatter.11.cloned.1.call-update) | async-done | bytes 1638416 | tf_op jit(solution)/shard_map/reduce_scatter | solution.py:250
  935.6 153.0 %reduce-scatter.15.cloned.1.call-done = bf16[640,5120]{1,0:T(8,128)(2,1)} async-done(((bf16[1280,5120]{1,0:T(8,128)(2,1)}), bf16[640,5120]{1,0:T(8,128)(2,1)}) %reduce-scatter.15.cloned.1.call-update) | async-done | bytes 6553616 | tf_op jit(solution)/shard_map/reduce_scatter | solution.py:268
  1088.6 152.9 %reduce-scatter.17.cloned.1.call-done = bf16[2560,1280]{1,0:T(8,128)(2,1)} async-done(((bf16[5120,1280]{1,0:T(8,128)(2,1)}), bf16[2560,1280]{1,0:T(8,128)(2,1)}) %reduce-scatter.17.cloned.1.call-update) | async-done | bytes 6553616 | tf_op jit(solution)/shard_map/reduce_scatter | solution.py:274
  1254.4 13.6 fusion.40
  1279.2 7.9 all-reduce.11
  1287.9 63.5 %all-reduce.9 = (bf16[640]{0:T(1024)(128)(2,1)S(1)}, bf16[640]{0:T(1024)(128)(2,1)S(1)}, bf16[640]{0:T(1024)(128)(2,1)S(1)}, bf16[640]{0:T(1024)(128)(2,1)S(1)},...) all-reduce(bf16[640]{0:T(1024)(128)(2,1)S(1)} %dynamic-slice.1, ...), channel_id=1, replica_groups=mesh['cell'=16,'seq'=2] {'cell'}, use_global_device_ids=true, to_apply=%region_15.0 | all-reduce | flops 7680 | bytes 30720 | tf_op jit(solution)/shard_map/psum | solution.py:315
  1361.3 231.1 %all-reduce.14.cloned.1.call-done = (bf16[640,1280]{1,0:T(8,128)(2,1)}, bf16[640,1280]{1,0:T(8,128)(2,1)}, bf16[640,1280]{1,0:T(8,128)(2,1)}, bf16[640,1280]{1,0...) async-done(((bf16[640,1280]{1,0:T(8,128)(2,1)}, bf16[640,1280]{1,0:T(8,128)(2,1)}, bf16[640,1280]{1,0:T(8,128)(2,1)}, bf16[640,1280]{1,0:T(8,128)(2,1)}, ...) | async-done | bytes 19660816 | tf_op jit(solution)/shard_map/psum | solution.py:317
  (218 shorter events, 187.4 us)
Async XLA Ops:
  7.2 52.0 %all-gather.16.cloned.1.call-start = ((), (), s32[]{:S(2)}) async-start(), calls=%async_computation.6 | async-start | bytes 4915200 | tf_op jit(solution)/shard_map/all_gather | solution.py:108
  7.9 99.3 %all-gather.18.cloned.1.call-start = ((), (), s32[]{:S(2)}) async-start(), calls=%async_computation.7 | async-start | bytes 4915200 | tf_op jit(solution)/shard_map/all_gather | solution.py:110
  8.7 172.1 %all-gather.20.cloned.1.call-start = ((), (), s32[]{:S(2)}) async-start(), calls=%async_computation.8 | async-start | bytes 4915200 | tf_op jit(solution)/shard_map/all_gather | solution.py:111
  9.4 247.5 %all-gather.22.cloned.1.call-start = ((), (), s32[]{:S(2)}) async-start(), calls=%async_computation.9 | async-start | bytes 4915200 | tf_op jit(solution)/shard_map/all_gather | solution.py:113
  10.0 404.2 %all-gather.24.cloned.1.call-start = ((), (), s32[]{:S(2)}) async-start(), calls=%async_computation.10 | async-start | bytes 19660800 | tf_op jit(solution)/shard_map/all_gather | solution.py:117
  10.6 563.4 %all-gather.26.cloned.1.call-start = ((), (), s32[]{:S(2)}) async-start(), calls=%async_computation.11 | async-start | bytes 19660800 | tf_op jit(solution)/shard_map/all_gather | solution.py:119
  11.2 11.1 copy-start.27
  11.2 15.5 copy-start.28
  11.2 19.9 %copy-start.29 = (bf16[640]{0:T(1024)(128)(2,1)S(1)}, bf16[640]{0:T(1024)(128)(2,1)}, u32[]{:S(2)}) copy-start(bf16[640]{0:T(1024)(128)(2,1)} %param.29) | copy-start | bytes 3844
  11.2 24.3 %copy-start.30 = (bf16[640]{0:T(1024)(128)(2,1)S(1)}, bf16[640]{0:T(1024)(128)(2,1)}, u32[]{:S(2)}) copy-start(bf16[640]{0:T(1024)(128)(2,1)} %param.30) | copy-start | bytes 3844
  11.2 28.7 %copy-start.31 = (bf16[640]{0:T(1024)(128)(2,1)S(1)}, bf16[640]{0:T(1024)(128)(2,1)}, u32[]{:S(2)}) copy-start(bf16[640]{0:T(1024)(128)(2,1)} %param.31) | copy-start | bytes 3844
  11.2 33.9 %copy-start.22 = (bf16[2560]{0:T(1024)(128)(2,1)S(1)}, bf16[2560]{0:T(1024)(128)(2,1)}, u32[]{:S(2)}) copy-start(bf16[2560]{0:T(1024)(128)(2,1)} %param.33) | copy-start | bytes 15364
  11.2 906.3 %reduce-scatter.13.cloned.1.call-start = ((), (), s32[]{:S(2)}) async-start(), calls=%async_computation.15 | async-start | bytes 4915200 | tf_op jit(solution)/shard_map/reduce_scatter | solution.py:256
  114.7 78.5 %collective-permute-start = (bf16[1,512,20,64]{1,3,2,0:T(8,128)(2,1)}, bf16[1,512,20,64]{1,3,2,0:T(8,128)(2,1)}, u32[]{:S(2)}, u32[]{:S(2)}) collective-permute-start(bf16[1,512,20,64]{1,3,2,0:T(8,128)(2,1)} %bitcast.174), channel_id=1, source_target_pairs={{0,1},{1,0},{2,3},{3,2},{4,5},{5,4},{6,7},{7,6},{8,9},{9,8},{10,11... | collective-permute-start | bytes 3932168 | tf_op jit(solution)/shard_map/ppermute | solution.py:13
  188.2 57.8 %collective-permute-start.1 = (bf16[1,512,20,64]{1,3,2,0:T(8,128)(2,1)}, bf16[1,512,20,64]{1,3,2,0:T(8,128)(2,1)}, u32[]{:S(2)}, u32[]{:S(2)}) collective-permute-start(bf16[1,512,20,64]{1,3,2,0:T(8,128)(2,1)} %bitcast.177), channel_id=1, source_target_pairs={{0,1},{1,0},{2,3},{3,2},{4,5},{5,4},{6,7},{7,6},{8,9},{9,8},{10,11... | collective-permute-start | bytes 3932168 | tf_op jit(solution)/shard_map/ppermute | solution.py:13
  193.1 13.7 copy-start
  414.2 159.7 %copy-start.18 = (bf16[1,512,1280]{2,1,0:T(8,128)(2,1)S(1)}, bf16[1,512,1280]{2,1,0:T(8,128)(2,1)}, u32[]{:S(2)}) copy-start(bf16[1,512,1280]{2,1,0:T(8,128)(2,1)} %param.19) | copy-start | bytes 3932164
  615.0 302.6 %reduce-scatter.7.cloned.1.call-start = ((), (), s32[]{:S(2)}) async-start(), calls=%async_computation.12 | async-start | bytes 4915200 | tf_op jit(solution)/shard_map/reduce_scatter | solution.py:241
  629.0 12.3 copy-start.8
  659.8 7.4 copy-start.4
  671.3 246.3 %reduce-scatter.9.cloned.1.call-start = ((), (), s32[]{:S(2)}) async-start(), calls=%async_computation.13 | async-start | bytes 4915200 | tf_op jit(solution)/shard_map/reduce_scatter | solution.py:247
  678.8 97.7 %copy-start.5 = (bf16[1,512,1280]{2,1,0:T(8,128)(2,1)S(1)}, bf16[1,512,1280]{2,1,0:T(8,128)(2,1)}, u32[]{:S(2)}) copy-start(bf16[1,512,1280]{2,1,0:T(8,128)(2,1)} %param.18) | copy-start | bytes 3932164
  678.8 59.4 %collective-permute-start.2 = (bf16[1,512,20,64]{1,3,2,0:T(8,128)(2,1)S(1)}, bf16[1,512,20,64]{1,3,2,0:T(8,128)(2,1)S(1)}, u32[]{:S(2)}, u32[]{:S(2)}) collective-permute-start(bf16[1,512,20,64]{1,3,2,0:T(8,128)(2,1)S(1)} %fusion.62), channel_id=1, source_target_pairs={{0,1},{1,0},{2,3},{3,2},{4,5},{5,4},{6,7},{7,6},{8,9},{9,8},{10,11... | collective-permute-start | bytes 3932168 | tf_op jit(solution)/shard_map/ppermute | solution.py:13
  745.4 29.9 %collective-permute-start.3 = (bf16[1,512,20,64]{1,3,2,0:T(8,128)(2,1)S(1)}, bf16[1,512,20,64]{1,3,2,0:T(8,128)(2,1)S(1)}, u32[]{:S(2)}, u32[]{:S(2)}) collective-permute-start(bf16[1,512,20,64]{1,3,2,0:T(8,128)(2,1)S(1)} %fusion.55), channel_id=1, source_target_pairs={{0,1},{1,0},{2,3},{3,2},{4,5},{5,4},{6,7},{7,6},{8,9},{9,8},{10,11... | collective-permute-start | bytes 3932168 | tf_op jit(solution)/shard_map/ppermute | solution.py:13
  780.4 155.2 %reduce-scatter.11.cloned.1.call-start = ((), (), s32[]{:S(2)}) async-start(), calls=%async_computation.14 | async-start | bytes 4915200 | tf_op jit(solution)/shard_map/reduce_scatter | solution.py:250
  790.5 96.2 %copy-start.6 = (bf16[1,512,1280]{2,1,0:T(8,128)(2,1)S(1)}, bf16[1,512,1280]{2,1,0:T(8,128)(2,1)}, u32[]{:S(2)}) copy-start(bf16[1,512,1280]{2,1,0:T(8,128)(2,1)} %param.18) | copy-start | bytes 3932164
  790.5 58.5 %collective-permute-start.4 = (bf16[1,512,20,64]{1,3,2,0:T(8,128)(2,1)S(1)}, bf16[1,512,20,64]{1,3,2,0:T(8,128)(2,1)S(1)}, u32[]{:S(2)}, u32[]{:S(2)}) collective-permute-start(bf16[1,512,20,64]{1,3,2,0:T(8,128)(2,1)S(1)} %fusion.63), channel_id=1, source_target_pairs={{0,1},{1,0},{2,3},{3,2},{4,5},{5,4},{6,7},{7,6},{8,9},{9,8},{10,11... | collective-permute-start | bytes 3932168 | tf_op jit(solution)/shard_map/ppermute | solution.py:13
  858.5 27.2 %collective-permute-start.5 = (bf16[1,512,20,64]{1,3,2,0:T(8,128)(2,1)S(1)}, bf16[1,512,20,64]{1,3,2,0:T(8,128)(2,1)S(1)}, u32[]{:S(2)}, u32[]{:S(2)}) collective-permute-start(bf16[1,512,20,64]{1,3,2,0:T(8,128)(2,1)S(1)} %fusion.54), channel_id=1, source_target_pairs={{0,1},{1,0},{2,3},{3,2},{4,5},{5,4},{6,7},{7,6},{8,9},{9,8},{10,11... | collective-permute-start | bytes 3932168 | tf_op jit(solution)/shard_map/ppermute | solution.py:13
  890.7 197.9 %reduce-scatter.15.cloned.1.call-start = ((), (), s32[]{:S(2)}) async-start(), calls=%async_computation.16 | async-start | bytes 19660800 | tf_op jit(solution)/shard_map/reduce_scatter | solution.py:268
  905.3 336.2 %reduce-scatter.17.cloned.1.call-start = ((), (), s32[]{:S(2)}) async-start(), calls=%async_computation.17 | async-start | bytes 19660800 | tf_op jit(solution)/shard_map/reduce_scatter | solution.py:274
  917.5 674.9 %all-reduce.14.cloned.1.call-start = ((), (), s32[]{:S(2)}) async-start(), calls=%async_computation.18 | async-start | bytes 39321600 | tf_op jit(solution)/shard_map/psum | solution.py:317
  1601.2 8.7 slice-start
  (27 other events, 94.4 us)
Sparse Core Ops, SparseCore 0:
  9.6 49.5 all-gather.15
  60.7 46.4 all-gather.17
  108.8 71.9 all-gather.19
  182.2 72.3 all-gather.21
  255.9 158.2 all-gather.23
  415.6 158.2 all-gather.25
  615.1 44.7 reduce-scatter.12
  671.4 72.9 reduce-scatter.6
  780.5 72.8 reduce-scatter.8
  890.8 44.7 reduce-scatter.10
  938.5 150.1 reduce-scatter.14
  1091.4 150.1 reduce-scatter.16
  1246.7 345.6 all-reduce.13
where the time goes:
time: 1630 us; the launch traced here: 1620 us
  waiting for transfers between devices  1160 us (71%)
  matrix products  250 us (15%)
  blocking collectives  112 us (7%)
  other arithmetic  53 us (3%)
  local copies, waits for them, and re-layouts  25.4 us (2%)
  between operations  16.7 us (1%)
    psum x1, waiting for transfers between devices, per_device(): lax.psum(grad_query_weight.astype(jnp.bfloat16), 'cell').astype(jnp.float32)  231 us
    ppermute x6, waiting for transfers between devices, from_behind(): return lax.ppermute(value, axis, pairs)  193 us
    reduce_scatter x1, waiting for transfers between devices, per_device(): lax.psum_scatter(grad_up_weight.astype(jnp.bfloat16), 'seq', scatter_dime...  153 us
    reduce_scatter x1, waiting for transfers between devices, per_device(): lax.psum_scatter(grad_down_weight.astype(jnp.bfloat16), 'seq', scatter_di...  153 us
    all_gather x1, waiting for transfers between devices, per_device(): lax.all_gather(up_weight, 'seq', axis=0, tiled=True)  151 us
    all_gather x1, waiting for transfers between devices, per_device(): lax.all_gather(down_weight, 'seq', axis=0, tiled=True)  143 us
    all_gather x1, waiting for transfers between devices, per_device(): lax.all_gather(value_weight, 'seq', axis=0, tiled=True)  65.8 us
    psum x1, blocking collectives, per_device(): lax.psum(grad_first_gain.astype(jnp.bfloat16), 'cell').astype(jnp.float32)  63.5 us
  transfers between devices with their start and end apart: 19, of which 14 were waited for; matrix products, arithmetic and copies ran while one was open for 16% of the time, Pallas kernels for 0%

commit v1 on v0

--- a/solution.py
+++ b/solution.py
@@ -1,6 +1,8 @@
 import jax
 import jax.numpy as jnp
 from jax import lax
+from jax.experimental import pallas as pl
+from jax.experimental.pallas import tpu as pltpu
 from jax.sharding import PartitionSpec as P
 
 HEADS = 20
@@ -66,7 +68,7 @@
     return jnp.sum(values.astype(jnp.float32), axis=0)
 
 
-def per_device(
+def general(
     tokens,
     out_grad,
     query_counts,
@@ -349,6 +351,395 @@
     )
 
 
+BOTH = ("cell", "seq")
+SEQ_BIT = 1
+CORE_BIT = 2
+Q_BLOCK = 512
+VMEM = 48 * 1024 * 1024
+
+
+def across(value, bit):
+    count = lax.axis_size("cell") * lax.axis_size("seq")
+    return lax.ppermute(value, BOTH, [(i, i ^ bit) for i in range(count)])
+
+
+def across_diagonal(value):
+    count = lax.axis_size("cell") * lax.axis_size("seq")
+    pairs = [(i, i ^ 3) for i in range(count) if (i & 3) in (1, 2)]
+    return lax.ppermute(value, BOTH, pairs)
+
+
+def in_order(first, own, received, axis=0):
+    low = jnp.where(first, own, received)
+    high = jnp.where(first, received, own)
+    return jnp.concatenate([low, high], axis=axis)
+
+
+def half_of(value, index, axis=0):
+    size = value.shape[axis] // 2
+    return lax.dynamic_slice_in_dim(value, index * size, size, axis)
+
+
+class Place:
+    def __init__(self):
+        self.x = lax.axis_index("seq")
+        cell = lax.axis_index("cell")
+        self.core = cell % 2
+        self.bits = []
+        bit = 2
+        while bit < lax.axis_size("cell"):
+            self.bits.append((2 * bit, (cell // bit) % 2))
+            bit *= 2
+
+    def share(self, value):
+        for _, index in self.bits:
+            value = half_of(value, index)
+        return value
+
+    def widen(self, block):
+        for bit, index in reversed(self.bits):
+            block = in_order(index == 0, block, across(block, bit))
+        return block
+
+    def fetch(self, piece):
+        return self.widen(across(self.share(piece), SEQ_BIT))
+
+    def add_up(self, keep, give):
+        total = keep.astype(jnp.float32) + across(give, SEQ_BIT).astype(jnp.float32)
+        for bit, index in self.bits:
+            send = half_of(total, 1 - index).astype(jnp.bfloat16)
+            total = half_of(total, index) + across(send, bit).astype(jnp.float32)
+        return self.widen(total.astype(jnp.bfloat16))
+
+
+def attend_kernel(q_ref, k_ref, v_ref, mixed_ref, total_ref):
+    f32, bf16 = jnp.float32, jnp.bfloat16
+    rows, lanes = q_ref.shape
+    lane = lax.broadcasted_iota(jnp.int32, (1, lanes), 1)
+    keys = k_ref[...]
+    values_t = v_ref[...].T
+    for block in range(rows // Q_BLOCK):
+        part = pl.ds(block * Q_BLOCK, Q_BLOCK)
+        queries = q_ref[part, :] * jnp.asarray(0.125, bf16)
+        outs = []
+        for head in range(2):
+            own = (lane // HDIM) == head
+            scores = lax.dot_general(
+                keys,
+                jnp.where(own, queries, jnp.zeros_like(queries)),
+                (((1,), (1,)), ((), ())),
+                preferred_element_type=f32,
+            )
+            largest = jnp.max(scores, axis=0, keepdims=True)
+            weights = jnp.exp(scores - largest)
+            total = jnp.sum(weights, axis=0, keepdims=True)
+            mixed = jnp.dot(
+                values_t[head * HDIM : (head + 1) * HDIM, :],
+                weights.astype(bf16),
+                preferred_element_type=f32,
+            )
+            outs.append(mixed / total)
+            total_ref[head, :, part] = largest + jnp.log(total)
+        mixed_ref[part, :] = jnp.concatenate(outs, axis=0).T.astype(bf16)
+
+
+def attend_back_kernel(q_ref, k_ref, v_ref, total_ref, grad_ref, dq_ref, dk_ref, dv_ref, dk_acc, dv_acc):
+    f32, bf16 = jnp.float32, jnp.bfloat16
+    rows, lanes = q_ref.shape
+    lane = lax.broadcasted_iota(jnp.int32, (1, lanes), 1)
+    keys = k_ref[...]
+    keys_t = keys.T
+    values = v_ref[...]
+    nt = (((1,), (1,)), ((), ()))
+    for block in range(rows // Q_BLOCK):
+        part = pl.ds(block * Q_BLOCK, Q_BLOCK)
+        queries = q_ref[part, :] * jnp.asarray(0.125, bf16)
+        grads = grad_ref[part, :]
+        outs = []
+        key_part = None
+        value_part = None
+        for head in range(2):
+            own = (lane // HDIM) == head
+            q_own = jnp.where(own, queries, jnp.zeros_like(queries))
+            g_own = jnp.where(own, grads, jnp.zeros_like(grads))
+            scores = lax.dot_general(keys, q_own, nt, preferred_element_type=f32)
+            probs = jnp.exp(scores - total_ref[head, :, part])
+            grad_probs = lax.dot_general(values, g_own, nt, preferred_element_type=f32)
+            delta = jnp.sum(probs * grad_probs, axis=0, keepdims=True)
+            grad_scores = (probs * (grad_probs - delta)).astype(bf16)
+            one_value = jnp.dot(probs.astype(bf16), g_own, preferred_element_type=f32)
+            one_key = jnp.dot(grad_scores, q_own, preferred_element_type=f32)
+            value_part = one_value if head == 0 else value_part + one_value
+            key_part = one_key if head == 0 else key_part + one_key
+            outs.append(
+                jnp.dot(
+                    keys_t[head * HDIM : (head + 1) * HDIM, :],
+                    grad_scores,
+                    preferred_element_type=f32,
+                )
+            )
+        dq_ref[part, :] = (jnp.concatenate(outs, axis=0) * 0.125).T.astype(bf16)
+        if block == 0:
+            dk_acc[...] = key_part
+            dv_acc[...] = value_part
+        else:
+            dk_acc[...] += key_part
+            dv_acc[...] += value_part
+    dk_ref[...] = dk_acc[...].astype(bf16)
+    dv_ref[...] = dv_acc[...].astype(bf16)
+
+
+def attend(qkv):
+    rows, width = qkv.shape[0], qkv.shape[1] // 3
+    pairs = width // 128
+    macs = 2 * rows * rows * width
+    return pl.pallas_call(
+        attend_kernel,
+        grid=(pairs,),
+        in_specs=[
+            pl.BlockSpec((rows, 128), lambda p: (0, p)),
+            pl.BlockSpec((rows, 128), lambda p: (0, pairs + p)),
+            pl.BlockSpec((rows, 128), lambda p: (0, 2 * pairs + p)),
+        ],
+        out_specs=[
+            pl.BlockSpec((rows, 128), lambda p: (0, p)),
+            pl.BlockSpec((2, 1, rows), lambda p: (p, 0, 0)),
+        ],
+        out_shape=[
+            jax.ShapeDtypeStruct((rows, width), jnp.bfloat16),
+            jax.ShapeDtypeStruct((2 * pairs, 1, rows), jnp.float32),
+        ],
+        compiler_params=pltpu.CompilerParams(vmem_limit_bytes=VMEM),
+        cost_estimate=pl.CostEstimate(
+            flops=8 * macs, bytes_accessed=8 * rows * width, transcendentals=macs // 128
+        ),
+        name="attend",
+    )(qkv, qkv, qkv)
+
+
+def attend_back(qkv, total, grad_mixed):
+    rows, width = grad_mixed.shape
+    pairs = width // 128
+    macs = 5 * rows * rows * width
+    block = pl.BlockSpec((rows, 128), lambda p: (0, p))
+    return pl.pallas_call(
+        attend_back_kernel,
+        grid=(pairs,),
+        in_specs=[
+            block,
+            pl.BlockSpec((rows, 128), lambda p: (0, pairs + p)),
+            pl.BlockSpec((rows, 128), lambda p: (0, 2 * pairs + p)),
+            pl.BlockSpec((2, 1, rows), lambda p: (p, 0, 0)),
+            block,
+        ],
+        out_specs=[block] * 3,
+        out_shape=[jax.ShapeDtypeStruct((rows, width), jnp.bfloat16)] * 3,
+        scratch_shapes=[pltpu.VMEM((rows, 128), jnp.float32)] * 2,
+        compiler_params=pltpu.CompilerParams(vmem_limit_bytes=VMEM),
+        cost_estimate=pl.CostEstimate(
+            flops=8 * macs, bytes_accessed=14 * rows * width, transcendentals=macs // 320
+        ),
+        name="attend_back",
+    )(qkv, qkv, qkv, total, grad_mixed)
+
+
+def tuned(
+    tokens,
+    out_grad,
+    query_counts,
+    first_gain,
+    first_bias,
+    query_weight,
+    query_bias,
+    key_weight,
+    value_weight,
+    value_bias,
+    output_weight,
+    output_bias,
+    second_gain,
+    second_bias,
+    up_weight,
+    up_bias,
+    down_weight,
+    down_bias,
+):
+    f32, bf16 = jnp.float32, jnp.bfloat16
+    at = Place()
+    x, core = at.x, at.core
+    swapped = x != core
+    rows, width = tokens.shape[1:]
+    hidden_width = up_weight.shape[1] // 2
+    head_width = width // 2
+
+    vectors = (first_gain, first_bias, query_bias, value_bias, output_bias, second_gain, second_bias, down_bias, up_bias)
+    packed = jnp.concatenate(vectors)
+    packed = in_order(x == 0, packed[None], across(packed, SEQ_BIT)[None])
+    full = []
+    start = 0
+    for vector in vectors:
+        full.append(packed[:, start : start + vector.shape[0]].reshape(-1).astype(f32))
+        start += vector.shape[0]
+    gain_one, bias_one, q_bias, v_bias, o_bias, gain_two, bias_two, d_bias, u_bias = full
+
+    own = tokens[0]
+    own = jnp.where(swapped, across_diagonal(own), own)
+    own_grad = out_grad[0]
+    own_grad = jnp.where(swapped, across_diagonal(own_grad), own_grad)
+    weight_cell = jnp.broadcast_to(jnp.sqrt(query_counts.astype(f32) / 1000.0), (8, 128))
+    weight_cell = jnp.where(swapped, across_diagonal(weight_cell), weight_cell)[:1, :1]
+
+    def columns(weight):
+        return half_of(weight, core, 1)
+
+    def up_columns(weight):
+        halves = weight.reshape(weight.shape[0], 2, 2, hidden_width // 2)
+        halves = lax.dynamic_index_in_dim(halves, core, 2, keepdims=False)
+        return halves.reshape(weight.shape[0], hidden_width)
+
+    qkv_piece = jnp.concatenate([columns(query_weight), columns(key_weight), columns(value_weight)], axis=1)
+    qkv_weight = in_order(x == 0, qkv_piece, at.fetch(qkv_piece))
+    out_piece = at.fetch(half_of(output_weight, core))
+    out_piece = in_order(core == 0, out_piece, across(out_piece, CORE_BIT))
+    out_weight = in_order(x == 0, output_weight, out_piece)
+    up_piece = up_columns(up_weight)
+    up_all = in_order(x == 0, up_piece, at.fetch(up_piece))
+    down_piece = half_of(down_weight, core)
+    down_all = in_order(x == 0, down_piece, at.fetch(down_piece))
+
+    own = own.astype(f32)
+    standard_one, inverse_one = standardize(own)
+    normed_own = (standard_one * gain_one + bias_one).astype(bf16)
+    normed_one = jnp.concatenate([normed_own, across(normed_own, CORE_BIT)])
+    qkv_bias = jnp.concatenate(
+        [half_of(q_bias, core), jnp.zeros((head_width,), f32), half_of(v_bias, core)]
+    )
+    qkv = (matmul(normed_one, qkv_weight) + qkv_bias).astype(bf16)
+    mixed_heads, log_total = attend(qkv)
+    other_heads = across(mixed_heads, CORE_BIT)
+    other_heads = jnp.concatenate([other_heads[rows:], other_heads[:rows]])
+    mixed = in_order(core == 0, mixed_heads, other_heads, axis=1)
+    middle = own + matmul(mixed[:rows], out_weight) + o_bias
+    standard_two, inverse_two = standardize(middle)
+    normed_own = (standard_two * gain_two + bias_two).astype(bf16)
+    normed_two = jnp.concatenate([normed_own, across(normed_own, CORE_BIT)])
+    up_bias_own = lax.dynamic_index_in_dim(u_bias.reshape(2, 2, -1), core, 1, keepdims=False).reshape(-1)
+    up_proj = matmul(normed_two, up_all) + up_bias_own
+    hidden = gelu_value(up_proj).astype(bf16)
+
+    grad_result = own_grad.astype(f32) * weight_cell
+    grad_own = grad_result.astype(bf16)
+    grad_ffn = jnp.concatenate([grad_own, across(grad_own, CORE_BIT)])
+
+    def weight_sum(left, right):
+        give = weight_grad(half_of(left, 1 - x, 1), right).astype(bf16)
+        keep = weight_grad(half_of(left, x, 1), right).astype(bf16)
+        return at.add_up(keep, give)
+
+    sum_down = weight_sum(hidden, grad_ffn)
+    grad_up = (matmul_right_t(grad_ffn, down_all) * gelu_slope(up_proj)).astype(bf16)
+    sum_up = weight_sum(normed_two, grad_up)
+    partial = matmul_right_t(grad_up, up_all)
+    grad_normed_two = partial[:rows] + across(partial[rows:].astype(bf16), CORE_BIT).astype(f32)
+    grad_middle = grad_result + standardize_back(grad_normed_two, standard_two, inverse_two, gain_two)
+    grad_attn_own = grad_middle.astype(bf16)
+    grad_attn = jnp.concatenate([grad_attn_own, across(grad_attn_own, CORE_BIT)])
+    sum_out = weight_sum(mixed, half_of(grad_attn, core, 1))
+
+    partial = matmul(hidden, down_all)
+    result = middle + partial[:rows] + across(partial[rows:].astype(bf16), CORE_BIT).astype(f32) + d_bias
+    result = result.astype(bf16)
+    result = jnp.where(swapped, across_diagonal(result), result)
+
+    grad_mixed = matmul_right_t(grad_attn, half_of(out_weight, core)).astype(bf16)
+    grad_qkv = jnp.concatenate(attend_back(qkv, log_total, grad_mixed), axis=1)
+    sum_qkv = weight_sum(normed_one, grad_qkv)
+    partial = matmul_right_t(grad_qkv, qkv_weight)
+    grad_normed_one = partial[:rows] + across(partial[rows:].astype(bf16), CORE_BIT).astype(f32)
+    input_grad = grad_middle + standardize_back(grad_normed_one, standard_one, inverse_one, gain_one)
+    input_grad = input_grad.astype(bf16)
+    input_grad = jnp.where(swapped, across_diagonal(input_grad), input_grad)
+
+    def at_core(value):
+        zero = jnp.zeros_like(value)
+        return jnp.concatenate([jnp.where(core == 0, value, zero), jnp.where(core == 0, zero, value)], axis=-1)
+
+    qkv_sum = column_sum(grad_qkv).reshape(3, head_width)
+    up_sum = at_core(column_sum(grad_up).reshape(2, 1, -1)).reshape(-1)
+    sums = [
+        jnp.sum(grad_normed_one * standard_one, axis=0),
+        jnp.sum(grad_normed_one, axis=0),
+        at_core(qkv_sum[0]),
+        at_core(qkv_sum[2]),
+        column_sum(grad_attn_own),
+        jnp.sum(grad_normed_two * standard_two, axis=0),
+        jnp.sum(grad_normed_two, axis=0),
+        column_sum(grad_own),
+        up_sum,
+    ]
+    sums = [half_of(v, x) for v in jnp.split(lax.psum(jnp.concatenate(sums), BOTH), np_offsets(sums))]
+    s_gain_one, s_bias_one, s_q_bias, s_v_bias, s_o_bias, s_gain_two, s_bias_two, s_d_bias, s_u_bias = sums
+
+    def both_columns(value):
+        return in_order(core == 0, value, across(value, CORE_BIT), axis=1).astype(f32)
+
+    other = across(sum_qkv, CORE_BIT)
+    each = [
+        in_order(
+            core == 0,
+            sum_qkv[:, i * head_width : (i + 1) * head_width],
+            other[:, i * head_width : (i + 1) * head_width],
+            axis=1,
+        ).astype(f32)
+        for i in range(3)
+    ]
+    up_own = sum_up.reshape(-1, 2, hidden_width // 2)
+    up_other = across(sum_up, CORE_BIT).reshape(-1, 2, hidden_width // 2)
+    s_up = jnp.concatenate(
+        [in_order(core == 0, up_own[:, h], up_other[:, h], axis=1) for h in range(2)], axis=1
+    ).astype(f32)
+    s_down = in_order(core == 0, sum_down, across(sum_down, CORE_BIT)).astype(f32)
+    return (
+        result[None],
+        input_grad[None],
+        s_gain_one,
+        s_bias_one,
+        each[0],
+        s_q_bias,
+        each[1],
+        each[2],
+        s_v_bias,
+        both_columns(sum_out),
+        s_o_bias,
+        s_gain_two,
+        s_bias_two,
+        s_up,
+        s_u_bias,
+        s_down,
+        s_d_bias,
+    )
+
+
+def np_offsets(values):
+    offsets = []
+    total = 0
+    for value in values[:-1]:
+        total += value.shape[0]
+        offsets.append(total)
+    return offsets
+
+
+def chosen(mesh):
+    cells, blocks = mesh.shape["cell"], mesh.shape["seq"]
+
+    def per_device(tokens, *rest):
+        power = cells & (cells - 1) == 0
+        if blocks == 2 and power and cells >= 4 and tokens.shape[0] == 1:
+            return tuned(tokens, *rest)
+        return general(tokens, *rest)
+
+    return per_device
+
+
 def solution(mesh):
     placed = (
         P("cell", "seq", None),
@@ -371,7 +762,7 @@
         P("seq"),
     )
     return jax.shard_map(
-        per_device,
+        chosen(mesh),
         mesh=mesh,
         in_specs=placed,
         out_specs=(

time: 1630 us -> 997 us (0.61)
  waiting for transfers between devices: 1160 us -> 374 us
  starting transfers between devices: 2.83 us -> 166 us
  matrix products: 250 us -> 101 us
  local copies, waits for them, and re-layouts: 25.4 us -> 137 us
  blocking collectives: 112 us -> 49.5 us
  Pallas kernels: 0 us -> 55.5 us
  other arithmetic: 53 us -> 104 us
    all_gather x6 -> x0, waiting for transfers between devices: 411 us -> none  [the longest x1 151 us: per_device(): lax.all_gather(up_weight, 'seq', axis=0, tiled=True)]
    reduce_scatter x6 -> x0, waiting for transfers between devices: 324 us -> none  [the longest x1 153 us: per_device(): lax.psum_scatter(grad_up_weight.astype(jnp.bfloat16), 'seq', scatter_dime...]
    psum x1 -> x0, waiting for transfers between devices: 231 us -> none  [per_device(): lax.psum(grad_query_weight.astype(jnp.bfloat16), 'cell').astype(jnp.float32)]
    ppermute x6 -> x63, waiting for transfers between devices: 193 us -> 374 us  [the longest x58 374 us: across(): return lax.ppermute(value, BOTH, [(i, i ^ bit) for i in range(count)])]
    ppermute x6 -> x63, starting transfers between devices: 1.69 us -> 166 us  [the longest x58 161 us: across(): return lax.ppermute(value, BOTH, [(i, i ^ bit) for i in range(count)])]
    dot_general x12 -> x0, matrix products: 108 us -> none  [the longest x2 24.8 us: per_device(): jnp.einsum('cqhd,ckhd->chqk', grad_mixed, block_values, preferred_element...]
    dynamic_slice x0 -> x20, local copies, waits for them, and re-layouts: none -> 65.3 us  [the longest x1 51.3 us: up_columns(): halves = lax.dynamic_index_in_dim(halves, core, 2, keepdims=False)]
    pallas_call x0 -> x2, Pallas kernels: none -> 55.5 us  [the longest x1 34.5 us: attend_back(): pl.pallas_call(attend_back_kernel, grid=(pairs,), in_specs=[block, pl.Blo...]
  transfers between devices with their start and end apart: 19 -> 63, of which waited for: 14 -> 25; matrix products, arithmetic and copies ran while one was open for 16% -> 28% of each run, Pallas kernels for 0% -> 6%
where the time goes in v1:
time: 997 us; the launch traced here: 993 us
  waiting for transfers between devices  374 us (38%)
  starting transfers between devices  166 us (17%)
  local copies, waits for them, and re-layouts  137 us (14%)
  other arithmetic  104 us (10%)
  matrix products  101 us (10%)
  Pallas kernels  55.5 us (6%)
  blocking collectives  49.5 us (5%)
    ppermute x58, waiting for transfers between devices, across(): return lax.ppermute(value, BOTH, [(i, i ^ bit) for i in range(count)])  374 us
    ppermute x58, starting transfers between devices, across(): return lax.ppermute(value, BOTH, [(i, i ^ bit) for i in range(count)])  161 us
    dynamic_slice x1, local copies, waits for them, and re-layouts, up_columns(): halves = lax.dynamic_index_in_dim(halves, core, 2, keepdims=False)  51.3 us
    psum x1, blocking collectives, tuned(): lax.psum(jnp.concatenate(sums), BOTH)  49.5 us
    select_n x34, other arithmetic, in_order(): low = jnp.where(first, own, received)  38.5 us
    dot_general x8, matrix products, weight_grad(): jnp.einsum('ti,to->io', left, right, preferred_element_type=jnp.float32)  38 us
    pallas_call x1, Pallas kernels, attend_back(): pl.pallas_call(attend_back_kernel, grid=(pairs,), in_specs=[block, pl.Blo...  34.5 us
    dot_general x4, matrix products, matmul_right_t(): jnp.einsum('to,io->ti', left, right, preferred_element_type=jnp.float32)  33.7 us
  transfers between devices with their start and end apart: 63, of which 25 were waited for; matrix products, arithmetic and copies ran while one was open for 28% of the time, Pallas kernels for 6%

profile of v1, /device:TPU:0, one launch (start us, length us, event | category | flops | bytes accessed | tf_op | source)
XLA Modules:
  0.0 992.7 jit_solution(2610746713054502191)
XLA Ops:
  20.4 15.2 %reshape.199 = bf16[640,2,2,1280]{3,2,1,0:T(2,128)(2,1)} reshape(bf16[640,5120]{1,0:T(8,128)(2,1)} %param.32) | data formatting | bytes 13107200 | tf_op jit(solution)/shard_map/reshape | solution.py:595
  35.5 51.3 %dynamic-slice_reduce_fusion = bf16[640,2,1280]{2,1,0:T(2,128)(2,1)S(1)} fusion(bf16[640,2,2,1280]{3,2,1,0:T(2,128)(2,1)} %reshape.199, s32[]{:T(128)S(6)} %select_n.719), kind=kLoop, calls=%fused_computation.21 | loop fusion | bytes 6553604 | tf_op jit(solution)/shard_map/jit(dynamic_index_in_dim)/dynamic_slice | solution.py:596
  120.1 20.5 %collective-permute-done.4 = bf16[80,1920]{1,0:T(8,128)(2,1)S(1)} collective-permute-done((bf16[80,1920]{1,0:T(8,128)(2,1)}, bf16[80,1920]{1,0:T(8,128)(2,1)S(1)}, u32[]{:S(2)}, u32[]{:S(2)}) %collective-permute-start.4) | collective-permute-done | bytes 307232 | tf_op jit(solution)/shard_map/ppermute | solution.py:363
  144.3 14.0 %collective-permute-done.15 = bf16[80,2560]{1,0:T(8,128)(2,1)S(1)} collective-permute-done((bf16[80,2560]{1,0:T(8,128)(2,1)S(1)}, bf16[80,2560]{1,0:T(8,128)(2,1)S(1)}, u32[]{:S(2)}, u32[]{:S(2)}) %collective-permute-start.15) | collective-permute-done | bytes 409632 | tf_op jit(solution)/shard_map/ppermute | solution.py:363
  159.5 7.5 collective-permute-done.19
  194.4 12.6 %collective-permute-done.20 = bf16[320,1280]{1,0:T(8,128)(2,1)S(1)} collective-permute-done((bf16[320,1280]{1,0:T(8,128)(2,1)S(1)}, bf16[320,1280]{1,0:T(8,128)(2,1)S(1)}, u32[]{:S(2)}, u32[]{:S(2)}) %collective-permute-start.20) | collective-permute-done | bytes 819232 | tf_op jit(solution)/shard_map/ppermute | solution.py:363
  225.5 21.0 %attend.1 = (bf16[1024,640]{1,0:T(8,128)(2,1)S(1)}, f32[10,1,1024]{2,1,0:T(1,128)S(1)}) custom-call(bf16[1024,1920]{1,0:T(8,128)(2,1)S(1)} %add_convert_fusion.q_ref.k_ref.v_ref, bf16[1024,1920]{1,0:T(8,128)(2,1)S(1)} %add_convert_fusion.q_ref.k_ref.v_ref, bf16[1024,1920]{1,0:T(8,128)(2,1)S(1)} %add_convert_fusion.q_ref.k_ref.v_ref), custom_call_target="tpu_custom_call" | custom-call | flops 10737418240 | bytes 5242880 | tf_op jit(solution)/shard_map/attend/pallas_call | solution.py:496
  247.7 33.0 %collective-permute-done.21 = bf16[640,1280]{1,0:T(8,128)(2,1)} collective-permute-done((bf16[640,1280]{1,0:T(8,128)(2,1)}, bf16[640,1280]{1,0:T(8,128)(2,1)}, u32[]{:S(2)}, u32[]{:S(2)}) %collective-permute-start.21) | collective-permute-done | bytes 1638432 | tf_op jit(solution)/shard_map/ppermute | solution.py:363
  299.5 12.2 %multiply_convert_fusion = (bf16[1024,2560]{1,0:T(8,128)(2,1)}, f32[1024,2560]{1,0:T(8,128)}) fusion(f32[2560]{0:T(1024)S(1)} %add.318, bf16[640,2560]{1,0:T(8,128)(2,1)S(1)} %get-tuple-element.51, bf16[640,2560]{1,0:T(8,128)(2,1)S(1)} %get-tuple-element.50, bf16[512,1280]{1,0:T(8,128)(2,1)} %copy-done.62, bf16[512,1280]{1,0:T(8,128)(2,1)S(1)} %copy-done.42), kind=kOutput, calls=%fused_computation.8 | convolution fusion | flops 6744965120 | bytes 24913920 | tf_op jit(solution)/shard_map/dot_general | solution.py:23
  311.7 16.4 %convert_reduce_fusion = (f32[2560]{0:T(1024)S(1)}, bf16[1024,2560]{1,0:T(8,128)(2,1)}) fusion(f32[1024,2560]{1,0:T(8,128)} %get-tuple-element.146, f32[2560]{0:T(1024)S(1)} %add.318, bf16[1280,1280]{1,0:T(8,128)(2,1)S(1)} %copy-done.24, bf16[1280,1280]{1,0:T(8,128)(2,1)S(1)} %get-tuple-element.42, bf16[512,1280]{1,0:T(8,128)(2,1)} %collective-permute-done.26, ...), kind=kOutput, calls=%fused_computation.7 | convolution fusion | flops 6763312640 | bytes 24924160 | tf_op jit(solution)/shard_map/to,io->ti/dot_general | solution.py:27
  328.1 9.1 fusion.9
  338.8 9.6 fusion.8
  351.6 8.3 convolution_convert_fusion.2
  368.1 7.4 convolution_convert_fusion
  384.7 34.5 %attend_back.1 = (bf16[1024,640]{1,0:T(8,128)(2,1)S(1)}, bf16[1024,640]{1,0:T(8,128)(2,1)S(1)}, bf16[1024,640]{1,0:T(8,128)(2,1)S(1)}) custom-call(bf16[1024,1920]{1,0:T(8,128)(2,1)} %copy-done.2, bf16[1024,1920]{1,0:T(8,128)(2,1)} %copy-done.2, bf16[1024,1920]{1,0:T(8,128)(2,1)} %copy-done.2, f32[10,1,1024]{2,1,0:T(1,128)S(1)} %get-tuple-element.23.total_ref, ...), custom_call_target="tpu_custom_call" | custom-call | flops 26843545600 | bytes 9175040 | tf_op jit(solution)/shard_map/attend_back/pallas_call | solution.py:525
  438.6 93.3 %collective-permute-start.39 = (bf16[640,640]{1,0:T(8,128)(2,1)S(1)}, bf16[640,640]{1,0:T(8,128)(2,1)S(1)}, u32[]{:S(2)}, u32[]{:S(2)}) collective-permute-start(bf16[640,640]{1,0:T(8,128)(2,1)S(1)} %convolution_convert_fusion.6), channel_id=1, source_target_pairs={{0,1},{1,0},{2,3},{3,2},{4,5},{5,4},{6,7},{7,6},{8,9},{9,8},{10,11... | collective-permute-start | bytes 2457608 | tf_op jit(solution)/shard_map/ppermute | solution.py:363
  543.2 44.4 %collective-permute-done.39 = bf16[640,640]{1,0:T(8,128)(2,1)S(1)} collective-permute-done((bf16[640,640]{1,0:T(8,128)(2,1)S(1)}, bf16[640,640]{1,0:T(8,128)(2,1)S(1)}, u32[]{:S(2)}, u32[]{:S(2)}) %collective-permute-start.39) | collective-permute-done | bytes 819232 | tf_op jit(solution)/shard_map/ppermute | solution.py:363
  589.5 7.3 fusion.7
  607.3 6.6 collective-permute-done.42
  628.1 49.5 %psum.7 = f32[15360]{0:T(1024)S(1)} all-reduce(f32[15360]{0:T(1024)S(1)} %constant_dynamic-update-slice_fusion.6), channel_id=1, replica_groups=mesh['cell'=16,'seq'=2] {'cell','seq'}, use_global_device_ids=true, to_apply=%region_16.17 | all-reduce | flops 15360 | bytes 122880 | tf_op jit(solution)/shard_map/psum | solution.py:679
  702.5 10.9 %collective-permute-done.49 = bf16[160,2560]{1,0:T(8,128)(2,1)S(1)} collective-permute-done((bf16[160,2560]{1,0:T(8,128)(2,1)S(1)}, bf16[160,2560]{1,0:T(8,128)(2,1)S(1)}, u32[]{:S(2)}, u32[]{:S(2)}) %collective-permute-start.49) | collective-permute-done | bytes 819232 | tf_op jit(solution)/shard_map/ppermute | solution.py:363
  713.8 25.2 %collective-permute-done.57 = bf16[320,1280]{1,0:T(8,128)(2,1)S(1)} collective-permute-done((bf16[320,1280]{1,0:T(8,128)(2,1)S(1)}, bf16[320,1280]{1,0:T(8,128)(2,1)S(1)}, u32[]{:S(2)}, u32[]{:S(2)}) %collective-permute-start.57) | collective-permute-done | bytes 819232 | tf_op jit(solution)/shard_map/ppermute | solution.py:363
  742.3 25.2 %collective-permute-done.58 = bf16[160,1280]{1,0:T(8,128)(2,1)S(1)} collective-permute-done((bf16[160,1280]{1,0:T(8,128)(2,1)S(1)}, bf16[160,1280]{1,0:T(8,128)(2,1)S(1)}, u32[]{:S(2)}, u32[]{:S(2)}) %collective-permute-start.58) | collective-permute-done | bytes 409632 | tf_op jit(solution)/shard_map/ppermute | solution.py:363
  770.8 14.4 %collective-permute-done.51 = bf16[80,2560]{1,0:T(8,128)(2,1)S(1)} collective-permute-done((bf16[80,2560]{1,0:T(8,128)(2,1)S(1)}, bf16[80,2560]{1,0:T(8,128)(2,1)S(1)}, u32[]{:S(2)}, u32[]{:S(2)}) %collective-permute-start.51) | collective-permute-done | bytes 409632 | tf_op jit(solution)/shard_map/ppermute | solution.py:363
  785.3 14.4 %collective-permute-done.33 = bf16[160,1920]{1,0:T(8,128)(2,1)S(1)} collective-permute-done((bf16[160,1920]{1,0:T(8,128)(2,1)S(1)}, bf16[160,1920]{1,0:T(8,128)(2,1)S(1)}, u32[]{:S(2)}, u32[]{:S(2)}) %collective-permute-start.33) | collective-permute-done | bytes 614432 | tf_op jit(solution)/shard_map/ppermute | solution.py:363
  802.9 11.9 %collective-permute-done.34 = bf16[80,1920]{1,0:T(8,128)(2,1)S(1)} collective-permute-done((bf16[80,1920]{1,0:T(8,128)(2,1)S(1)}, bf16[80,1920]{1,0:T(8,128)(2,1)S(1)}, u32[]{:S(2)}, u32[]{:S(2)}) %collective-permute-start.34) | collective-permute-done | bytes 307232 | tf_op jit(solution)/shard_map/ppermute | solution.py:363
  818.3 12.1 %collective-permute-done.52 = bf16[160,2560]{1,0:T(8,128)(2,1)S(1)} collective-permute-done((bf16[160,2560]{1,0:T(8,128)(2,1)S(1)}, bf16[160,2560]{1,0:T(8,128)(2,1)S(1)}, u32[]{:S(2)}, u32[]{:S(2)}) %collective-permute-start.52) | collective-permute-done | bytes 819232 | tf_op jit(solution)/shard_map/ppermute | solution.py:363
  831.0 7.2 collective-permute-done.35
  848.6 11.5 %collective-permute-done.36 = bf16[160,1920]{1,0:T(8,128)(2,1)S(1)} collective-permute-done((bf16[160,1920]{1,0:T(8,128)(2,1)S(1)}, bf16[160,1920]{1,0:T(8,128)(2,1)S(1)}, u32[]{:S(2)}, u32[]{:S(2)}) %collective-permute-start.36) | collective-permute-done | bytes 614432 | tf_op jit(solution)/shard_map/ppermute | solution.py:363
  860.6 9.0 collective-permute-done.53
  872.1 56.0 %collective-permute-done.37 = bf16[320,1920]{1,0:T(8,128)(2,1)S(1)} collective-permute-done((bf16[320,1920]{1,0:T(8,128)(2,1)S(1)}, bf16[320,1920]{1,0:T(8,128)(2,1)S(1)}, u32[]{:S(2)}, u32[]{:S(2)}) %collective-permute-start.37) | collective-permute-done | bytes 1228832 | tf_op jit(solution)/shard_map/ppermute | solution.py:363
  933.5 6.8 reshape.202
  (450 shorter events, 310.6 us)
Async XLA Ops:
  8.3 87.3 %collective-permute-start.1 = (bf16[7680]{0:T(1024)(128)(2,1)S(1)}, bf16[7680]{0:T(1024)(128)(2,1)S(1)}, u32[]{:S(2)}, u32[]{:S(2)}) collective-permute-start(bf16[7680]{0:T(1024)(128)(2,1)S(1)} %constant_dynamic-update-slice_fusion.4), channel_id=1, source_target_pairs={{0,1},{1,0},{2,3},{3,2},{4,5},{5,4},{6,7},{7,6},{8,9},{9,8},{10,11... | collective-permute-start | bytes 46088 | tf_op jit(solution)/shard_map/ppermute | solution.py:363
  12.2 83.5 %collective-permute-start.8 = (bf16[40,1280]{1,0:T(8,128)(2,1)S(1)}, bf16[40,1280]{1,0:T(8,128)(2,1)S(1)}, u32[]{:S(2)}, u32[]{:S(2)}) collective-permute-start(bf16[40,1280]{1,0:T(8,128)(2,1)S(1)} %constant_dynamic-slice_fusion.3), channel_id=1, source_target_pairs={{0,1},{1,0},{2,3},{3,2},{4,5},{5,4},{6,7},{7,6},{8,9},{9,8},{10,11... | collective-permute-start | bytes 307208 | tf_op jit(solution)/shard_map/ppermute | solution.py:363
  15.1 97.9 %collective-permute-start.3 = (bf16[80,1920]{1,0:T(8,128)(2,1)}, bf16[80,1920]{1,0:T(8,128)(2,1)}, u32[]{:S(2)}, u32[]{:S(2)}) collective-permute-start(bf16[80,1920]{1,0:T(8,128)(2,1)} %constant_dynamic-slice_fusion.4), channel_id=1, source_target_pairs={{0,1},{1,0},{2,3},{3,2},{4,5},{5,4},{6,7},{7,6},{8,9},{9,8},{10,11... | collective-permute-start | bytes 921608 | tf_op jit(solution)/shard_map/ppermute | solution.py:363
  17.1 155.1 %collective-permute-start = (bf16[512,1280]{1,0:T(8,128)(2,1)}, bf16[512,1280]{1,0:T(8,128)(2,1)}, u32[]{:S(2)}, u32[]{:S(2)}) collective-permute-start(bf16[512,1280]{1,0:T(8,128)(2,1)} %bitcast), channel_id=1, source_target_pairs={{1,2},{2,1},{5,6},{6,5},{9,10},{10,9},{13,14},{14,13},{17,18},{18,... | collective-permute-start | bytes 3932168 | tf_op jit(solution)/shard_map/ppermute | solution.py:369
  19.5 72.3 %collective-permute-start.25 = (f32[8,128]{1,0:T(8,128)S(1)}, f32[8,128]{1,0:T(8,128)S(1)}, u32[]{:S(2)}, u32[]{:S(2)}) collective-permute-start(f32[8,128]{1,0:T(8,128)S(1)} %broadcast_in_dim.9), channel_id=1, source_target_pairs={{1,2},{2,1},{5,6},{6,5},{9,10},{10,9},{13,14},{14,13},{17,18},{18,... | collective-permute-start | bytes 12296 | tf_op jit(solution)/shard_map/ppermute | solution.py:369
  113.0 63.7 %collective-permute-start.24 = (bf16[512,1280]{1,0:T(8,128)(2,1)}, bf16[512,1280]{1,0:T(8,128)(2,1)S(1)}, u32[]{:S(2)}, u32[]{:S(2)}) collective-permute-start(bf16[512,1280]{1,0:T(8,128)(2,1)} %bitcast.35), channel_id=1, source_target_pairs={{1,2},{2,1},{5,6},{6,5},{9,10},{10,9},{13,14},{14,13},{17,18},{18,... | collective-permute-start | bytes 3932168 | tf_op jit(solution)/shard_map/ppermute | solution.py:369
  120.1 38.2 %collective-permute-start.15 = (bf16[80,2560]{1,0:T(8,128)(2,1)S(1)}, bf16[80,2560]{1,0:T(8,128)(2,1)S(1)}, u32[]{:S(2)}, u32[]{:S(2)}) collective-permute-start(bf16[80,2560]{1,0:T(8,128)(2,1)S(1)} %collective-permute-done.14), channel_id=1, source_target_pairs={{0,16},{1,17},{2,18},{3,19},{4,20},{5,21},{6,22},{7,23},{8,24},{9,... | collective-permute-start | bytes 1228808 | tf_op jit(solution)/shard_map/ppermute | solution.py:363
  158.3 51.8 %collective-permute-start.12 = (bf16[320,1280]{1,0:T(8,128)(2,1)S(1)}, bf16[320,1280]{1,0:T(8,128)(2,1)S(1)}, u32[]{:S(2)}, u32[]{:S(2)}) collective-permute-start(bf16[320,1280]{1,0:T(8,128)(2,1)S(1)} %pad_maximum_fusion.35), channel_id=1, source_target_pairs={{0,2},{1,3},{2,0},{3,1},{4,6},{5,7},{6,4},{7,5},{8,10},{9,11},{10,... | collective-permute-start | bytes 2457608 | tf_op jit(solution)/shard_map/ppermute | solution.py:363
  172.2 41.0 %collective-permute-start.6 = (bf16[320,1920]{1,0:T(8,128)(2,1)S(1)}, bf16[320,1920]{1,0:T(8,128)(2,1)S(1)}, u32[]{:S(2)}, u32[]{:S(2)}) collective-permute-start(bf16[320,1920]{1,0:T(8,128)(2,1)S(1)} %pad_maximum_fusion.33), channel_id=1, source_target_pairs={{0,4},{1,5},{2,6},{3,7},{4,0},{5,1},{6,2},{7,3},{8,12},{9,13},{10,... | collective-permute-start | bytes 3686408 | tf_op jit(solution)/shard_map/ppermute | solution.py:363
  176.7 40.4 %collective-permute-start.2 = (bf16[512,1280]{1,0:T(8,128)(2,1)S(1)}, bf16[512,1280]{1,0:T(8,128)(2,1)S(1)}, u32[]{:S(2)}, u32[]{:S(2)}) collective-permute-start(bf16[512,1280]{1,0:T(8,128)(2,1)S(1)} %fusion.21), channel_id=1, source_target_pairs={{0,2},{1,3},{2,0},{3,1},{4,6},{5,7},{6,4},{7,5},{8,10},{9,11},{10,... | collective-permute-start | bytes 3932168 | tf_op jit(solution)/shard_map/ppermute | solution.py:363
  189.4 122.2 %collective-permute-start.26 = (bf16[512,1280]{1,0:T(8,128)(2,1)}, bf16[512,1280]{1,0:T(8,128)(2,1)}, u32[]{:S(2)}, u32[]{:S(2)}) collective-permute-start(bf16[512,1280]{1,0:T(8,128)(2,1)} %get-tuple-element.36), channel_id=1, source_target_pairs={{0,2},{1,3},{2,0},{3,1},{4,6},{5,7},{6,4},{7,5},{8,10},{9,11},{10,... | collective-permute-start | bytes 3932168 | tf_op jit(solution)/shard_map/ppermute | solution.py:363
  207.0 87.4 %collective-permute-start.17 = (bf16[320,2560]{1,0:T(8,128)(2,1)}, bf16[320,2560]{1,0:T(8,128)(2,1)}, u32[]{:S(2)}, u32[]{:S(2)}) collective-permute-start(bf16[320,2560]{1,0:T(8,128)(2,1)} %pad_maximum_fusion.26), channel_id=1, source_target_pairs={{0,4},{1,5},{2,6},{3,7},{4,0},{5,1},{6,2},{7,3},{8,12},{9,13},{10,... | collective-permute-start | bytes 4915208 | tf_op jit(solution)/shard_map/ppermute | solution.py:363
  210.1 70.6 %collective-permute-start.21 = (bf16[640,1280]{1,0:T(8,128)(2,1)}, bf16[640,1280]{1,0:T(8,128)(2,1)}, u32[]{:S(2)}, u32[]{:S(2)}) collective-permute-start(bf16[640,1280]{1,0:T(8,128)(2,1)} %pad_maximum_fusion.27), channel_id=1, source_target_pairs={{0,4},{1,5},{2,6},{3,7},{4,0},{5,1},{6,2},{7,3},{8,12},{9,13},{10,... | collective-permute-start | bytes 4915208 | tf_op jit(solution)/shard_map/ppermute | solution.py:363
  246.5 40.6 %collective-permute-start.7 = (bf16[1024,640]{1,0:T(8,128)(2,1)S(1)}, bf16[1024,640]{1,0:T(8,128)(2,1)S(1)}, u32[]{:S(2)}, u32[]{:S(2)}) collective-permute-start(bf16[1024,640]{1,0:T(8,128)(2,1)S(1)} %get-tuple-element.22), channel_id=1, source_target_pairs={{0,2},{1,3},{2,0},{3,1},{4,6},{5,7},{6,4},{7,5},{8,10},{9,11},{10,... | collective-permute-start | bytes 3932168 | tf_op jit(solution)/shard_map/ppermute | solution.py:363
  359.9 178.6 %collective-permute-start.47 = (bf16[640,2560]{1,0:T(8,128)(2,1)}, bf16[640,2560]{1,0:T(8,128)(2,1)}, u32[]{:S(2)}, u32[]{:S(2)}) collective-permute-start(bf16[640,2560]{1,0:T(8,128)(2,1)} %convolution_convert_fusion.2), channel_id=1, source_target_pairs={{0,1},{1,0},{2,3},{3,2},{4,5},{5,4},{6,7},{7,6},{8,9},{9,8},{10,11... | collective-permute-start | bytes 9830408 | tf_op jit(solution)/shard_map/ppermute | solution.py:363
  375.5 214.0 %collective-permute-start.55 = (bf16[1280,1280]{1,0:T(8,128)(2,1)}, bf16[1280,1280]{1,0:T(8,128)(2,1)}, u32[]{:S(2)}, u32[]{:S(2)}) collective-permute-start(bf16[1280,1280]{1,0:T(8,128)(2,1)} %convolution_convert_fusion), channel_id=1, source_target_pairs={{0,1},{1,0},{2,3},{3,2},{4,5},{5,4},{6,7},{7,6},{8,9},{9,8},{10,11... | collective-permute-start | bytes 9830408 | tf_op jit(solution)/shard_map/ppermute | solution.py:363
  381.3 57.3 %collective-permute-start.23 = (bf16[512,1280]{1,0:T(8,128)(2,1)}, bf16[512,1280]{1,0:T(8,128)(2,1)S(1)}, u32[]{:S(2)}, u32[]{:S(2)}) collective-permute-start(bf16[512,1280]{1,0:T(8,128)(2,1)} %get-tuple-element.74), channel_id=1, source_target_pairs={{1,2},{2,1},{5,6},{6,5},{9,10},{10,9},{13,14},{14,13},{17,18},{18,... | collective-permute-start | bytes 3932168 | tf_op jit(solution)/shard_map/ppermute | solution.py:369
  427.6 171.3 %collective-permute-start.29 = (bf16[512,1280]{1,0:T(8,128)(2,1)S(1)}, bf16[512,1280]{1,0:T(8,128)(2,1)S(1)}, u32[]{:S(2)}, u32[]{:S(2)}) collective-permute-start(bf16[512,1280]{1,0:T(8,128)(2,1)S(1)} %slice.246), channel_id=1, source_target_pairs={{0,2},{1,3},{2,0},{3,1},{4,6},{5,7},{6,4},{7,5},{8,10},{9,11},{10,... | collective-permute-start | bytes 3932168 | tf_op jit(solution)/shard_map/ppermute | solution.py:363
  433.6 262.9 %collective-permute-start.31 = (bf16[640,1920]{1,0:T(8,128)(2,1)}, bf16[640,1920]{1,0:T(8,128)(2,1)}, u32[]{:S(2)}, u32[]{:S(2)}) collective-permute-start(bf16[640,1920]{1,0:T(8,128)(2,1)} %convolution_convert_fusion.4), channel_id=1, source_target_pairs={{0,1},{1,0},{2,3},{3,2},{4,5},{5,4},{6,7},{7,6},{8,9},{9,8},{10,11... | collective-permute-start | bytes 7372808 | tf_op jit(solution)/shard_map/ppermute | solution.py:363
  438.6 149.1 %collective-permute-start.39 = (bf16[640,640]{1,0:T(8,128)(2,1)S(1)}, bf16[640,640]{1,0:T(8,128)(2,1)S(1)}, u32[]{:S(2)}, u32[]{:S(2)}) collective-permute-start(bf16[640,640]{1,0:T(8,128)(2,1)S(1)} %convolution_convert_fusion.6), channel_id=1, source_target_pairs={{0,1},{1,0},{2,3},{3,2},{4,5},{5,4},{6,7},{7,6},{8,9},{9,8},{10,11... | collective-permute-start | bytes 2457608 | tf_op jit(solution)/shard_map/ppermute | solution.py:363
  541.6 147.8 %collective-permute-start.48 = (bf16[320,2560]{1,0:T(8,128)(2,1)S(1)}, bf16[320,2560]{1,0:T(8,128)(2,1)}, u32[]{:S(2)}, u32[]{:S(2)}) collective-permute-start(bf16[320,2560]{1,0:T(8,128)(2,1)S(1)} %dynamic-slice_convert_fusion.1), channel_id=1, source_target_pairs={{0,4},{1,5},{2,6},{3,7},{4,0},{5,1},{6,2},{7,3},{8,12},{9,13},{10,... | collective-permute-start | bytes 4915208 | tf_op jit(solution)/shard_map/ppermute | solution.py:363
  598.2 94.1 %collective-permute-start.56 = (bf16[640,1280]{1,0:T(8,128)(2,1)}, bf16[640,1280]{1,0:T(8,128)(2,1)}, u32[]{:S(2)}, u32[]{:S(2)}) collective-permute-start(bf16[640,1280]{1,0:T(8,128)(2,1)} %dynamic-slice_convert_fusion), channel_id=1, source_target_pairs={{0,4},{1,5},{2,6},{3,7},{4,0},{5,1},{6,2},{7,3},{8,12},{9,13},{10,... | collective-permute-start | bytes 4915208 | tf_op jit(solution)/shard_map/ppermute | solution.py:363
  627.1 57.2 %collective-permute-start.45 = (bf16[320,640]{1,0:T(8,128)(2,1)}, bf16[320,640]{1,0:T(8,128)(2,1)}, u32[]{:S(2)}, u32[]{:S(2)}) collective-permute-start(bf16[320,640]{1,0:T(8,128)(2,1)} %pad_maximum_fusion.47), channel_id=1, source_target_pairs={{0,4},{1,5},{2,6},{3,7},{4,0},{5,1},{6,2},{7,3},{8,12},{9,13},{10,... | collective-permute-start | bytes 1228808 | tf_op jit(solution)/shard_map/ppermute | solution.py:363
  694.4 44.6 %collective-permute-start.57 = (bf16[320,1280]{1,0:T(8,128)(2,1)S(1)}, bf16[320,1280]{1,0:T(8,128)(2,1)S(1)}, u32[]{:S(2)}, u32[]{:S(2)}) collective-permute-start(bf16[320,1280]{1,0:T(8,128)(2,1)S(1)} %dynamic-slice_convert_fusion.3), channel_id=1, source_target_pairs={{0,8},{1,9},{2,10},{3,11},{4,12},{5,13},{6,14},{7,15},{8,0},{9,1},... | collective-permute-start | bytes 2457608 | tf_op jit(solution)/shard_map/ppermute | solution.py:363
  698.8 68.9 %collective-permute-start.32 = (bf16[320,1920]{1,0:T(8,128)(2,1)S(1)}, bf16[320,1920]{1,0:T(8,128)(2,1)S(1)}, u32[]{:S(2)}, u32[]{:S(2)}) collective-permute-start(bf16[320,1920]{1,0:T(8,128)(2,1)S(1)} %dynamic-slice_convert_fusion.2), channel_id=1, source_target_pairs={{0,4},{1,5},{2,6},{3,7},{4,0},{5,1},{6,2},{7,3},{8,12},{9,13},{10,... | collective-permute-start | bytes 3686408 | tf_op jit(solution)/shard_map/ppermute | solution.py:363
  739.4 45.8 %collective-permute-start.51 = (bf16[80,2560]{1,0:T(8,128)(2,1)S(1)}, bf16[80,2560]{1,0:T(8,128)(2,1)S(1)}, u32[]{:S(2)}, u32[]{:S(2)}) collective-permute-start(bf16[80,2560]{1,0:T(8,128)(2,1)S(1)} %add_convert_fusion.3), channel_id=1, source_target_pairs={{0,16},{1,17},{2,18},{3,19},{4,20},{5,21},{6,22},{7,23},{8,24},{9,... | collective-permute-start | bytes 1228808 | tf_op jit(solution)/shard_map/ppermute | solution.py:363
  785.3 45.2 %collective-permute-start.52 = (bf16[160,2560]{1,0:T(8,128)(2,1)S(1)}, bf16[160,2560]{1,0:T(8,128)(2,1)S(1)}, u32[]{:S(2)}, u32[]{:S(2)}) collective-permute-start(bf16[160,2560]{1,0:T(8,128)(2,1)S(1)} %pad_maximum_fusion.39), channel_id=1, source_target_pairs={{0,8},{1,9},{2,10},{3,11},{4,12},{5,13},{6,14},{7,15},{8,0},{9,1},... | collective-permute-start | bytes 2457608 | tf_op jit(solution)/shard_map/ppermute | solution.py:363
  800.4 47.6 %collective-permute-start.60 = (bf16[320,1280]{1,0:T(8,128)(2,1)S(1)}, bf16[320,1280]{1,0:T(8,128)(2,1)S(1)}, u32[]{:S(2)}, u32[]{:S(2)}) collective-permute-start(bf16[320,1280]{1,0:T(8,128)(2,1)S(1)} %pad_maximum_fusion.40), channel_id=1, source_target_pairs={{0,8},{1,9},{2,10},{3,11},{4,12},{5,13},{6,14},{7,15},{8,0},{9,1},... | collective-permute-start | bytes 2457608 | tf_op jit(solution)/shard_map/ppermute | solution.py:363
  830.8 38.8 %collective-permute-start.53 = (bf16[320,2560]{1,0:T(8,128)(2,1)S(1)}, bf16[320,2560]{1,0:T(8,128)(2,1)S(1)}, u32[]{:S(2)}, u32[]{:S(2)}) collective-permute-start(bf16[320,2560]{1,0:T(8,128)(2,1)S(1)} %pad_maximum_fusion.28), channel_id=1, source_target_pairs={{0,4},{1,5},{2,6},{3,7},{4,0},{5,1},{6,2},{7,3},{8,12},{9,13},{10,... | collective-permute-start | bytes 4915208 | tf_op jit(solution)/shard_map/ppermute | solution.py:363
  848.4 82.8 %collective-permute-start.61 = (bf16[640,1280]{1,0:T(8,128)(2,1)S(1)}, bf16[640,1280]{1,0:T(8,128)(2,1)S(1)}, u32[]{:S(2)}, u32[]{:S(2)}) collective-permute-start(bf16[640,1280]{1,0:T(8,128)(2,1)S(1)} %pad_maximum_fusion.29), channel_id=1, source_target_pairs={{0,4},{1,5},{2,6},{3,7},{4,0},{5,1},{6,2},{7,3},{8,12},{9,13},{10,... | collective-permute-start | bytes 4915208 | tf_op jit(solution)/shard_map/ppermute | solution.py:363
  860.4 67.6 %collective-permute-start.37 = (bf16[320,1920]{1,0:T(8,128)(2,1)S(1)}, bf16[320,1920]{1,0:T(8,128)(2,1)S(1)}, u32[]{:S(2)}, u32[]{:S(2)}) collective-permute-start(bf16[320,1920]{1,0:T(8,128)(2,1)S(1)} %pad_maximum_fusion.34), channel_id=1, source_target_pairs={{0,4},{1,5},{2,6},{3,7},{4,0},{5,1},{6,2},{7,3},{8,12},{9,13},{10,... | collective-permute-start | bytes 3686408 | tf_op jit(solution)/shard_map/ppermute | solution.py:363
  872.1 88.4 %collective-permute-start.54 = (bf16[640,2560]{1,0:T(8,128)(2,1)}, bf16[640,2560]{1,0:T(8,128)(2,1)}, u32[]{:S(2)}, u32[]{:S(2)}) collective-permute-start(bf16[640,2560]{1,0:T(8,128)(2,1)} %pad_maximum_fusion.14), channel_id=1, source_target_pairs={{0,2},{1,3},{2,0},{3,1},{4,6},{5,7},{6,4},{7,5},{8,10},{9,11},{10,... | collective-permute-start | bytes 9830408 | tf_op jit(solution)/shard_map/ppermute | solution.py:363
  (103 other events, 1305.1 us)

commit v2 on v1

--- a/solution.py
+++ b/solution.py
@@ -352,7 +352,6 @@
 
 
 BOTH = ("cell", "seq")
-SEQ_BIT = 1
 CORE_BIT = 2
 Q_BLOCK = 512
 VMEM = 48 * 1024 * 1024
@@ -380,36 +379,334 @@
     return lax.dynamic_slice_in_dim(value, index * size, size, axis)
 
 
-class Place:
+MESH = pl.DeviceIdType.MESH
+ANY = pl.BlockSpec(memory_space=pl.ANY)
+EDGE = 640
+
+
+class Spot:
     def __init__(self):
         self.x = lax.axis_index("seq")
-        cell = lax.axis_index("cell")
-        self.core = cell % 2
-        self.bits = []
-        bit = 2
-        while bit < lax.axis_size("cell"):
-            self.bits.append((2 * bit, (cell // bit) % 2))
-            bit *= 2
-
-    def share(self, value):
-        for _, index in self.bits:
-            value = half_of(value, index)
-        return value
-
-    def widen(self, block):
-        for bit, index in reversed(self.bits):
-            block = in_order(index == 0, block, across(block, bit))
-        return block
-
-    def fetch(self, piece):
-        return self.widen(across(self.share(piece), SEQ_BIT))
-
-    def add_up(self, keep, give):
-        total = keep.astype(jnp.float32) + across(give, SEQ_BIT).astype(jnp.float32)
-        for bit, index in self.bits:
-            send = half_of(total, 1 - index).astype(jnp.bfloat16)
-            total = half_of(total, index) + across(send, bit).astype(jnp.float32)
-        return self.widen(total.astype(jnp.bfloat16))
+        self.cell = lax.axis_index("cell")
+        self.core = lax.rem(self.cell, 2)
+        self.y = lax.rem(self.cell // 2, 2)
+        self.low = lax.rem(self.cell // 4, 2)
+        self.high = lax.rem(self.cell // 8, 2)
+
+    def flip(self, index, bit):
+        return {"cell": self.cell + bit - 2 * bit * index}
+
+    def over(self, name):
+        if name == "x":
+            return {"seq": 1 - self.x}
+        if name == "core":
+            return self.flip(self.core, 1)
+        if name == "diagonal":
+            return {"seq": 1 - self.x, **self.flip(self.core, 1)}
+        return self.flip(*{"y": (self.y, 2), "low": (self.low, 4), "high": (self.high, 8)}[name])
+
+    def meet(self, names):
+        barrier = pltpu.get_barrier_semaphore()
+        for name in names:
+            pl.semaphore_signal(barrier, inc=1, device_id=self.over(name), device_id_type=MESH)
+        pl.semaphore_wait(barrier, len(names))
+
+    def send(self, name, source, target, send_sem, recv_sem):
+        return pltpu.make_async_remote_copy(
+            source, target, send_sem, recv_sem, device_id=self.over(name), device_id_type=MESH
+        )
+
+
+def rows_at(start, size):
+    return pl.ds(pl.multiple_of(start, 16), size)
+
+
+def lanes_at(start, size):
+    return pl.ds(pl.multiple_of(start, 128), size)
+
+
+def gather_kernel(
+    tokens, out_grad, cell_weight, vectors, wq, wk, wv, wo, wup, wdown,
+    own, own_grad, own_weight, all_vectors, qkv_w, out_w, up_w, down_w,
+    send_sems, recv_sems, local_sems, side_send, side_recv, side_local,
+):
+    at = Spot()
+    x, core = at.x, at.core
+    at.meet(("x", "core", "diagonal", "y", "low", "high"))
+    side = [(tokens, own), (cell_weight, own_weight), (out_grad, own_grad)]
+    diagonal = [at.send("diagonal", s, t, side_send.at[i], side_recv.at[i]) for i, (s, t) in enumerate(side)]
+    straight = [pltpu.make_async_copy(s, t, side_local.at[i]) for i, (s, t) in enumerate(side)]
+
+    def swap_start(i):
+        @pl.when(x != core)
+        def _():
+            diagonal[i].start()
+
+        @pl.when(x == core)
+        def _():
+            straight[i].start()
+
+    swap_start(0)
+    swap_start(1)
+    vector_copy = at.send("x", vectors, all_vectors.at[x], side_send.at[3], side_recv.at[3])
+    vector_copy.start()
+    vector_local = pltpu.make_async_copy(vectors, all_vectors.at[x], side_local.at[3])
+    vector_local.start()
+
+    chunks = []
+    for i, ref in enumerate((wq, wk, wv)):
+        chunks.append((ref.at[:, lanes_at(core * EDGE, EDGE)], qkv_w, EDGE, 0, i * EDGE))
+    for i in range(4):
+        start = (i // 2) * 4 * EDGE + core * 2 * EDGE + (i % 2) * EDGE
+        chunks.append((wup.at[:, lanes_at(start, EDGE)], up_w, EDGE, 0, i * EDGE))
+    for i in range(4):
+        source = wdown.at[rows_at(core * 2 * EDGE + (i // 2) * EDGE, EDGE), pl.ds((i % 2) * EDGE, EDGE)]
+        chunks.append((source, down_w, 2 * EDGE, (i // 2) * EDGE, (i % 2) * EDGE))
+    eighth = EDGE // 8
+    place = at.y * 4 + at.low * 2 + at.high
+
+    def region(k, half, start, size):
+        _, ref, stride, row, column = chunks[k]
+        return ref.at[rows_at(half * stride + row + start * eighth, size * eighth), pl.ds(column, EDGE)]
+
+    stages = {}
+    for k, chunk in enumerate(chunks):
+        stages["x", k] = at.send(
+            "x", chunk[0].at[rows_at(place * eighth, eighth)], region(k, x, place, 1), send_sems.at[0, k], recv_sems.at[0, k]
+        )
+        for s, (name, start, size) in enumerate(
+            (("high", place, 1), ("low", at.y * 4 + at.low * 2, 2), ("y", at.y * 4, 4))
+        ):
+            part = region(k, 1 - x, start, size)
+            stages[name, k] = at.send(name, part, part, send_sems.at[s + 1, k], recv_sems.at[s + 1, k])
+        stages["local", k] = pltpu.make_async_copy(chunk[0], region(k, x, 0, 8), local_sems.at[k])
+
+    half = EDGE // 2
+    out_x = at.send(
+        "x", wo.at[rows_at(core * half, half)], out_w.at[rows_at(x * EDGE + core * half, half)], side_send.at[4], side_recv.at[4]
+    )
+    part = out_w.at[rows_at((1 - x) * EDGE + core * half, half)]
+    out_core = at.send("core", part, part, side_send.at[5], side_recv.at[5])
+    out_local = pltpu.make_async_copy(wo, out_w.at[rows_at(x * EDGE, EDGE)], side_local.at[4])
+
+    count = len(chunks)
+    for k in range(3):
+        stages["x", k].start()
+    out_x.start()
+    for k in range(3, count):
+        stages["x", k].start()
+    swap_start(2)
+    for k in range(count):
+        stages["local", k].start()
+    out_local.start()
+    for tick in range(count + 3):
+        for before, name, after in ((0, "x", "high"), (1, "high", "low"), (2, "low", "y"), (3, "y", None)):
+            k = tick - before
+            if 0 <= k < count:
+                stages[name, k].wait_recv()
+                if after:
+                    stages[after, k].start()
+        if tick == 3:
+            out_x.wait_recv()
+            out_core.start()
+    out_core.wait_recv()
+    vector_copy.wait()
+    vector_local.wait()
+    for i in range(3):
+
+        @pl.when(x != core)
+        def _():
+            diagonal[i].wait()
+
+        @pl.when(x == core)
+        def _():
+            straight[i].wait()
+
+    for k in range(count):
+        stages["local", k].wait()
+        for name in ("x", "high", "low", "y"):
+            stages[name, k].wait_send()
+    out_local.wait()
+    out_x.wait_send()
+    out_core.wait_send()
+
+
+def gather(*args):
+    tokens = args[0]
+    bf16 = jnp.bfloat16
+    shape = jax.ShapeDtypeStruct
+    width = tokens.shape[1]
+    vectors = args[3]
+    return pl.pallas_call(
+        gather_kernel,
+        in_specs=[ANY] * len(args),
+        out_specs=[ANY] * 8,
+        out_shape=[
+            shape(tokens.shape, bf16),
+            shape(tokens.shape, bf16),
+            shape(args[2].shape, jnp.float32),
+            shape((2,) + vectors.shape, bf16),
+            shape((width, 3 * EDGE), bf16),
+            shape((width, width), bf16),
+            shape((width, 4 * EDGE), bf16),
+            shape((4 * EDGE, width), bf16),
+        ],
+        scratch_shapes=[
+            pltpu.SemaphoreType.DMA((4, 11)),
+            pltpu.SemaphoreType.DMA((4, 11)),
+            pltpu.SemaphoreType.DMA((11,)),
+            pltpu.SemaphoreType.DMA((6,)),
+            pltpu.SemaphoreType.DMA((6,)),
+            pltpu.SemaphoreType.DMA((5,)),
+        ],
+        compiler_params=pltpu.CompilerParams(collective_id=0, has_side_effects=True),
+        name="gather",
+    )(*args)
+
+
+def reduce_kernel(
+    give_down, keep_down, give_up, keep_up, give_out, keep_out, give_qkv, keep_qkv, vec,
+    down_ref, up_ref, out_ref, q_ref, k_ref, v_ref, vec_ref,
+    acc, from_x, from_y, from_low, from_high, res, vec_acc, vec_in,
+    send_sems, recv_sems, load_sems, store_sems, vec_send, vec_recv, vec_local,
+):
+    f32, bf16 = jnp.float32, jnp.bfloat16
+    at = Spot()
+    core = at.core
+    at.meet(("x", "core", "y", "low", "high"))
+    chunks = []
+    for i in range(4):
+        part = (pl.ds((i // 2) * EDGE, EDGE), pl.ds((i % 2) * EDGE, EDGE))
+        target = down_ref.at[rows_at(core * 2 * EDGE + (i // 2) * EDGE, EDGE), pl.ds((i % 2) * EDGE, EDGE)]
+        chunks.append((give_down.at[part], keep_down.at[part], target))
+    for i in range(4):
+        part = (slice(None), pl.ds(i * EDGE, EDGE))
+        target = up_ref.at[:, lanes_at((i // 2) * 4 * EDGE + core * 2 * EDGE + (i % 2) * EDGE, EDGE)]
+        chunks.append((give_up.at[part], keep_up.at[part], target))
+    mine = lanes_at(core * EDGE, EDGE)
+    chunks.append((give_out, keep_out, out_ref.at[:, mine]))
+    for i, ref in enumerate((q_ref, k_ref, v_ref)):
+        part = (slice(None), pl.ds(i * EDGE, EDGE))
+        chunks.append((give_qkv.at[part], keep_qkv.at[part], ref.at[:, mine]))
+    count = len(chunks)
+
+    half, quarter, eighth = EDGE // 2, EDGE // 4, EDGE // 8
+    y0 = at.y * half
+    l0 = y0 + at.low * quarter
+    h0 = l0 + at.high * eighth
+    ops = {}
+    for k, (give, keep, target) in enumerate(chunks):
+        hops = (
+            ("x", "x", give, from_x.at[k]),
+            ("y", "y", acc.at[k, rows_at((1 - at.y) * half, half)], from_y.at[k]),
+            ("low", "low", acc.at[k, rows_at(y0 + (1 - at.low) * quarter, quarter)], from_low.at[k]),
+            ("high", "high", acc.at[k, rows_at(l0 + (1 - at.high) * eighth, eighth)], from_high.at[k]),
+            ("all_high", "high", res.at[k, rows_at(h0, eighth)], res.at[k, rows_at(h0, eighth)]),
+            ("all_low", "low", res.at[k, rows_at(l0, quarter)], res.at[k, rows_at(l0, quarter)]),
+            ("all_y", "y", res.at[k, rows_at(y0, half)], res.at[k, rows_at(y0, half)]),
+            ("core", "core", res.at[k], target),
+        )
+        for s, (stage, name, source, goal) in enumerate(hops):
+            ops[stage, k] = at.send(name, source, goal, send_sems.at[s, k], recv_sems.at[s, k])
+        ops["load", k] = pltpu.make_async_copy(keep, acc.at[k], load_sems.at[k])
+        ops["store", k] = pltpu.make_async_copy(res.at[k], target, store_sems.at[k])
+
+    def add(k, start, size, other, goal):
+        @pl.loop(0, size // 80)
+        def _(i):
+            here = rows_at(start + i * 80, 80)
+            there = rows_at(i * 80, 80)
+            goal[k, here, :] = (acc[k, here, :].astype(f32) + other[k, there, :].astype(f32)).astype(bf16)
+
+    for k in range(count):
+        ops["x", k].start()
+        ops["load", k].start()
+    vec_load = pltpu.make_async_copy(vec, vec_acc.at[0], vec_local.at[0])
+    vec_load.start()
+    vec_load.wait()
+    vec_names = ("x", "core", "y", "low", "high")
+    vec_ops = [
+        at.send(name, vec_acc.at[i], vec_in.at[i], vec_send.at[i], vec_recv.at[i]) for i, name in enumerate(vec_names)
+    ]
+    vec_ops[0].start()
+    after = ("y", "low", "high", "all_high", "all_low", "all_y", "core", None)
+    stages = ("x",) + after[:-1]
+    for tick in range(count + 7):
+        for before, (stage, following) in enumerate(zip(stages, after)):
+            k = tick - before
+            if not 0 <= k < count:
+                continue
+            ops[stage, k].wait_recv()
+            if stage == "x":
+                ops["load", k].wait()
+                add(k, 0, EDGE, from_x, acc)
+            elif stage == "y":
+                add(k, y0, half, from_y, acc)
+            elif stage == "low":
+                add(k, l0, quarter, from_low, acc)
+            elif stage == "high":
+                add(k, h0, eighth, from_high, res)
+            if following:
+                ops[following, k].start()
+            if stage == "all_y":
+                ops["store", k].start()
+        if tick < 5:
+            vec_ops[tick].wait_recv()
+            vec_acc[tick + 1] = vec_acc[tick] + vec_in[tick]
+            if tick < 4:
+                vec_ops[tick + 1].start()
+    vec_store = pltpu.make_async_copy(vec_acc.at[5], vec_ref, vec_local.at[1])
+    vec_store.start()
+    vec_store.wait()
+    for op in vec_ops:
+        op.wait_send()
+    for k in range(count):
+        for stage in stages:
+            ops[stage, k].wait_send()
+        ops["store", k].wait()
+
+
+def reduce(*args):
+    bf16, f32 = jnp.bfloat16, jnp.float32
+    shape = jax.ShapeDtypeStruct
+    vec = args[-1]
+    count = 12
+    square = shape((EDGE, 2 * EDGE), bf16)
+    return pl.pallas_call(
+        reduce_kernel,
+        in_specs=[ANY] * len(args),
+        out_specs=[ANY] * 7,
+        out_shape=[
+            shape((4 * EDGE, 2 * EDGE), bf16),
+            shape((EDGE, 8 * EDGE), bf16),
+            square,
+            square,
+            square,
+            square,
+            shape(vec.shape, f32),
+        ],
+        scratch_shapes=[
+            pltpu.VMEM((count, EDGE, EDGE), bf16),
+            pltpu.VMEM((count, EDGE, EDGE), bf16),
+            pltpu.VMEM((count, EDGE // 2, EDGE), bf16),
+            pltpu.VMEM((count, EDGE // 4, EDGE), bf16),
+            pltpu.VMEM((count, EDGE // 8, EDGE), bf16),
+            pltpu.VMEM((count, EDGE, EDGE), bf16),
+            pltpu.VMEM((6,) + vec.shape, f32),
+            pltpu.VMEM((5,) + vec.shape, f32),
+            pltpu.SemaphoreType.DMA((8, count)),
+            pltpu.SemaphoreType.DMA((8, count)),
+            pltpu.SemaphoreType.DMA((count,)),
+            pltpu.SemaphoreType.DMA((count,)),
+            pltpu.SemaphoreType.DMA((5,)),
+            pltpu.SemaphoreType.DMA((5,)),
+            pltpu.SemaphoreType.DMA((2,)),
+        ],
+        compiler_params=pltpu.CompilerParams(
+            collective_id=1, has_side_effects=True, vmem_limit_bytes=56 * 1024 * 1024
+        ),
+        name="reduce",
+    )(*args)
 
 
 def attend_kernel(q_ref, k_ref, v_ref, mixed_ref, total_ref):
@@ -564,47 +861,35 @@
     down_bias,
 ):
     f32, bf16 = jnp.float32, jnp.bfloat16
-    at = Place()
-    x, core = at.x, at.core
+    x = lax.axis_index("seq")
+    core = lax.axis_index("cell") % 2
     swapped = x != core
     rows, width = tokens.shape[1:]
     hidden_width = up_weight.shape[1] // 2
     head_width = width // 2
 
-    vectors = (first_gain, first_bias, query_bias, value_bias, output_bias, second_gain, second_bias, down_bias, up_bias)
-    packed = jnp.concatenate(vectors)
-    packed = in_order(x == 0, packed[None], across(packed, SEQ_BIT)[None])
-    full = []
-    start = 0
-    for vector in vectors:
-        full.append(packed[:, start : start + vector.shape[0]].reshape(-1).astype(f32))
-        start += vector.shape[0]
-    gain_one, bias_one, q_bias, v_bias, o_bias, gain_two, bias_two, d_bias, u_bias = full
-
-    own = tokens[0]
-    own = jnp.where(swapped, across_diagonal(own), own)
-    own_grad = out_grad[0]
-    own_grad = jnp.where(swapped, across_diagonal(own_grad), own_grad)
-    weight_cell = jnp.broadcast_to(jnp.sqrt(query_counts.astype(f32) / 1000.0), (8, 128))
-    weight_cell = jnp.where(swapped, across_diagonal(weight_cell), weight_cell)[:1, :1]
-
-    def columns(weight):
-        return half_of(weight, core, 1)
-
-    def up_columns(weight):
-        halves = weight.reshape(weight.shape[0], 2, 2, hidden_width // 2)
-        halves = lax.dynamic_index_in_dim(halves, core, 2, keepdims=False)
-        return halves.reshape(weight.shape[0], hidden_width)
-
-    qkv_piece = jnp.concatenate([columns(query_weight), columns(key_weight), columns(value_weight)], axis=1)
-    qkv_weight = in_order(x == 0, qkv_piece, at.fetch(qkv_piece))
-    out_piece = at.fetch(half_of(output_weight, core))
-    out_piece = in_order(core == 0, out_piece, across(out_piece, CORE_BIT))
-    out_weight = in_order(x == 0, output_weight, out_piece)
-    up_piece = up_columns(up_weight)
-    up_all = in_order(x == 0, up_piece, at.fetch(up_piece))
-    down_piece = half_of(down_weight, core)
-    down_all = in_order(x == 0, down_piece, at.fetch(down_piece))
+    vectors = (first_gain, first_bias, query_bias, value_bias, output_bias, second_gain, second_bias, down_bias)
+    vectors = jnp.stack(vectors)
+    vectors = jnp.pad(vectors, ((0, 15 - vectors.shape[0]), (0, hidden_width - vectors.shape[1])))
+    vectors = jnp.concatenate([vectors, up_bias[None]])
+    cell_weight = jnp.broadcast_to(jnp.sqrt(query_counts.astype(f32) / 1000.0), (8, 128))
+    own, own_grad, cell_weight, vectors, qkv_weight, out_weight, up_all, down_all = gather(
+        tokens[0],
+        out_grad[0],
+        cell_weight,
+        vectors,
+        query_weight,
+        key_weight,
+        value_weight,
+        output_weight,
+        up_weight,
+        down_weight,
+    )
+    weight_cell = cell_weight[:1, :1]
+    vectors = vectors.astype(f32)
+    short = [vectors[:, i, :head_width].reshape(-1) for i in range(8)]
+    gain_one, bias_one, q_bias, v_bias, o_bias, gain_two, bias_two, d_bias = short
+    u_bias = vectors[:, 15].reshape(-1)
 
     own = own.astype(f32)
     standard_one, inverse_one = standardize(own)
@@ -633,7 +918,7 @@
     def weight_sum(left, right):
         give = weight_grad(half_of(left, 1 - x, 1), right).astype(bf16)
         keep = weight_grad(half_of(left, x, 1), right).astype(bf16)
-        return at.add_up(keep, give)
+        return give, keep
 
     sum_down = weight_sum(hidden, grad_ffn)
     grad_up = (matmul_right_t(grad_ffn, down_all) * gelu_slope(up_proj)).astype(bf16)
@@ -676,64 +961,43 @@
         column_sum(grad_own),
         up_sum,
     ]
-    sums = [half_of(v, x) for v in jnp.split(lax.psum(jnp.concatenate(sums), BOTH), np_offsets(sums))]
+    sizes = [value.shape[0] for value in sums]
+    packed = jnp.concatenate(sums)
+    packed = jnp.pad(packed, (0, -packed.shape[0] % 8192)).reshape(-1, 1024)
+    down_sum, up_sum, out_sum, *qkv_sum, packed = reduce(*sum_down, *sum_up, *sum_out, *sum_qkv, packed)
+    packed = packed.reshape(-1)
+    sums = []
+    for size in sizes:
+        sums.append(half_of(packed[:size], x))
+        packed = packed[size:]
     s_gain_one, s_bias_one, s_q_bias, s_v_bias, s_o_bias, s_gain_two, s_bias_two, s_d_bias, s_u_bias = sums
 
-    def both_columns(value):
-        return in_order(core == 0, value, across(value, CORE_BIT), axis=1).astype(f32)
-
-    other = across(sum_qkv, CORE_BIT)
-    each = [
-        in_order(
-            core == 0,
-            sum_qkv[:, i * head_width : (i + 1) * head_width],
-            other[:, i * head_width : (i + 1) * head_width],
-            axis=1,
-        ).astype(f32)
-        for i in range(3)
-    ]
-    up_own = sum_up.reshape(-1, 2, hidden_width // 2)
-    up_other = across(sum_up, CORE_BIT).reshape(-1, 2, hidden_width // 2)
-    s_up = jnp.concatenate(
-        [in_order(core == 0, up_own[:, h], up_other[:, h], axis=1) for h in range(2)], axis=1
-    ).astype(f32)
-    s_down = in_order(core == 0, sum_down, across(sum_down, CORE_BIT)).astype(f32)
     return (
         result[None],
         input_grad[None],
         s_gain_one,
         s_bias_one,
-        each[0],
+        qkv_sum[0].astype(f32),
         s_q_bias,
-        each[1],
-        each[2],
+        qkv_sum[1].astype(f32),
+        qkv_sum[2].astype(f32),
         s_v_bias,
-        both_columns(sum_out),
+        out_sum.astype(f32),
         s_o_bias,
         s_gain_two,
         s_bias_two,
-        s_up,
+        up_sum.astype(f32),
         s_u_bias,
-        s_down,
+        down_sum.astype(f32),
         s_d_bias,
     )
-
-
-def np_offsets(values):
-    offsets = []
-    total = 0
-    for value in values[:-1]:
-        total += value.shape[0]
-        offsets.append(total)
-    return offsets
 
 
 def chosen(mesh):
     cells, blocks = mesh.shape["cell"], mesh.shape["seq"]
 
     def per_device(tokens, *rest):
-        power = cells & (cells - 1) == 0
-        if blocks == 2 and power and cells >= 4 and tokens.shape[0] == 1:
+        if blocks == 2 and cells == 16 and tokens.shape == (1, 512, 1280):
             return tuned(tokens, *rest)
         return general(tokens, *rest)
 

time: 997 us -> 1110 us (1.11)
  Pallas kernels: 55.5 us -> 903 us
  waiting for transfers between devices: 374 us -> 5.96 us
  starting transfers between devices: 166 us -> 5.12 us
  local copies, waits for them, and re-layouts: 137 us -> 27 us
  other arithmetic: 104 us -> 46.8 us
  blocking collectives: 49.5 us -> 0 us
  matrix products: 101 us -> 114 us
    pallas_call x0 -> x2, Pallas kernels: none -> 848 us  [the longest x1 437 us: reduce(): pl.pallas_call(reduce_kernel, in_specs=[ANY] * len(args), out_specs=[ANY]...]
    ppermute x58 -> x8, waiting for transfers between devices: 374 us -> 5.96 us  [across(): return lax.ppermute(value, BOTH, [(i, i ^ bit) for i in range(count)])]
    ppermute x58 -> x8, starting transfers between devices: 161 us -> 3.39 us  [across(): return lax.ppermute(value, BOTH, [(i, i ^ bit) for i in range(count)])]
    dynamic_slice x1 -> x0, local copies, waits for them, and re-layouts: 51.3 us -> none  [up_columns(): halves = lax.dynamic_index_in_dim(halves, core, 2, keepdims=False)]
    psum x1 -> x0, blocking collectives: 49.5 us -> none  [tuned(): lax.psum(jnp.concatenate(sums), BOTH)]
    select_n x35 -> x0, other arithmetic: 38.5 us -> none  [the longest x34 38.5 us: in_order(): low = jnp.where(first, own, received)]
    reshape x3 -> x1, local copies, waits for them, and re-layouts: 28.6 us -> 0.63 us  [tuned(): packed = jnp.pad(packed, (0, -packed.shape[0] % 8192)).reshape(-1, 1024)]
    unnamed x161 -> x91, local copies, waits for them, and re-layouts: 21.6 us -> 5.61 us
  transfers between devices with their start and end apart: 63 -> 10, of which waited for: 25 -> 2; matrix products, arithmetic and copies ran while one was open for 28% -> 11% of each run, Pallas kernels for 6% -> 43%
where the time goes in v2:
time: 1110 us; the launch traced here: 1100 us
  Pallas kernels  903 us (81%)
  matrix products  114 us (10%)
  other arithmetic  46.8 us (4%)
  local copies, waits for them, and re-layouts  27 us (2%)
    pallas_call x1, Pallas kernels, reduce(): pl.pallas_call(reduce_kernel, in_specs=[ANY] * len(args), out_specs=[ANY]...  437 us
    pallas_call x1, Pallas kernels, gather(): pl.pallas_call(gather_kernel, in_specs=[ANY] * len(args), out_specs=[ANY]...  411 us
    dot_general x8, matrix products, weight_grad(): jnp.einsum('ti,to->io', left, right, preferred_element_type=jnp.float32)  44.8 us
    dot_general x4, matrix products, matmul_right_t(): jnp.einsum('to,io->ti', left, right, preferred_element_type=jnp.float32)  34.8 us
    pallas_call x1, Pallas kernels, attend_back(): pl.pallas_call(attend_back_kernel, grid=(pairs,), in_specs=[block, pl.Blo...  34.3 us
    dot_general x4, matrix products, matmul(): return jnp.dot(left, right, preferred_element_type=jnp.float32)  34.2 us
  transfers between devices with their start and end apart: 10, of which 2 were waited for; matrix products, arithmetic and copies ran while one was open for 11% of the time, Pallas kernels for 43%

profile of v2, /device:TPU:0, one launch (start us, length us, event | category | flops | bytes accessed | tf_op | source)
XLA Modules:
  0.0 1104.4 jit_solution(17062831424237550422)
XLA Ops:
  8.8 410.8 %gather.1 = (bf16[512,1280]{1,0:T(8,128)(2,1)}, bf16[512,1280]{1,0:T(8,128)(2,1)}, f32[8,128]{1,0:T(8,128)}, bf16[2,16,2560]{2,1,0:T(8,128)(2,1)}, bf16[1280,192...) custom-call(bf16[512,1280]{1,0:T(8,128)(2,1)} %bitcast.29, ...), custom_call_target="tpu_custom_call" | custom-call | tf_op jit(solution)/shard_map/gather/pallas_call | solution.py:540
  423.8 2.9 collective-permute-done
  426.8 8.7 add_convert_fusion.q_ref.k_ref.v_ref
  435.5 21.0 %attend.1 = (bf16[1024,640]{1,0:T(8,128)(2,1)S(1)}, f32[10,1,1024]{2,1,0:T(1,128)S(1)}) custom-call(bf16[1024,1920]{1,0:T(8,128)(2,1)S(1)} %add_convert_fusion.q_ref.k_ref.v_ref, bf16[1024,1920]{1,0:T(8,128)(2,1)S(1)} %add_convert_fusion.q_ref.k_ref.v_ref, bf16[1024,1920]{1,0:T(8,128)(2,1)S(1)} %add_convert_fusion.q_ref.k_ref.v_ref), custom_call_target="tpu_custom_call" | custom-call | flops 10737418240 | bytes 5242880 | tf_op jit(solution)/shard_map/attend/pallas_call | solution.py:793
  456.8 3.0 collective-permute-done.1
  461.8 2.3 copy-done.27
  464.1 2.0 fusion.81
  468.9 2.6 convert_reduce_fusion.3
  472.1 13.5 %multiply_convert_fusion = (bf16[1024,2560]{1,0:T(8,128)(2,1)}, f32[1024,2560]{1,0:T(8,128)}) fusion(f32[2560]{0:T(1024)S(1)} %add.164, bf16[1280,2560]{1,0:T(8,128)(2,1)} %get-tuple-element.42, bf16[512,1280]{1,0:T(8,128)(2,1)} %collective-permute-done.2, bf16[512,1280]{1,0:T(8,128)(2,1)S(1)} %add_convert_fusion.1), kind=kOutput, calls=%fused_computation.8 | convolution fusion | flops 6731857920 | bytes 24913920 | tf_op jit(solution)/shard_map/dot_general | solution.py:23
  485.6 15.5 %convert_reduce_fusion = (f32[2560]{0:T(1024)S(1)}, bf16[1024,2560]{1,0:T(8,128)(2,1)}) fusion(f32[1024,2560]{1,0:T(8,128)} %get-tuple-element.96, f32[2560]{0:T(1024)S(1)} %add.164, bf16[2560,1280]{1,0:T(8,128)(2,1)} %get-tuple-element.43, bf16[512,1280]{1,0:T(8,128)(2,1)} %collective-permute-done.5, bf16[512,1280]{1,0:T(8,128)(2,1)} %get-tuple-element.74), kind=kOutput, calls=%fused_computation.7 | convolution fusion | flops 6750205440 | bytes 24924160 | tf_op jit(solution)/shard_map/to,io->ti/dot_general | solution.py:27
  501.1 8.9 fusion.83
  511.5 10.0 fusion.82
  524.4 8.3 convolution_convert_fusion.3.give_up
  532.8 8.0 convolution_convert_fusion.1.give_down
  542.2 3.9 convert_reduce_fusion.4
  546.5 7.0 convolution_convert_fusion.keep_down
  553.6 6.5 convolution_convert_fusion.2.keep_up
  560.8 2.2 fusion.31.grad_ref
  563.0 34.3 %attend_back.1 = (bf16[1024,640]{1,0:T(8,128)(2,1)S(1)}, bf16[1024,640]{1,0:T(8,128)(2,1)S(1)}, bf16[1024,640]{1,0:T(8,128)(2,1)S(1)}) custom-call(bf16[1024,1920]{1,0:T(8,128)(2,1)} %copy-done, bf16[1024,1920]{1,0:T(8,128)(2,1)} %copy-done, bf16[1024,1920]{1,0:T(8,128)(2,1)} %copy-done, f32[10,1,1024]{2,1,0:T(1,128)S(1)} %get-tuple-element.46.total_ref, ...), custom_call_target="tpu_custom_call" | custom-call | flops 26843545600 | bytes 9175040 | tf_op jit(solution)/shard_map/attend_back/pallas_call | solution.py:822
  598.0 8.2 fusion.84
  606.3 1.9 collective-permute-start.8
  608.2 2.2 convolution_convert_fusion.7.give_out
  612.2 2.2 convolution_convert_fusion.6.keep_out
  614.5 5.2 convolution_convert_fusion.5.give_qkv
  619.7 5.4 convolution_convert_fusion.4.keep_qkv
  629.5 437.0 %reduce.21 = (bf16[2560,1280]{1,0:T(8,128)(2,1)}, bf16[640,5120]{1,0:T(8,128)(2,1)}, bf16[640,1280]{1,0:T(8,128)(2,1)}, bf16[640,1280]{1,0:T(8,128)(2,1)}, bf16[...) custom-call(bf16[1280,1280]{1,0:T(8,128)(2,1)} %convolution_convert_fusion.1.give_down, ...), custom_call_target="tpu_custom_call" | custom-call | tf_op jit(solution)/shard_map/reduce/pallas_call | solution.py:675
  1070.5 3.4 convert_element_type.141
  1074.6 2.0 convert_element_type.142
  1076.5 2.0 convert_element_type.143
  1079.1 2.0 convert_element_type.144
  1083.1 9.6 convert_element_type.145
  1092.7 8.8 convert_element_type.146
  (195 shorter events, 40.5 us)
Async XLA Ops:
  423.5 3.2 collective-permute-start
  435.5 21.0 %copy-start = (bf16[1024,1920]{1,0:T(8,128)(2,1)}, bf16[1024,1920]{1,0:T(8,128)(2,1)S(1)}, u32[]{:S(2)}) copy-start(bf16[1024,1920]{1,0:T(8,128)(2,1)S(1)} %add_convert_fusion.q_ref.k_ref.v_ref) | copy-start | bytes 11796484
  456.5 3.2 collective-permute-start.1
  467.6 18.0 %copy-start.13 = (bf16[512,1280]{1,0:T(8,128)(2,1)}, bf16[512,1280]{1,0:T(8,128)(2,1)S(1)}, u32[]{:S(2)}) copy-start(bf16[512,1280]{1,0:T(8,128)(2,1)S(1)} %add_convert_fusion.1) | copy-start | bytes 3932164
  467.6 4.5 collective-permute-start.2
  471.5 14.1 %collective-permute-start.5 = (bf16[512,1280]{1,0:T(8,128)(2,1)}, bf16[512,1280]{1,0:T(8,128)(2,1)}, u32[]{:S(2)}, u32[]{:S(2)}) collective-permute-start(bf16[512,1280]{1,0:T(8,128)(2,1)} %get-tuple-element.74), channel_id=1, source_target_pairs={{0,2},{1,3},{2,0},{3,1},{4,6},{5,7},{6,4},{7,5},{8,10},{9,11},{10,... | collective-permute-start | bytes 3932168 | tf_op jit(solution)/shard_map/ppermute | solution.py:362
  472.1 29.0 %slice-start.6 = ((s8[6553600]{0:T(1024)(128)(4,1)}), s8[4194304]{0:T(1024)(128)(4,1)S(1)}, s32[]{:S(2)}) async-start(s8[6553600]{0:T(1024)(128)(4,1)} %bitcast.36), calls=%async_computation.6 | async-start | bytes 8388608
  472.1 39.4 %slice-start.4 = ((s8[6553600]{0:T(1024)(128)(4,1)}), s8[4194304]{0:T(1024)(128)(4,1)S(1)}, s32[]{:S(2)}) async-start(s8[6553600]{0:T(1024)(128)(4,1)} %bitcast.34), calls=%async_computation.4 | async-start | bytes 8388608
  485.6 15.5 %slice-start.7 = ((s8[6553600]{0:T(1024)(128)(4,1)}), s8[2359296]{0:T(1024)(128)(4,1)S(1)}, s32[]{:S(2)}) async-start(s8[6553600]{0:T(1024)(128)(4,1)} %bitcast.36), calls=%async_computation.7 | async-start | bytes 4718592
  485.6 25.9 %slice-start.5 = ((s8[6553600]{0:T(1024)(128)(4,1)}), s8[2359296]{0:T(1024)(128)(4,1)S(1)}, s32[]{:S(2)}) async-start(s8[6553600]{0:T(1024)(128)(4,1)} %bitcast.34), calls=%async_computation.5 | async-start | bytes 4718592
  510.1 11.5 %copy-start.5 = (f32[1024,1280]{1,0:T(8,128)}, f32[1024,1280]{1,0:T(8,128)S(1)}, u32[]{:S(2)}) copy-start(f32[1024,1280]{1,0:T(8,128)S(1)} %fusion.83) | copy-start | bytes 15728644
  511.4 29.4 %collective-permute-start.6 = (bf16[512,1280]{1,0:T(8,128)(2,1)}, bf16[512,1280]{1,0:T(8,128)(2,1)S(1)}, u32[]{:S(2)}, u32[]{:S(2)}) collective-permute-start(bf16[512,1280]{1,0:T(8,128)(2,1)} %slice.242), channel_id=1, source_target_pairs={{0,2},{1,3},{2,0},{3,1},{4,6},{5,7},{6,4},{7,5},{8,10},{9,11},{10,... | collective-permute-start | bytes 3932168 | tf_op jit(solution)/shard_map/ppermute | solution.py:362
  524.2 17.9 %collective-permute-start.3 = (bf16[512,1280]{1,0:T(8,128)(2,1)}, bf16[512,1280]{1,0:T(8,128)(2,1)}, u32[]{:S(2)}, u32[]{:S(2)}) collective-permute-start(bf16[512,1280]{1,0:T(8,128)(2,1)} %slice.243), channel_id=1, source_target_pairs={{0,2},{1,3},{2,0},{3,1},{4,6},{5,7},{6,4},{7,5},{8,10},{9,11},{10,... | collective-permute-start | bytes 3932168 | tf_op jit(solution)/shard_map/ppermute | solution.py:362
  524.4 16.4 %slice-start = ((s8[5242880]{0:T(1024)(128)(4,1)}), s8[4194304]{0:T(1024)(128)(4,1)S(1)}, s32[]{:S(2)}) async-start(s8[5242880]{0:T(1024)(128)(4,1)} %bitcast.25), calls=%async_computation | async-start | bytes 8388608
  524.4 17.7 %slice-start.2 = ((s8[5242880]{0:T(1024)(128)(4,1)}), s8[4194304]{0:T(1024)(128)(4,1)S(1)}, s32[]{:S(2)}) async-start(s8[5242880]{0:T(1024)(128)(4,1)} %bitcast.27), calls=%async_computation.2 | async-start | bytes 8388608
  532.8 8.0 copy-start.2
  532.8 8.0 slice-start.1
  532.8 9.3 slice-start.3
  540.8 5.7 slice-start.10
  546.0 7.5 slice-start.8
  546.0 7.5 copy-start.14
  546.1 7.5 slice-start.9
  546.1 14.7 %collective-permute-start.7 = (bf16[512,1280]{1,0:T(8,128)(2,1)S(1)}, bf16[512,1280]{1,0:T(8,128)(2,1)S(1)}, u32[]{:S(2)}, u32[]{:S(2)}) collective-permute-start(bf16[512,1280]{1,0:T(8,128)(2,1)S(1)} %get-tuple-element.76), channel_id=1, source_target_pairs={{0,2},{1,3},{2,0},{3,1},{4,6},{5,7},{6,4},{7,5},{8,10},{9,11},{10,... | collective-permute-start | bytes 3932168 | tf_op jit(solution)/shard_map/ppermute | solution.py:362
  553.6 7.2 copy-start.28
  560.0 51.0 %collective-permute-start.4 = (bf16[512,1280]{1,0:T(8,128)(2,1)S(1)}, bf16[512,1280]{1,0:T(8,128)(2,1)S(1)}, u32[]{:S(2)}, u32[]{:S(2)}) collective-permute-start(bf16[512,1280]{1,0:T(8,128)(2,1)S(1)} %get-tuple-element.78), channel_id=1, source_target_pairs={{1,2},{2,1},{5,6},{6,5},{9,10},{10,9},{13,14},{14,13},{17,18},{18,... | collective-permute-start | bytes 3932168 | tf_op jit(solution)/shard_map/ppermute | solution.py:368
  598.0 10.2 copy-start.16
  598.0 10.2 copy-start.18
  606.3 18.8 %collective-permute-start.8 = (bf16[512,1280]{1,0:T(8,128)(2,1)S(1)}, bf16[512,1280]{1,0:T(8,128)(2,1)S(1)}, u32[]{:S(2)}, u32[]{:S(2)}) collective-permute-start(bf16[512,1280]{1,0:T(8,128)(2,1)S(1)} %slice.241), channel_id=1, source_target_pairs={{0,2},{1,3},{2,0},{3,1},{4,6},{5,7},{6,4},{7,5},{8,10},{9,11},{10,... | collective-permute-start | bytes 3932168 | tf_op jit(solution)/shard_map/ppermute | solution.py:362
  619.7 5.4 copy-start.23
  619.7 5.4 copy-start.25
  627.7 475.2 %collective-permute-start.9 = (bf16[512,1280]{1,0:T(8,128)(2,1)S(1)}, bf16[512,1280]{1,0:T(8,128)(2,1)S(1)}, u32[]{:S(2)}, u32[]{:S(2)}) collective-permute-start(bf16[512,1280]{1,0:T(8,128)(2,1)S(1)} %fusion.20), channel_id=1, source_target_pairs={{1,2},{2,1},{5,6},{6,5},{9,10},{10,9},{13,14},{14,13},{17,18},{18,... | collective-permute-start | bytes 3932168 | tf_op jit(solution)/shard_map/ppermute | solution.py:368
  1067.4 7.2 copy-start.10
  (19 other events, 62.3 us)

commit v3 on v2

--- a/solution.py
+++ b/solution.py
@@ -421,47 +421,86 @@
     return pl.ds(pl.multiple_of(start, 16), size)
 
 
-def lanes_at(start, size):
+def cols(start, size):
     return pl.ds(pl.multiple_of(start, 128), size)
 
 
-def gather_kernel(
+def attend_pair(qkv, mixed, total_ref, pair, base):
+    f32, bf16 = jnp.float32, jnp.bfloat16
+    rows = qkv.shape[0]
+    lane = lax.broadcasted_iota(jnp.int32, (1, 128), 1)
+    here = pair * 128
+    keys = qkv[:, cols(EDGE + here, 128)]
+    values_t = qkv[:, cols(2 * EDGE + here, 128)].T
+    for block in range(rows // Q_BLOCK):
+        part = pl.ds(block * Q_BLOCK, Q_BLOCK)
+        queries = qkv[part, cols(here, 128)] * jnp.asarray(0.125, bf16)
+        outs = []
+        for head in range(2):
+            own = (lane // HDIM) == head
+            scores = lax.dot_general(
+                keys,
+                jnp.where(own, queries, jnp.zeros_like(queries)),
+                (((1,), (1,)), ((), ())),
+                preferred_element_type=f32,
+            )
+            largest = jnp.max(scores, axis=0, keepdims=True)
+            weights = jnp.exp(scores - largest)
+            total = jnp.sum(weights, axis=0, keepdims=True)
+            out = jnp.dot(
+                values_t[head * HDIM : (head + 1) * HDIM, :],
+                weights.astype(bf16),
+                preferred_element_type=f32,
+            )
+            outs.append(out / total)
+            total_ref[2 * pair + head, :, part] = largest + jnp.log(total)
+        mixed[part, cols(base + here, 128)] = jnp.concatenate(outs, axis=0).T.astype(bf16)
+
+
+def forward_kernel(
     tokens, out_grad, cell_weight, vectors, wq, wk, wv, wo, wup, wdown,
-    own, own_grad, own_weight, all_vectors, qkv_w, out_w, up_w, down_w,
-    send_sems, recv_sems, local_sems, side_send, side_recv, side_local,
+    own_out, grad_out, weight_out, vectors_out, qkv_w_out, out_w_out, up_w_out, down_w_out,
+    normed_one_out, qkv_out, mixed_out, total_out, middle_out, normed_two_out, hidden_out, slope_out, ffn_out,
+    tok, grad, scale, vec, qkv_w, out_w, up_w, down_w,
+    normed_one, qkv, mixed, totals, middle, normed_two, hidden, slope, ffn,
+    send_sems, recv_sems, local_sems, side_send, side_recv, side_local, out_sems,
 ):
+    f32, bf16 = jnp.float32, jnp.bfloat16
     at = Spot()
     x, core = at.x, at.core
+    rows = tok.shape[0]
+    width = tok.shape[1]
     at.meet(("x", "core", "diagonal", "y", "low", "high"))
-    side = [(tokens, own), (cell_weight, own_weight), (out_grad, own_grad)]
+
+    side = [(tokens, tok), (cell_weight, scale), (out_grad, grad)]
     diagonal = [at.send("diagonal", s, t, side_send.at[i], side_recv.at[i]) for i, (s, t) in enumerate(side)]
     straight = [pltpu.make_async_copy(s, t, side_local.at[i]) for i, (s, t) in enumerate(side)]
 
-    def swap_start(i):
+    def swap(i, remote, local):
         @pl.when(x != core)
         def _():
-            diagonal[i].start()
+            remote(diagonal[i])
 
         @pl.when(x == core)
         def _():
-            straight[i].start()
-
-    swap_start(0)
-    swap_start(1)
-    vector_copy = at.send("x", vectors, all_vectors.at[x], side_send.at[3], side_recv.at[3])
-    vector_copy.start()
-    vector_local = pltpu.make_async_copy(vectors, all_vectors.at[x], side_local.at[3])
-    vector_local.start()
+            local(straight[i])
+
+    def swap_start(i):
+        swap(i, lambda c: c.start(), lambda c: c.start())
+
+    def swap_wait(i):
+        swap(i, lambda c: c.wait(), lambda c: c.wait())
 
     chunks = []
     for i, ref in enumerate((wq, wk, wv)):
-        chunks.append((ref.at[:, lanes_at(core * EDGE, EDGE)], qkv_w, EDGE, 0, i * EDGE))
+        chunks.append((ref.at[:, cols(core * EDGE, EDGE)], qkv_w, EDGE, 0, i * EDGE))
     for i in range(4):
         start = (i // 2) * 4 * EDGE + core * 2 * EDGE + (i % 2) * EDGE
-        chunks.append((wup.at[:, lanes_at(start, EDGE)], up_w, EDGE, 0, i * EDGE))
+        chunks.append((wup.at[:, cols(start, EDGE)], up_w, EDGE, 0, i * EDGE))
     for i in range(4):
         source = wdown.at[rows_at(core * 2 * EDGE + (i // 2) * EDGE, EDGE), pl.ds((i % 2) * EDGE, EDGE)]
         chunks.append((source, down_w, 2 * EDGE, (i // 2) * EDGE, (i % 2) * EDGE))
+    count = len(chunks)
     eighth = EDGE // 8
     place = at.y * 4 + at.low * 2 + at.high
 
@@ -469,18 +508,17 @@
         _, ref, stride, row, column = chunks[k]
         return ref.at[rows_at(half * stride + row + start * eighth, size * eighth), pl.ds(column, EDGE)]
 
-    stages = {}
+    ops = {}
     for k, chunk in enumerate(chunks):
-        stages["x", k] = at.send(
+        ops["x", k] = at.send(
             "x", chunk[0].at[rows_at(place * eighth, eighth)], region(k, x, place, 1), send_sems.at[0, k], recv_sems.at[0, k]
         )
         for s, (name, start, size) in enumerate(
             (("high", place, 1), ("low", at.y * 4 + at.low * 2, 2), ("y", at.y * 4, 4))
         ):
             part = region(k, 1 - x, start, size)
-            stages[name, k] = at.send(name, part, part, send_sems.at[s + 1, k], recv_sems.at[s + 1, k])
-        stages["local", k] = pltpu.make_async_copy(chunk[0], region(k, x, 0, 8), local_sems.at[k])
-
+            ops[name, k] = at.send(name, part, part, send_sems.at[s + 1, k], recv_sems.at[s + 1, k])
+        ops["local", k] = pltpu.make_async_copy(chunk[0], region(k, x, 0, 8), local_sems.at[k])
     half = EDGE // 2
     out_x = at.send(
         "x", wo.at[rows_at(core * half, half)], out_w.at[rows_at(x * EDGE + core * half, half)], side_send.at[4], side_recv.at[4]
@@ -488,79 +526,233 @@
     part = out_w.at[rows_at((1 - x) * EDGE + core * half, half)]
     out_core = at.send("core", part, part, side_send.at[5], side_recv.at[5])
     out_local = pltpu.make_async_copy(wo, out_w.at[rows_at(x * EDGE, EDGE)], side_local.at[4])
-
-    count = len(chunks)
-    for k in range(3):
-        stages["x", k].start()
-    out_x.start()
-    for k in range(3, count):
-        stages["x", k].start()
-    swap_start(2)
-    for k in range(count):
-        stages["local", k].start()
-    out_local.start()
-    for tick in range(count + 3):
-        for before, name, after in ((0, "x", "high"), (1, "high", "low"), (2, "low", "y"), (3, "y", None)):
-            k = tick - before
+    vec_x = at.send("x", vectors, vec.at[x], side_send.at[3], side_recv.at[3])
+    vec_local = pltpu.make_async_copy(vectors, vec.at[x], side_local.at[3])
+    top, bottom = pl.ds(0, rows), pl.ds(rows, rows)
+
+    def core_copy(i, source, target):
+        return at.send("core", source, target, side_send.at[i], side_recv.at[i])
+
+    normed_one_core = core_copy(6, normed_one.at[top], normed_one.at[bottom])
+    heads = cols(core * EDGE, EDGE)
+    mixed_core = [
+        core_copy(7, mixed.at[top, heads], mixed.at[bottom, heads]),
+        core_copy(8, mixed.at[bottom, heads], mixed.at[top, heads]),
+    ]
+    normed_two_core = core_copy(9, normed_two.at[top], normed_two.at[bottom])
+    ffn_core = core_copy(10, ffn.at[top], ffn.at[bottom])
+
+    outs = []
+    early = []
+
+    def put(source, target):
+        copy = pltpu.make_async_copy(source, target, out_sems.at[len(outs)])
+        copy.start()
+        outs.append(copy)
+        return copy
+
+    issue = {
+        0: [ops["x", 3], ops["x", 4]],
+        1: [ops["x", 5], ops["x", 6]],
+        2: [out_x, out_local, ops["local", 3], ops["local", 4], ops["local", 5], ops["local", 6]],
+        3: [ops["x", 7], ops["x", 8]],
+        4: [ops["x", 9], ops["x", 10], ops["local", 7], ops["local", 8], ops["local", 9], ops["local", 10]],
+    }
+
+    def tick(t):
+        for op in issue.get(t, ()):
+            op.start()
+        if t == 5:
+            swap_start(2)
+        for before, name, after in ((3, "y", None), (2, "low", "y"), (1, "high", "low"), (0, "x", "high")):
+            k = t - before
             if 0 <= k < count:
-                stages[name, k].wait_recv()
+                ops[name, k].wait_recv()
                 if after:
-                    stages[after, k].start()
-        if tick == 3:
+                    ops[after, k].start()
+        if t == 6:
             out_x.wait_recv()
             out_core.start()
+
+    for k in range(3):
+        ops["x", k].start()
+    vec_x.start()
+    swap_start(0)
+    swap_start(1)
+    vec_local.start()
+    for k in range(3):
+        ops["local", k].start()
+    tick(0)
+    tick(1)
+    vec_x.wait_recv()
+    vec_local.wait()
+
+    def vector(i):
+        return jnp.concatenate([vec[0, i : i + 1, :], vec[1, i : i + 1, :]], axis=1)
+
+    def norm(values, gain, bias):
+        average = jnp.mean(values, axis=-1, keepdims=True)
+        centred = values - average
+        inverse = lax.rsqrt(jnp.mean(centred * centred, axis=-1, keepdims=True) + 1e-05)
+        return (centred * inverse * gain + bias).astype(bf16)
+
+    swap_wait(0)
+    gain_one, bias_one = vector(0), vector(1)
+
+    @pl.loop(0, rows // 64)
+    def _(i):
+        here = rows_at(i * 64, 64)
+        normed_one[here, :] = norm(tok[here, :].astype(f32), gain_one, bias_one)
+
+    normed_one_core.start()
+    tick(2)
+    put(tok, own_out)
+    normed_one_core.wait_recv()
+    put(normed_one, normed_one_out)
+
+    for i in range(3):
+        tick(3 + i)
+        ops["local", i].wait()
+        lanes = pl.ds(i * EDGE, EDGE)
+        bias = 0.0 if i == 1 else vec[core, 2 + i // 2 : 3 + i // 2, :]
+
+        @pl.loop(0, 2 * rows // 256)
+        def _(r):
+            here = rows_at(r * 256, 256)
+            value = jnp.dot(normed_one[here, :], qkv_w[:, lanes], preferred_element_type=f32)
+            qkv[here, lanes] = (value + bias).astype(bf16)
+
+    put(qkv, qkv_out)
+    put(qkv_w, qkv_w_out)
+
+    @pl.loop(0, EDGE // 128)
+    def _(pair):
+        attend_pair(qkv, mixed, totals, pair, core * EDGE)
+
+        @pl.when(pair == 1)
+        def _():
+            tick(6)
+
+        @pl.when(pair == 3)
+        def _():
+            tick(7)
+
+    mixed_core[0].start()
+    mixed_core[1].start()
+    put(totals, total_out)
+    tick(8)
+    out_local.wait()
     out_core.wait_recv()
-    vector_copy.wait()
-    vector_local.wait()
-    for i in range(3):
-
-        @pl.when(x != core)
-        def _():
-            diagonal[i].wait()
-
-        @pl.when(x == core)
-        def _():
-            straight[i].wait()
-
+    mixed_core[1].wait_recv()
+    gain_two, bias_two, out_bias = vector(5), vector(6), vector(4)
+
+    @pl.loop(0, rows // 128)
+    def _(r):
+        here = rows_at(r * 128, 128)
+        value = jnp.dot(mixed[here, :], out_w[...], preferred_element_type=f32)
+        value = tok[here, :].astype(f32) + value + out_bias
+        middle[here, :] = value
+        normed_two[here, :] = norm(value, gain_two, bias_two)
+
+    normed_two_core.start()
+    mixed_core[0].wait_recv()
+    put(out_w, out_w_out)
+    put(mixed, mixed_out)
+    put(middle, middle_out)
+    tick(9)
+    normed_two_core.wait_recv()
+    put(normed_two, normed_two_out)
+    waits = {}
+    for i in range(4):
+        ops["local", 3 + i].wait()
+        slot = i % 2
+        if i >= 2:
+            for copy in waits[slot]:
+                copy.wait()
+                early.append(copy)
+        lanes = pl.ds(i * EDGE, EDGE)
+        bias = vec[i // 2, pl.ds(8 + core * 2 + i % 2, 1), :]
+
+        @pl.loop(0, 2 * rows // 128)
+        def _(r):
+            here = rows_at(r * 128, 128)
+            up = jnp.dot(normed_two[here, :], up_w[:, lanes], preferred_element_type=f32) + bias
+            cdf = 0.5 * (1.0 + lax.erf(up * 0.7071067811865476))
+            hidden[slot, here, :] = (up * cdf).astype(bf16)
+            slope[slot, here, :] = (cdf + up * jnp.exp(-0.5 * up * up) * 0.3989422804014327).astype(bf16)
+
+        waits[slot] = (
+            put(hidden.at[slot], hidden_out.at[:, lanes]),
+            put(slope.at[slot], slope_out.at[:, lanes]),
+        )
+        if i == 1:
+            swap_wait(1)
+            swap_wait(2)
+            weight = scale[0:1, 0:1]
+
+            @pl.loop(0, rows // 64)
+            def _(r):
+                here = rows_at(r * 64, 64)
+                ffn[here, :] = (grad[here, :].astype(f32) * weight).astype(bf16)
+
+            ffn_core.start()
+            put(grad, grad_out)
+            put(scale, weight_out)
+            put(vec, vectors_out)
+        tick(10 + i)
+    put(up_w, up_w_out)
+    ffn_core.wait_recv()
+    put(ffn, ffn_out)
+    for k in range(7, count):
+        ops["local", k].wait()
+    put(down_w, down_w_out)
     for k in range(count):
-        stages["local", k].wait()
         for name in ("x", "high", "low", "y"):
-            stages[name, k].wait_send()
-    out_local.wait()
-    out_x.wait_send()
-    out_core.wait_send()
-
-
-def gather(*args):
-    tokens = args[0]
-    bf16 = jnp.bfloat16
+            ops[name, k].wait_send()
+    for op in (out_x, out_core, vec_x, normed_one_core, *mixed_core, normed_two_core, ffn_core):
+        op.wait_send()
+    for copy in outs:
+        if not any(copy is other for other in early):
+            copy.wait()
+
+
+def forward(*args):
+    bf16, f32 = jnp.bfloat16, jnp.float32
     shape = jax.ShapeDtypeStruct
-    width = tokens.shape[1]
-    vectors = args[3]
+    rows, width = args[0].shape
+    both = 2 * rows
+    arrays = [
+        ((rows, width), bf16),
+        ((rows, width), bf16),
+        (args[2].shape, f32),
+        ((2,) + args[3].shape, f32),
+        ((width, 3 * EDGE), bf16),
+        ((width, width), bf16),
+        ((width, 4 * EDGE), bf16),
+        ((4 * EDGE, width), bf16),
+        ((both, width), bf16),
+        ((both, 3 * EDGE), bf16),
+        ((both, width), bf16),
+        ((EDGE // HDIM, 1, both), f32),
+        ((rows, width), f32),
+        ((both, width), bf16),
+        ((both, 4 * EDGE), bf16),
+        ((both, 4 * EDGE), bf16),
+        ((both, width), bf16),
+    ]
+    scratch = [pltpu.VMEM(*array) for array in arrays]
+    scratch[14] = scratch[15] = pltpu.VMEM((2, both, EDGE), bf16)
+    dma = pltpu.SemaphoreType.DMA
     return pl.pallas_call(
-        gather_kernel,
+        forward_kernel,
         in_specs=[ANY] * len(args),
-        out_specs=[ANY] * 8,
-        out_shape=[
-            shape(tokens.shape, bf16),
-            shape(tokens.shape, bf16),
-            shape(args[2].shape, jnp.float32),
-            shape((2,) + vectors.shape, bf16),
-            shape((width, 3 * EDGE), bf16),
-            shape((width, width), bf16),
-            shape((width, 4 * EDGE), bf16),
-            shape((4 * EDGE, width), bf16),
-        ],
-        scratch_shapes=[
-            pltpu.SemaphoreType.DMA((4, 11)),
-            pltpu.SemaphoreType.DMA((4, 11)),
-            pltpu.SemaphoreType.DMA((11,)),
-            pltpu.SemaphoreType.DMA((6,)),
-            pltpu.SemaphoreType.DMA((6,)),
-            pltpu.SemaphoreType.DMA((5,)),
-        ],
-        compiler_params=pltpu.CompilerParams(collective_id=0, has_side_effects=True),
-        name="gather",
+        out_specs=[ANY] * len(arrays),
+        out_shape=[shape(*array) for array in arrays],
+        scratch_shapes=scratch + [dma((4, 11)), dma((4, 11)), dma((11,)), dma((11,)), dma((11,)), dma((5,)), dma((24,))],
+        compiler_params=pltpu.CompilerParams(
+            collective_id=0, has_side_effects=True, vmem_limit_bytes=60 * 1024 * 1024
+        ),
+        name="forward",
     )(*args)
 
 
@@ -581,9 +773,9 @@
         chunks.append((give_down.at[part], keep_down.at[part], target))
     for i in range(4):
         part = (slice(None), pl.ds(i * EDGE, EDGE))
-        target = up_ref.at[:, lanes_at((i // 2) * 4 * EDGE + core * 2 * EDGE + (i % 2) * EDGE, EDGE)]
+        target = up_ref.at[:, cols((i // 2) * 4 * EDGE + core * 2 * EDGE + (i % 2) * EDGE, EDGE)]
         chunks.append((give_up.at[part], keep_up.at[part], target))
-    mine = lanes_at(core * EDGE, EDGE)
+    mine = cols(core * EDGE, EDGE)
     chunks.append((give_out, keep_out, out_ref.at[:, mine]))
     for i, ref in enumerate((q_ref, k_ref, v_ref)):
         part = (slice(None), pl.ds(i * EDGE, EDGE))
@@ -618,7 +810,7 @@
             there = rows_at(i * 80, 80)
             goal[k, here, :] = (acc[k, here, :].astype(f32) + other[k, there, :].astype(f32)).astype(bf16)
 
-    for k in range(count):
+    for k in range(2):
         ops["x", k].start()
         ops["load", k].start()
     vec_load = pltpu.make_async_copy(vec, vec_acc.at[0], vec_local.at[0])
@@ -632,12 +824,15 @@
     after = ("y", "low", "high", "all_high", "all_low", "all_y", "core", None)
     stages = ("x",) + after[:-1]
     for tick in range(count + 7):
-        for before, (stage, following) in enumerate(zip(stages, after)):
+        for before, (stage, following) in reversed(list(enumerate(zip(stages, after)))):
             k = tick - before
             if not 0 <= k < count:
                 continue
             ops[stage, k].wait_recv()
             if stage == "x":
+                if k + 2 < count:
+                    ops["x", k + 2].start()
+                    ops["load", k + 2].start()
                 ops["load", k].wait()
                 add(k, 0, EDGE, from_x, acc)
             elif stage == "y":
@@ -707,37 +902,6 @@
         ),
         name="reduce",
     )(*args)
-
-
-def attend_kernel(q_ref, k_ref, v_ref, mixed_ref, total_ref):
-    f32, bf16 = jnp.float32, jnp.bfloat16
-    rows, lanes = q_ref.shape
-    lane = lax.broadcasted_iota(jnp.int32, (1, lanes), 1)
-    keys = k_ref[...]
-    values_t = v_ref[...].T
-    for block in range(rows // Q_BLOCK):
-        part = pl.ds(block * Q_BLOCK, Q_BLOCK)
-        queries = q_ref[part, :] * jnp.asarray(0.125, bf16)
-        outs = []
-        for head in range(2):
-            own = (lane // HDIM) == head
-            scores = lax.dot_general(
-                keys,
-                jnp.where(own, queries, jnp.zeros_like(queries)),
-                (((1,), (1,)), ((), ())),
-                preferred_element_type=f32,
-            )
-            largest = jnp.max(scores, axis=0, keepdims=True)
-            weights = jnp.exp(scores - largest)
-            total = jnp.sum(weights, axis=0, keepdims=True)
-            mixed = jnp.dot(
-                values_t[head * HDIM : (head + 1) * HDIM, :],
-                weights.astype(bf16),
-                preferred_element_type=f32,
-            )
-            outs.append(mixed / total)
-            total_ref[head, :, part] = largest + jnp.log(total)
-        mixed_ref[part, :] = jnp.concatenate(outs, axis=0).T.astype(bf16)
 
 
 def attend_back_kernel(q_ref, k_ref, v_ref, total_ref, grad_ref, dq_ref, dk_ref, dv_ref, dk_acc, dv_acc):
@@ -786,34 +950,6 @@
     dv_ref[...] = dv_acc[...].astype(bf16)
 
 
-def attend(qkv):
-    rows, width = qkv.shape[0], qkv.shape[1] // 3
-    pairs = width // 128
-    macs = 2 * rows * rows * width
-    return pl.pallas_call(
-        attend_kernel,
-        grid=(pairs,),
-        in_specs=[
-            pl.BlockSpec((rows, 128), lambda p: (0, p)),
-            pl.BlockSpec((rows, 128), lambda p: (0, pairs + p)),
-            pl.BlockSpec((rows, 128), lambda p: (0, 2 * pairs + p)),
-        ],
-        out_specs=[
-            pl.BlockSpec((rows, 128), lambda p: (0, p)),
-            pl.BlockSpec((2, 1, rows), lambda p: (p, 0, 0)),
-        ],
-        out_shape=[
-            jax.ShapeDtypeStruct((rows, width), jnp.bfloat16),
-            jax.ShapeDtypeStruct((2 * pairs, 1, rows), jnp.float32),
-        ],
-        compiler_params=pltpu.CompilerParams(vmem_limit_bytes=VMEM),
-        cost_estimate=pl.CostEstimate(
-            flops=8 * macs, bytes_accessed=8 * rows * width, transcendentals=macs // 128
-        ),
-        name="attend",
-    )(qkv, qkv, qkv)
-
-
 def attend_back(qkv, total, grad_mixed):
     rows, width = grad_mixed.shape
     pairs = width // 128
@@ -869,15 +1005,31 @@
     head_width = width // 2
 
     vectors = (first_gain, first_bias, query_bias, value_bias, output_bias, second_gain, second_bias, down_bias)
-    vectors = jnp.stack(vectors)
-    vectors = jnp.pad(vectors, ((0, 15 - vectors.shape[0]), (0, hidden_width - vectors.shape[1])))
-    vectors = jnp.concatenate([vectors, up_bias[None]])
+    vectors = jnp.concatenate([jnp.stack(vectors), up_bias.reshape(4, -1), jnp.zeros((4, head_width), bf16)])
     cell_weight = jnp.broadcast_to(jnp.sqrt(query_counts.astype(f32) / 1000.0), (8, 128))
-    own, own_grad, cell_weight, vectors, qkv_weight, out_weight, up_all, down_all = gather(
+    (
+        own,
+        own_grad,
+        cell_weight,
+        vectors,
+        qkv_weight,
+        out_weight,
+        up_all,
+        down_all,
+        normed_one,
+        qkv,
+        mixed,
+        log_total,
+        middle,
+        normed_two,
+        hidden,
+        slope,
+        grad_ffn,
+    ) = forward(
         tokens[0],
         out_grad[0],
         cell_weight,
-        vectors,
+        vectors.astype(f32),
         query_weight,
         key_weight,
         value_weight,
@@ -885,35 +1037,11 @@
         up_weight,
         down_weight,
     )
-    weight_cell = cell_weight[:1, :1]
-    vectors = vectors.astype(f32)
-    short = [vectors[:, i, :head_width].reshape(-1) for i in range(8)]
-    gain_one, bias_one, q_bias, v_bias, o_bias, gain_two, bias_two, d_bias = short
-    u_bias = vectors[:, 15].reshape(-1)
-
-    own = own.astype(f32)
-    standard_one, inverse_one = standardize(own)
-    normed_own = (standard_one * gain_one + bias_one).astype(bf16)
-    normed_one = jnp.concatenate([normed_own, across(normed_own, CORE_BIT)])
-    qkv_bias = jnp.concatenate(
-        [half_of(q_bias, core), jnp.zeros((head_width,), f32), half_of(v_bias, core)]
-    )
-    qkv = (matmul(normed_one, qkv_weight) + qkv_bias).astype(bf16)
-    mixed_heads, log_total = attend(qkv)
-    other_heads = across(mixed_heads, CORE_BIT)
-    other_heads = jnp.concatenate([other_heads[rows:], other_heads[:rows]])
-    mixed = in_order(core == 0, mixed_heads, other_heads, axis=1)
-    middle = own + matmul(mixed[:rows], out_weight) + o_bias
+    gain_one, gain_two, d_bias = (vectors[:, i].reshape(-1) for i in (0, 5, 7))
+    standard_one, inverse_one = standardize(own.astype(f32))
     standard_two, inverse_two = standardize(middle)
-    normed_own = (standard_two * gain_two + bias_two).astype(bf16)
-    normed_two = jnp.concatenate([normed_own, across(normed_own, CORE_BIT)])
-    up_bias_own = lax.dynamic_index_in_dim(u_bias.reshape(2, 2, -1), core, 1, keepdims=False).reshape(-1)
-    up_proj = matmul(normed_two, up_all) + up_bias_own
-    hidden = gelu_value(up_proj).astype(bf16)
-
-    grad_result = own_grad.astype(f32) * weight_cell
-    grad_own = grad_result.astype(bf16)
-    grad_ffn = jnp.concatenate([grad_own, across(grad_own, CORE_BIT)])
+
+    grad_result = own_grad.astype(f32) * cell_weight[:1, :1]
 
     def weight_sum(left, right):
         give = weight_grad(half_of(left, 1 - x, 1), right).astype(bf16)
@@ -921,7 +1049,7 @@
         return give, keep
 
     sum_down = weight_sum(hidden, grad_ffn)
-    grad_up = (matmul_right_t(grad_ffn, down_all) * gelu_slope(up_proj)).astype(bf16)
+    grad_up = (matmul_right_t(grad_ffn, down_all) * slope.astype(f32)).astype(bf16)
     sum_up = weight_sum(normed_two, grad_up)
     partial = matmul_right_t(grad_up, up_all)
     grad_normed_two = partial[:rows] + across(partial[rows:].astype(bf16), CORE_BIT).astype(f32)
@@ -958,7 +1086,7 @@
         column_sum(grad_attn_own),
         jnp.sum(grad_normed_two * standard_two, axis=0),
         jnp.sum(grad_normed_two, axis=0),
-        column_sum(grad_own),
+        column_sum(grad_ffn[:rows]),
         up_sum,
     ]
     sizes = [value.shape[0] for value in sums]

time: 1110 us -> 664 us (0.60)
  Pallas kernels: 903 us -> 484 us
  matrix products: 114 us -> 91.5 us
    pallas_call x2 -> x1, Pallas kernels: 432 us -> 153 us  [forward(): pl.pallas_call(forward_kernel, in_specs=[ANY] * len(args), out_specs=[ANY...]
    pallas_call x1, Pallas kernels: 437 us -> 297 us  [reduce(): pl.pallas_call(reduce_kernel, in_specs=[ANY] * len(args), out_specs=[ANY]...]
    dot_general x4 -> x1, matrix products: 34.2 us -> 6.91 us  [matmul(): return jnp.dot(left, right, preferred_element_type=jnp.float32)]
  transfers between devices with their start and end apart: 10 -> 6, of which waited for: 2 -> 0; matrix products, arithmetic and copies ran while one was open for 11% -> 18% of each run, Pallas kernels for 43% -> 51%
where the time goes in v3:
time: 664 us; the launch traced here: 654 us
  Pallas kernels  484 us (73%)
  matrix products  91.5 us (14%)
  other arithmetic  43.3 us (7%)
  local copies, waits for them, and re-layouts  23.2 us (3%)
  starting transfers between devices  9.18 us (1%)
    pallas_call x1, Pallas kernels, reduce(): pl.pallas_call(reduce_kernel, in_specs=[ANY] * len(args), out_specs=[ANY]...  297 us
    pallas_call x1, Pallas kernels, forward(): pl.pallas_call(forward_kernel, in_specs=[ANY] * len(args), out_specs=[ANY...  153 us
    dot_general x8, matrix products, weight_grad(): jnp.einsum('ti,to->io', left, right, preferred_element_type=jnp.float32)  52 us
    pallas_call x1, Pallas kernels, attend_back(): pl.pallas_call(attend_back_kernel, grid=(pairs,), in_specs=[block, pl.Blo...  34.4 us
    dot_general x4, matrix products, matmul_right_t(): jnp.einsum('to,io->ti', left, right, preferred_element_type=jnp.float32)  32.6 us
  transfers between devices with their start and end apart: 6, of which 0 were waited for; matrix products, arithmetic and copies ran while one was open for 18% of the time, Pallas kernels for 51%

profile of v3, /device:TPU:0, one launch (start us, length us, event | category | flops | bytes accessed | tf_op | source)
XLA Modules:
  0.0 654.1 jit_solution(1413839811175765005)
XLA Ops:
  8.8 153.5 %forward.1 = (bf16[512,1280]{1,0:T(8,128)(2,1)}, bf16[512,1280]{1,0:T(8,128)(2,1)}, f32[8,128]{1,0:T(8,128)}, f32[2,16,640]{2,1,0:T(8,128)}, bf16[1280,1920]{1,0...) custom-call(bf16[512,1280]{1,0:T(8,128)(2,1)} %bitcast.31, ...), custom_call_target="tpu_custom_call" | custom-call | tf_op jit(solution)/shard_map/forward/pallas_call | solution.py:746
  162.4 12.9 %convert_reduce_fusion = (f32[2560]{0:T(1024)S(1)}, bf16[1024,2560]{1,0:T(8,128)(2,1)}) fusion(bf16[1024,2560]{1,0:T(8,128)(2,1)} %get-tuple-element.51, bf16[1024,1280]{1,0:T(8,128)(2,1)} %get-tuple-element.50, bf16[2560,1280]{1,0:T(8,128)(2,1)} %get-tuple-element.46), kind=kOutput, calls=%fused_computation | convolution fusion | flops 6723991040 | bytes 19671040 | tf_op jit(solution)/shard_map/to,io->ti/dot_general | solution.py:27
  175.3 9.3 %fusion.46 = f32[1024,1280]{1,0:T(8,128)S(1)} fusion(bf16[1024,2560]{1,0:T(8,128)(2,1)} %get-tuple-element.97, bf16[1280,2560]{1,0:T(8,128)(2,1)S(1)} %copy-done.15), kind=kOutput, calls=%fused_computation.103 | convolution fusion | flops 6710886400 | bytes 17039360 | tf_op jit(solution)/shard_map/to,io->ti/dot_general | solution.py:27
  184.6 1.3 slice.184
  185.9 6.9 %fusion.45 = f32[1024,1280]{1,0:T(8,128)S(1)} fusion(bf16[1024,2560]{1,0:T(8,128)(2,1)S(1)} %copy-done.16, bf16[2560,1280]{1,0:T(8,128)(2,1)S(1)} %copy-done.14), kind=kOutput, calls=%fused_computation.102 | convolution fusion | flops 6710886400 | bytes 17039360 | tf_op jit(solution)/shard_map/dot_general | solution.py:23
  194.1 1.9 copy-done.4
  199.3 1.6 convert_reduce_fusion.2
  200.9 1.8 fusion.12
  202.8 8.2 %convolution_convert_fusion.2.keep_up = bf16[640,2560]{1,0:T(8,128)(2,1)} fusion(bf16[1024,2560]{1,0:T(8,128)(2,1)} %get-tuple-element.97, bf16[1024,1280]{1,0:T(8,128)(2,1)} %get-tuple-element.61, s32[]{:T(128)S(6)} %select_n.112), kind=kOutput, calls=%fused_computation.5 | convolution fusion | flops 3357081600 | bytes 9830404 | tf_op jit(solution)/shard_map/ti,to->io/dot_general | solution.py:31
  211.0 18.5 %convolution_convert_fusion.1.give_down = bf16[1280,1280]{1,0:T(8,128)(2,1)} fusion(bf16[1024,1280]{1,0:T(8,128)(2,1)} %get-tuple-element.50, bf16[1024,2560]{1,0:T(8,128)(2,1)} %get-tuple-element.45, s32[]{:T(128)S(6)} %select_n.109), kind=kOutput, calls=%fused_computation.4 | convolution fusion | flops 3357081600 | bytes 8519684 | tf_op jit(solution)/shard_map/ti,to->io/dot_general | solution.py:31
  229.5 7.6 %convolution_convert_fusion.keep_down = bf16[1280,1280]{1,0:T(8,128)(2,1)} fusion(bf16[1024,1280]{1,0:T(8,128)(2,1)S(1)} %copy-done.12, bf16[1024,2560]{1,0:T(8,128)(2,1)} %get-tuple-element.45, s32[]{:T(128)S(6)} %select_n.110), kind=kOutput, calls=%fused_computation.3 | convolution fusion | flops 3357081600 | bytes 8519684 | tf_op jit(solution)/shard_map/ti,to->io/dot_general | solution.py:31
  237.1 2.7 multiply_reduce_fusion
  240.0 5.1 convert_reduce_fusion.4
  245.8 5.1 convolution_convert_fusion.3.give_up
  251.7 2.2 fusion.19.grad_ref
  253.9 34.4 %attend_back.1 = (bf16[1024,640]{1,0:T(8,128)(2,1)S(1)}, bf16[1024,640]{1,0:T(8,128)(2,1)S(1)}, bf16[1024,640]{1,0:T(8,128)(2,1)S(1)}) custom-call(bf16[1024,1920]{1,0:T(8,128)(2,1)} %get-tuple-element.54.q_ref.k_ref.v_ref, bf16[1024,1920]{1,0:T(8,128)(2,1)} %get-tuple-element.54.q_ref.k_ref.v_ref, bf16[1024,1920]{1,0:T(8,128)(2,1)} %get-tuple-element.54.q_ref.k_ref.v_ref, ...), custom_call_target="tpu_custom_call" | custom-call | flops 26843545600 | bytes 9175040 | tf_op jit(solution)/shard_map/attend_back/pallas_call | solution.py:958
  288.9 8.2 %fusion.47 = f32[1024,1280]{1,0:T(8,128)S(1)} fusion(bf16[1024,1920]{1,0:T(8,128)(2,1)S(1)} %constant_dynamic-update-slice_fusion, bf16[1280,1920]{1,0:T(8,128)(2,1)} %get-tuple-element.60), kind=kOutput, calls=%fused_computation.104 | convolution fusion | flops 5033164800 | bytes 14090240 | tf_op jit(solution)/shard_map/to,io->ti/dot_general | solution.py:27
  297.3 6.7 %collective-permute-start.4 = (bf16[512,1280]{1,0:T(8,128)(2,1)S(1)}, bf16[512,1280]{1,0:T(8,128)(2,1)S(1)}, u32[]{:S(2)}, u32[]{:S(2)}) collective-permute-start(bf16[512,1280]{1,0:T(8,128)(2,1)S(1)} %slice.183), channel_id=1, source_target_pairs={{0,2},{1,3},{2,0},{3,1},{4,6},{5,7},{6,4},{7,5},{8,10},{9,11},{10,... | collective-permute-start | bytes 3932168 | tf_op jit(solution)/shard_map/ppermute | solution.py:362
  304.0 2.2 convolution_convert_fusion.6.keep_out
  306.7 2.6 select_bitcast_fusion.1
  309.4 2.1 convolution_convert_fusion.7.give_out
  311.5 4.1 convolution_convert_fusion.4.keep_qkv
  315.7 4.1 convolution_convert_fusion.5.give_qkv
  319.8 1.4 fusion.11
  321.2 1.3 fusion.10
  324.1 296.6 %reduce.7 = (bf16[2560,1280]{1,0:T(8,128)(2,1)}, bf16[640,5120]{1,0:T(8,128)(2,1)}, bf16[640,1280]{1,0:T(8,128)(2,1)}, bf16[640,1280]{1,0:T(8,128)(2,1)}, bf16[6...) custom-call(bf16[1280,1280]{1,0:T(8,128)(2,1)} %convolution_convert_fusion.1.give_down, ...), custom_call_target="tpu_custom_call" | custom-call | tf_op jit(solution)/shard_map/reduce/pallas_call | solution.py:870
  622.7 9.7 %convert_element_type.127 = f32[640,5120]{1,0:T(8,128)} convert(bf16[640,5120]{1,0:T(8,128)(2,1)} %get-tuple-element.69) | non-fusion elementwise | flops 3276800 | bytes 19660800 | tf_op jit(solution)/shard_map/convert_element_type | solution.py:1117
  632.5 6.0 convert_element_type.128
  638.4 2.0 convert_element_type.123
  640.4 2.0 convert_element_type.124
  642.4 2.0 convert_element_type.125
  644.4 2.0 convert_element_type.126
  (145 shorter events, 25.8 us)
Async XLA Ops:
  162.3 12.9 %copy-start.15 = (bf16[1280,2560]{1,0:T(8,128)(2,1)S(1)}, bf16[1280,2560]{1,0:T(8,128)(2,1)}, u32[]{:S(2)}) copy-start(bf16[1280,2560]{1,0:T(8,128)(2,1)} %get-tuple-element.52) | copy-start | bytes 19660804
  175.3 10.7 %copy-start.14 = (bf16[2560,1280]{1,0:T(8,128)(2,1)S(1)}, bf16[2560,1280]{1,0:T(8,128)(2,1)}, u32[]{:S(2)}) copy-start(bf16[2560,1280]{1,0:T(8,128)(2,1)} %get-tuple-element.46) | copy-start | bytes 19660804
  175.3 10.7 %copy-start.16 = (bf16[1024,2560]{1,0:T(8,128)(2,1)S(1)}, bf16[1024,2560]{1,0:T(8,128)(2,1)}, u32[]{:S(2)}) copy-start(bf16[1024,2560]{1,0:T(8,128)(2,1)} %get-tuple-element.45) | copy-start | bytes 15728644
  184.6 8.3 %copy-start.3 = (f32[1024,1280]{1,0:T(8,128)}, f32[1024,1280]{1,0:T(8,128)S(1)}, u32[]{:S(2)}) copy-start(f32[1024,1280]{1,0:T(8,128)S(1)} %fusion.46) | copy-start | bytes 15728644
  185.9 51.2 %collective-permute-start.2 = (bf16[512,1280]{1,0:T(8,128)(2,1)}, bf16[512,1280]{1,0:T(8,128)(2,1)}, u32[]{:S(2)}, u32[]{:S(2)}) collective-permute-start(bf16[512,1280]{1,0:T(8,128)(2,1)} %slice.184), channel_id=1, source_target_pairs={{0,2},{1,3},{2,0},{3,1},{4,6},{5,7},{6,4},{7,5},{8,10},{9,11},{10,... | collective-permute-start | bytes 3932168 | tf_op jit(solution)/shard_map/ppermute | solution.py:362
  192.9 3.1 copy-start.4
  192.9 3.7 copy-start.1
  196.0 43.9 %collective-permute-start = (bf16[512,1280]{1,0:T(8,128)(2,1)}, bf16[512,1280]{1,0:T(8,128)(2,1)}, u32[]{:S(2)}, u32[]{:S(2)}) collective-permute-start(bf16[512,1280]{1,0:T(8,128)(2,1)} %slice.185), channel_id=1, source_target_pairs={{0,2},{1,3},{2,0},{3,1},{4,6},{5,7},{6,4},{7,5},{8,10},{9,11},{10,... | collective-permute-start | bytes 3932168 | tf_op jit(solution)/shard_map/ppermute | solution.py:362
  211.0 18.5 %copy-start.12 = (bf16[1024,1280]{1,0:T(8,128)(2,1)S(1)}, bf16[1024,1280]{1,0:T(8,128)(2,1)}, u32[]{:S(2)}) copy-start(bf16[1024,1280]{1,0:T(8,128)(2,1)} %get-tuple-element.50) | copy-start | bytes 7864324
  211.0 26.1 %slice-start = ((s8[5242880]{0:T(1024)(128)(4,1)}), s8[4194304]{0:T(1024)(128)(4,1)S(1)}, s32[]{:S(2)}) async-start(s8[5242880]{0:T(1024)(128)(4,1)} %bitcast.25), calls=%async_computation | async-start | bytes 8388608
  211.0 28.9 %slice-start.4 = ((s8[5242880]{0:T(1024)(128)(4,1)}), s8[4194304]{0:T(1024)(128)(4,1)S(1)}, s32[]{:S(2)}) async-start(s8[5242880]{0:T(1024)(128)(4,1)} %bitcast.29), calls=%async_computation.4 | async-start | bytes 8388608
  229.5 7.6 %slice-start.1 = ((s8[5242880]{0:T(1024)(128)(4,1)}), s8[1048576]{0:T(1024)(128)(4,1)S(1)}, s32[]{:S(2)}) async-start(s8[5242880]{0:T(1024)(128)(4,1)} %bitcast.25), calls=%async_computation.1 | async-start | bytes 2097152
  229.5 10.4 %slice-start.5 = ((s8[5242880]{0:T(1024)(128)(4,1)}), s8[1048576]{0:T(1024)(128)(4,1)S(1)}, s32[]{:S(2)}) async-start(s8[5242880]{0:T(1024)(128)(4,1)} %bitcast.29), calls=%async_computation.5 | async-start | bytes 2097152
  237.1 2.8 copy-start.9
  237.1 8.6 %slice-start.6 = ((s8[5242880]{0:T(1024)(128)(4,1)}), s8[4194304]{0:T(1024)(128)(4,1)S(1)}, s32[]{:S(2)}) async-start(s8[5242880]{0:T(1024)(128)(4,1)} %bitcast.36), calls=%async_computation.6 | async-start | bytes 8388608
  239.9 5.8 copy-start.20
  239.9 5.8 slice-start.7
  245.0 6.6 %copy-start.10 = (bf16[512,1280]{1,0:T(8,128)(2,1)}, bf16[512,1280]{1,0:T(8,128)(2,1)S(1)}, u32[]{:S(2)}) copy-start(bf16[512,1280]{1,0:T(8,128)(2,1)S(1)} %get-tuple-element.83) | copy-start | bytes 3932164
  245.0 6.6 %collective-permute-start.3 = (bf16[512,1280]{1,0:T(8,128)(2,1)S(1)}, bf16[512,1280]{1,0:T(8,128)(2,1)S(1)}, u32[]{:S(2)}, u32[]{:S(2)}) collective-permute-start(bf16[512,1280]{1,0:T(8,128)(2,1)S(1)} %get-tuple-element.83), channel_id=1, source_target_pairs={{0,2},{1,3},{2,0},{3,1},{4,6},{5,7},{6,4},{7,5},{8,10},{9,11},{10,... | collective-permute-start | bytes 3932168 | tf_op jit(solution)/shard_map/ppermute | solution.py:362
  245.8 5.9 copy-start.17
  250.9 55.8 %collective-permute-start.1 = (bf16[512,1280]{1,0:T(8,128)(2,1)}, bf16[512,1280]{1,0:T(8,128)(2,1)S(1)}, u32[]{:S(2)}, u32[]{:S(2)}) collective-permute-start(bf16[512,1280]{1,0:T(8,128)(2,1)} %get-tuple-element.85), channel_id=1, source_target_pairs={{1,2},{2,1},{5,6},{6,5},{9,10},{10,9},{13,14},{14,13},{17,18},{18,... | collective-permute-start | bytes 3932168 | tf_op jit(solution)/shard_map/ppermute | solution.py:368
  251.6 2.3 copy-start.21
  288.9 15.0 %copy-start.19 = (bf16[1024,1280]{1,0:T(8,128)(2,1)S(1)}, bf16[1024,1280]{1,0:T(8,128)(2,1)}, u32[]{:S(2)}) copy-start(bf16[1024,1280]{1,0:T(8,128)(2,1)} %get-tuple-element.62) | copy-start | bytes 7864324
  297.1 6.9 %copy-start.11 = (bf16[512,1280]{1,0:T(8,128)(2,1)S(1)}, bf16[512,1280]{1,0:T(8,128)(2,1)}, u32[]{:S(2)}) copy-start(bf16[512,1280]{1,0:T(8,128)(2,1)} %copy-done.10) | copy-start | bytes 3932164
  297.1 6.9 %copy-start.22 = (bf16[512,1280]{1,0:T(8,128)(2,1)S(1)}, bf16[512,1280]{1,0:T(8,128)(2,1)}, u32[]{:S(2)}) copy-start(bf16[512,1280]{1,0:T(8,128)(2,1)} %copy-done.21) | copy-start | bytes 3932164
  297.3 22.6 %collective-permute-start.4 = (bf16[512,1280]{1,0:T(8,128)(2,1)S(1)}, bf16[512,1280]{1,0:T(8,128)(2,1)S(1)}, u32[]{:S(2)}, u32[]{:S(2)}) collective-permute-start(bf16[512,1280]{1,0:T(8,128)(2,1)S(1)} %slice.183), channel_id=1, source_target_pairs={{0,2},{1,3},{2,0},{3,1},{4,6},{5,7},{6,4},{7,5},{8,10},{9,11},{10,... | collective-permute-start | bytes 3932168 | tf_op jit(solution)/shard_map/ppermute | solution.py:362
  315.7 4.1 copy-start.2
  322.6 329.9 %collective-permute-start.5 = (bf16[512,1280]{1,0:T(8,128)(2,1)S(1)}, bf16[512,1280]{1,0:T(8,128)(2,1)S(1)}, u32[]{:S(2)}, u32[]{:S(2)}) collective-permute-start(bf16[512,1280]{1,0:T(8,128)(2,1)S(1)} %fusion.10), channel_id=1, source_target_pairs={{1,2},{2,1},{5,6},{6,5},{9,10},{10,9},{13,14},{14,13},{17,18},{18,... | collective-permute-start | bytes 3932168 | tf_op jit(solution)/shard_map/ppermute | solution.py:368
  620.7 11.8 %slice-start.2 = ((s8[6553600]{0:T(1024)(128)(4,1)}), s8[4194304]{0:T(1024)(128)(4,1)S(1)}, s32[]{:S(2)}) async-start(s8[6553600]{0:T(1024)(128)(4,1)} %bitcast.27), calls=%async_computation.2 | async-start | bytes 8388608
  622.7 9.7 %slice-start.3 = ((s8[6553600]{0:T(1024)(128)(4,1)}), s8[2359296]{0:T(1024)(128)(4,1)S(1)}, s32[]{:S(2)}) async-start(s8[6553600]{0:T(1024)(128)(4,1)} %bitcast.27), calls=%async_computation.3 | async-start | bytes 4718592
  632.5 6.0 copy-start.8
  644.4 4.0 copy-start.13
  (5 other events, 10.4 us)

commit v4 on v3

--- a/solution.py
+++ b/solution.py
@@ -351,32 +351,7 @@
     )
 
 
-BOTH = ("cell", "seq")
-CORE_BIT = 2
 Q_BLOCK = 512
-VMEM = 48 * 1024 * 1024
-
-
-def across(value, bit):
-    count = lax.axis_size("cell") * lax.axis_size("seq")
-    return lax.ppermute(value, BOTH, [(i, i ^ bit) for i in range(count)])
-
-
-def across_diagonal(value):
-    count = lax.axis_size("cell") * lax.axis_size("seq")
-    pairs = [(i, i ^ 3) for i in range(count) if (i & 3) in (1, 2)]
-    return lax.ppermute(value, BOTH, pairs)
-
-
-def in_order(first, own, received, axis=0):
-    low = jnp.where(first, own, received)
-    high = jnp.where(first, received, own)
-    return jnp.concatenate([low, high], axis=axis)
-
-
-def half_of(value, index, axis=0):
-    size = value.shape[axis] // 2
-    return lax.dynamic_slice_in_dim(value, index * size, size, axis)
 
 
 MESH = pl.DeviceIdType.MESH
@@ -756,30 +731,96 @@
     )(*args)
 
 
-def reduce_kernel(
-    give_down, keep_down, give_up, keep_up, give_out, keep_out, give_qkv, keep_qkv, vec,
-    down_ref, up_ref, out_ref, q_ref, k_ref, v_ref, vec_ref,
-    acc, from_x, from_y, from_low, from_high, res, vec_acc, vec_in,
-    send_sems, recv_sems, load_sems, store_sems, vec_send, vec_recv, vec_local,
+def attend_back_pair(qkv, totals, keys_acc, values_acc, pair):
+    f32, bf16 = jnp.float32, jnp.bfloat16
+    rows = qkv.shape[0]
+    size = Q_BLOCK // 2
+    lane = lax.broadcasted_iota(jnp.int32, (1, 128), 1)
+    here, key_lanes, value_lanes, grad_lanes = (cols(i * EDGE + pair * 128, 128) for i in range(4))
+    keys = qkv[:, key_lanes]
+    keys_t = keys.T
+    nt = (((1,), (1,)), ((), ()))
+    keys_acc[...] = jnp.zeros_like(keys_acc)
+    values_acc[...] = jnp.zeros_like(values_acc)
+
+    @pl.loop(0, rows // size)
+    def _(block):
+        part = rows_at(block * size, size)
+        queries = qkv[part, here] * jnp.asarray(0.125, bf16)
+        grads = qkv[part, grad_lanes]
+        values = qkv[:, value_lanes]
+        outs = []
+        key_part = value_part = 0.0
+        for head in range(2):
+            own = (lane // HDIM) == head
+            q_own = jnp.where(own, queries, jnp.zeros_like(queries))
+            g_own = jnp.where(own, grads, jnp.zeros_like(grads))
+            scores = lax.dot_general(keys, q_own, nt, preferred_element_type=f32)
+            probs = jnp.exp(scores - totals[2 * pair + head, :, cols(block * size, size)])
+            grad_probs = lax.dot_general(values, g_own, nt, preferred_element_type=f32)
+            delta = jnp.sum(probs * grad_probs, axis=0, keepdims=True)
+            grad_scores = (probs * (grad_probs - delta)).astype(bf16)
+            value_part += jnp.dot(probs.astype(bf16), g_own, preferred_element_type=f32)
+            key_part += jnp.dot(grad_scores, q_own, preferred_element_type=f32)
+            outs.append(jnp.dot(keys_t[head * HDIM : (head + 1) * HDIM, :], grad_scores, preferred_element_type=f32))
+        qkv[part, here] = (jnp.concatenate(outs, axis=0) * 0.125).T.astype(bf16)
+        keys_acc[...] += key_part
+        values_acc[...] += value_part
+
+    qkv[:, key_lanes] = keys_acc[...].astype(bf16)
+    qkv[:, value_lanes] = values_acc[...].astype(bf16)
+
+
+def backward_kernel(
+    own, own_grad, cell_weight, vectors, qkv_w, out_w, up_w, down_w,
+    normed_one, qkv, mixed, totals, middle, normed_two, hidden, slope, ffn,
+    result_ref, input_ref, down_ref, up_ref, out_ref, q_ref, k_ref, v_ref, vec_ref,
+    wide, grad_up, normed, pair_buf, ffn_buf, down_buf, up_buf, part_buf, taken, given, mid, tot, vec, scale, keys_acc, values_acc,
+    blocks, from_x, from_y, from_low, from_high, res, sums,
+    send_sems, recv_sems, store_sems, load_sems, core_send, core_recv, swap_send, swap_recv, swap_local, vec_send, vec_recv, vec_local,
 ):
     f32, bf16 = jnp.float32, jnp.bfloat16
     at = Spot()
-    core = at.core
-    at.meet(("x", "core", "y", "low", "high"))
+    x, core = at.x, at.core
+    rows, width = own.shape
+    both = 2 * rows
+    top, bottom = pl.ds(0, rows), pl.ds(rows, rows)
+    nt = (((1,), (1,)), ((), ()))
+    tn = (((0,), (0,)), ((), ()))
+    loads = {}
+
+    def load(name, source, target):
+        copy = pltpu.make_async_copy(source, target, load_sems.at[len(loads)])
+        copy.start()
+        loads[name] = copy
+
+    load("hidden", hidden, wide)
+    load("ffn", ffn, ffn_buf)
+    load("down_w", down_w, down_buf)
+    slopes = [(slope.at[:, pl.ds(i * EDGE, EDGE)], pair_buf.at[:, pl.ds((i % 2) * EDGE, EDGE)]) for i in range(4)]
+    load("slope0", *slopes[0])
+    load("slope1", *slopes[1])
+    load("up_w", up_w, up_buf)
+    load("normed_two", normed_two, normed)
+    load("middle", middle, mid)
+    load("vectors", vectors, vec)
+    load("scale", cell_weight, scale)
+    load("totals", totals, tot)
+    sums[0] = jnp.zeros(sums.shape[1:], f32)
+    at.meet(("x", "core", "diagonal", "y", "low", "high"))
+
     chunks = []
     for i in range(4):
-        part = (pl.ds((i // 2) * EDGE, EDGE), pl.ds((i % 2) * EDGE, EDGE))
         target = down_ref.at[rows_at(core * 2 * EDGE + (i // 2) * EDGE, EDGE), pl.ds((i % 2) * EDGE, EDGE)]
-        chunks.append((give_down.at[part], keep_down.at[part], target))
+        chunks.append((wide, 2 * EDGE, (i // 2) * EDGE, ffn_buf, (i % 2) * EDGE, target))
     for i in range(4):
-        part = (slice(None), pl.ds(i * EDGE, EDGE))
         target = up_ref.at[:, cols((i // 2) * 4 * EDGE + core * 2 * EDGE + (i % 2) * EDGE, EDGE)]
-        chunks.append((give_up.at[part], keep_up.at[part], target))
+        chunks.append((normed, EDGE, 0, grad_up, i * EDGE, target))
     mine = cols(core * EDGE, EDGE)
-    chunks.append((give_out, keep_out, out_ref.at[:, mine]))
+    mixed_rows = pl.ds(EDGE, both)
+    chunks.append((down_buf.at[mixed_rows], EDGE, 0, ffn_buf, core * EDGE, out_ref.at[:, mine]))
     for i, ref in enumerate((q_ref, k_ref, v_ref)):
-        part = (slice(None), pl.ds(i * EDGE, EDGE))
-        chunks.append((give_qkv.at[part], keep_qkv.at[part], ref.at[:, mine]))
+        chunks.append((normed, EDGE, 0, wide, i * EDGE, ref.at[:, mine]))
     count = len(chunks)
 
     half, quarter, eighth = EDGE // 2, EDGE // 4, EDGE // 8
@@ -787,193 +828,359 @@
     l0 = y0 + at.low * quarter
     h0 = l0 + at.high * eighth
     ops = {}
-    for k, (give, keep, target) in enumerate(chunks):
+    for k, chunk in enumerate(chunks):
+        acc, two, slot = k % 5, k % 2, k % 5
         hops = (
-            ("x", "x", give, from_x.at[k]),
-            ("y", "y", acc.at[k, rows_at((1 - at.y) * half, half)], from_y.at[k]),
-            ("low", "low", acc.at[k, rows_at(y0 + (1 - at.low) * quarter, quarter)], from_low.at[k]),
-            ("high", "high", acc.at[k, rows_at(l0 + (1 - at.high) * eighth, eighth)], from_high.at[k]),
-            ("all_high", "high", res.at[k, rows_at(h0, eighth)], res.at[k, rows_at(h0, eighth)]),
-            ("all_low", "low", res.at[k, rows_at(l0, quarter)], res.at[k, rows_at(l0, quarter)]),
-            ("all_y", "y", res.at[k, rows_at(y0, half)], res.at[k, rows_at(y0, half)]),
-            ("core", "core", res.at[k], target),
+            ("x", "x", blocks.at[5 + k % 3], from_x.at[k % 4]),
+            ("y", "y", blocks.at[acc, rows_at((1 - at.y) * half, half)], from_y.at[two]),
+            ("low", "low", blocks.at[acc, rows_at(y0 + (1 - at.low) * quarter, quarter)], from_low.at[two]),
+            ("high", "high", blocks.at[acc, rows_at(l0 + (1 - at.high) * eighth, eighth)], from_high.at[two]),
+            ("all_high", "high", res.at[slot, rows_at(h0, eighth)], res.at[slot, rows_at(h0, eighth)]),
+            ("all_low", "low", res.at[slot, rows_at(l0, quarter)], res.at[slot, rows_at(l0, quarter)]),
+            ("all_y", "y", res.at[slot, rows_at(y0, half)], res.at[slot, rows_at(y0, half)]),
+            ("core", "core", res.at[slot], chunk[5]),
         )
         for s, (stage, name, source, goal) in enumerate(hops):
             ops[stage, k] = at.send(name, source, goal, send_sems.at[s, k], recv_sems.at[s, k])
-        ops["load", k] = pltpu.make_async_copy(keep, acc.at[k], load_sems.at[k])
-        ops["store", k] = pltpu.make_async_copy(res.at[k], target, store_sems.at[k])
-
-    def add(k, start, size, other, goal):
+        ops["store", k] = pltpu.make_async_copy(res.at[slot], chunk[5], store_sems.at[k])
+
+    def make(k):
+        left, stride, left_at, right, right_at, _ = chunks[k]
+
+        @pl.loop(0, 2)
+        def _(j):
+            of = j * x + (1 - j) * (1 - x)
+            slot = j * (k % 5) + (1 - j) * (5 + k % 3)
+            lanes = right_at if isinstance(right_at, int) else pl.multiple_of(right_at, 128)
+            product = lax.dot_general(
+                left[:, cols(of * stride + left_at, EDGE)], right[:, pl.ds(lanes, EDGE)], tn, preferred_element_type=f32
+            )
+            blocks[slot] = product.astype(bf16)
+
+        ops["x", k].start()
+
+    def add(k, start, size, other, goal, goal_slot):
         @pl.loop(0, size // 80)
         def _(i):
             here = rows_at(start + i * 80, 80)
             there = rows_at(i * 80, 80)
-            goal[k, here, :] = (acc[k, here, :].astype(f32) + other[k, there, :].astype(f32)).astype(bf16)
-
-    for k in range(2):
-        ops["x", k].start()
-        ops["load", k].start()
-    vec_load = pltpu.make_async_copy(vec, vec_acc.at[0], vec_local.at[0])
-    vec_load.start()
-    vec_load.wait()
-    vec_names = ("x", "core", "y", "low", "high")
-    vec_ops = [
-        at.send(name, vec_acc.at[i], vec_in.at[i], vec_send.at[i], vec_recv.at[i]) for i, name in enumerate(vec_names)
-    ]
+            total = blocks[k % 5, here, :].astype(f32) + other[there, :].astype(f32)
+            goal[goal_slot, here, :] = total.astype(bf16)
+
+    def tick(t):
+        k = t - 7
+        if 0 <= k < count:
+            ops["core", k].wait_recv()
+            for stage in ("all_high", "all_low", "all_y", "core"):
+                ops[stage, k].wait_send()
+            ops["store", k].wait()
+        for before, stage, after in ((6, "all_y", "core"), (5, "all_low", "all_y"), (4, "all_high", "all_low")):
+            k = t - before
+            if 0 <= k < count:
+                ops[stage, k].wait_recv()
+                ops[after, k].start()
+                if after == "core":
+                    ops["store", k].start()
+        k = t - 3
+        if 0 <= k < count:
+            ops["high", k].wait_recv()
+            add(k, h0, eighth, from_high.at[k % 2], res, k % 5)
+            ops["all_high", k].start()
+            for stage in ("y", "low", "high"):
+                ops[stage, k].wait_send()
+        k = t - 2
+        if 0 <= k < count:
+            ops["low", k].wait_recv()
+            add(k, l0, quarter, from_low.at[k % 2], blocks, k % 5)
+            ops["high", k].start()
+        k = t - 1
+        if 0 <= k < count:
+            ops["y", k].wait_recv()
+            add(k, y0, half, from_y.at[k % 2], blocks, k % 5)
+            ops["low", k].start()
+        k = t
+        if 0 <= k < count:
+            ops["x", k].wait_recv()
+            add(k, 0, EDGE, from_x.at[k % 4], blocks, k % 5)
+            ops["y", k].start()
+            ops["x", k].wait_send()
+            if k + 2 < count:
+                make(k + 2)
+
+    def core_copy(i, source, target):
+        return at.send("core", source, target, core_send.at[i], core_recv.at[i])
+
+    two_copy = core_copy(0, given.at[0], taken.at[0])
+    result_copy = core_copy(1, given.at[1], taken.at[1])
+    attn_copy = core_copy(2, ffn_buf.at[top], ffn_buf.at[bottom])
+    one_copy = core_copy(3, given.at[0], taken.at[0])
+    swaps = []
+    for i, target in enumerate((result_ref, input_ref)):
+        source = taken.at[1 - i]
+        swaps.append(
+            (
+                at.send("diagonal", source, target, swap_send.at[i], swap_recv.at[i]),
+                pltpu.make_async_copy(source, target, swap_local.at[i]),
+            )
+        )
+
+    def swap(i, act):
+        @pl.when(x != core)
+        def _():
+            act(swaps[i][0])
+
+        @pl.when(x == core)
+        def _():
+            act(swaps[i][1])
+
+    def vector(i):
+        return jnp.concatenate([vec[0, i : i + 1, :], vec[1, i : i + 1, :]], axis=1)
+
+    def add_vector(i, value):
+        total = jnp.sum(value, axis=0, keepdims=True)
+        sums[0, 2 * i : 2 * i + 1, :] += total[:, :EDGE]
+        sums[0, 2 * i + 1 : 2 * i + 2, :] += total[:, EDGE:]
+
+    def norm_back(values, grad_normed, gain):
+        average = jnp.mean(values, axis=-1, keepdims=True)
+        centred = values - average
+        inverse = lax.rsqrt(jnp.mean(centred * centred, axis=-1, keepdims=True) + 1e-05)
+        standard = centred * inverse
+        scaled = grad_normed * gain
+        back = inverse * (
+            scaled
+            - jnp.mean(scaled, axis=-1, keepdims=True)
+            - standard * jnp.mean(scaled * standard, axis=-1, keepdims=True)
+        )
+        return standard, back
+
+    loads["hidden"].wait()
+    loads["ffn"].wait()
+    make(0)
+    make(1)
+    loads["down_w"].wait()
+    for i in range(4):
+        loads["slope%d" % i].wait()
+        lanes = pl.ds(i * EDGE, EDGE)
+        row = pl.ds(16 + (i // 2) * 4 + core * 2 + i % 2, 1)
+
+        @pl.loop(0, both // 256)
+        def _(r):
+            here = rows_at(r * 256, 256)
+            value = lax.dot_general(ffn_buf[here, :], down_buf[lanes, :], nt, preferred_element_type=f32)
+            value = (value * pair_buf[here, pl.ds((i % 2) * EDGE, EDGE)].astype(f32)).astype(bf16)
+            grad_up[here, lanes] = value
+            sums[0, row, :] += jnp.sum(value.astype(f32), axis=0, keepdims=True)
+
+        if i < 2:
+            load("slope%d" % (i + 2), *slopes[i + 2])
+    load("own_grad", own_grad, pair_buf.at[top])
+    load("own", own, pair_buf.at[bottom])
+    loads["normed_two"].wait()
+    tick(0)
+    loads["up_w"].wait()
+
+    @pl.loop(0, rows // 256)
+    def _(r):
+        value = lax.dot_general(grad_up[rows_at(rows + r * 256, 256), :], up_buf[...], nt, preferred_element_type=f32)
+        given[0, rows_at(r * 256, 256), :] = value.astype(bf16)
+
+    two_copy.start()
+
+    @pl.loop(0, rows // 256)
+    def _(r):
+        value = lax.dot_general(grad_up[rows_at(r * 256, 256), :], up_buf[...], nt, preferred_element_type=f32)
+        part_buf[rows_at(r * 256, 256), :] = value
+
+    tick(1)
+
+    @pl.loop(0, rows // 256)
+    def _(r):
+        value = jnp.dot(wide[rows_at(rows + r * 256, 256), :], down_buf[...], preferred_element_type=f32)
+        given[1, rows_at(r * 256, 256), :] = value.astype(bf16)
+
+    result_copy.start()
+    two_copy.wait_recv()
+    for name in ("middle", "vectors", "scale", "own_grad", "totals"):
+        loads[name].wait()
+    result_copy.wait_recv()
+    down_bias, gain_two, gain_one = vector(7), vector(5), vector(0)
+
+    @pl.loop(0, rows // 128)
+    def _(r):
+        here = rows_at(r * 128, 128)
+        value = jnp.dot(wide[here, :], down_buf[...], preferred_element_type=f32)
+        value = mid[here, :] + value + taken[1, here, :].astype(f32) + down_bias
+        taken[1, here, :] = value.astype(bf16)
+
+    swap(0, lambda copy: copy.start())
+    load("qkv", qkv, wide.at[:, pl.ds(0, 3 * EDGE)])
+    load("mixed", mixed, down_buf.at[mixed_rows])
+    load("out_w", out_w.at[rows_at(core * EDGE, EDGE)], down_buf.at[pl.ds(0, EDGE)])
+    load("qkv_w", qkv_w, up_buf.at[:, pl.ds(0, 3 * EDGE)])
+    weight = scale[0:1, 0:1]
+
+    @pl.loop(0, rows // 32)
+    def _(r):
+        here = rows_at(r * 32, 32)
+        add_vector(7, ffn_buf[here, :].astype(f32))
+        grad_normed = part_buf[here, :] + taken[0, here, :].astype(f32)
+        standard, back = norm_back(mid[here, :], grad_normed, gain_two)
+        add_vector(5, grad_normed * standard)
+        add_vector(6, grad_normed)
+        value = pair_buf[here, :].astype(f32) * weight + back
+        mid[here, :] = value
+        value = value.astype(bf16)
+        ffn_buf[here, :] = value
+        add_vector(4, value.astype(f32))
+
+    attn_copy.start()
+    two_copy.wait_send()
+    tick(2)
+    loads["out_w"].wait()
+    attn_copy.wait_recv()
+
+    @pl.loop(0, both // 256)
+    def _(r):
+        here = rows_at(r * 256, 256)
+        value = lax.dot_general(ffn_buf[here, :], down_buf[0:EDGE, :], nt, preferred_element_type=f32)
+        wide[here, pl.ds(3 * EDGE, EDGE)] = value.astype(bf16)
+
+    loads["qkv"].wait()
+
+    @pl.loop(0, EDGE // 128)
+    def _(pair):
+        attend_back_pair(wide, tot, keys_acc, values_acc, pair)
+
+        @pl.when(pair == 0)
+        def _():
+            tick(3)
+
+        @pl.when(pair == 2)
+        def _():
+            tick(4)
+
+    tick(5)
+    load("normed_one", normed_one, normed)
+    loads["mixed"].wait()
+    tick(6)
+    loads["qkv_w"].wait()
+    weights = pl.ds(0, 3 * EDGE)
+
+    @pl.loop(0, rows // 256)
+    def _(r):
+        value = lax.dot_general(
+            wide[rows_at(rows + r * 256, 256), weights], up_buf[:, weights], nt, preferred_element_type=f32
+        )
+        given[0, rows_at(r * 256, 256), :] = value.astype(bf16)
+
+    one_copy.start()
+    loads["normed_one"].wait()
+    tick(7)
+
+    @pl.loop(0, rows // 256)
+    def _(r):
+        value = lax.dot_general(wide[rows_at(r * 256, 256), weights], up_buf[:, weights], nt, preferred_element_type=f32)
+        part_buf[rows_at(r * 256, 256), :] = value
+
+    one_copy.wait_recv()
+    loads["own"].wait()
+
+    @pl.loop(0, rows // 32)
+    def _(r):
+        here = rows_at(r * 32, 32)
+        tok = pair_buf[rows_at(rows + r * 32, 32), :].astype(f32)
+        grad_normed = part_buf[here, :] + taken[0, here, :].astype(f32)
+        standard, back = norm_back(tok, grad_normed, gain_one)
+        add_vector(0, grad_normed * standard)
+        add_vector(1, grad_normed)
+        taken[0, here, :] = (mid[here, :] + back).astype(bf16)
+
+    swap(1, lambda copy: copy.start())
+
+    @pl.loop(0, both // 128)
+    def _(r):
+        here = rows_at(r * 128, 128)
+        for i in (0, 2):
+            row = pl.ds(4 + i + core, 1)
+            value = wide[here, pl.ds(i * EDGE, EDGE)].astype(f32)
+            sums[0, row, :] += jnp.sum(value, axis=0, keepdims=True)
+
+    names = ("x", "core", "y", "low", "high")
+    vec_ops = [at.send(name, sums.at[i], sums.at[6 + i], vec_send.at[i], vec_recv.at[i]) for i, name in enumerate(names)]
     vec_ops[0].start()
-    after = ("y", "low", "high", "all_high", "all_low", "all_y", "core", None)
-    stages = ("x",) + after[:-1]
-    for tick in range(count + 7):
-        for before, (stage, following) in reversed(list(enumerate(zip(stages, after)))):
-            k = tick - before
-            if not 0 <= k < count:
-                continue
-            ops[stage, k].wait_recv()
-            if stage == "x":
-                if k + 2 < count:
-                    ops["x", k + 2].start()
-                    ops["load", k + 2].start()
-                ops["load", k].wait()
-                add(k, 0, EDGE, from_x, acc)
-            elif stage == "y":
-                add(k, y0, half, from_y, acc)
-            elif stage == "low":
-                add(k, l0, quarter, from_low, acc)
-            elif stage == "high":
-                add(k, h0, eighth, from_high, res)
-            if following:
-                ops[following, k].start()
-            if stage == "all_y":
-                ops["store", k].start()
-        if tick < 5:
-            vec_ops[tick].wait_recv()
-            vec_acc[tick + 1] = vec_acc[tick] + vec_in[tick]
-            if tick < 4:
-                vec_ops[tick + 1].start()
-    vec_store = pltpu.make_async_copy(vec_acc.at[5], vec_ref, vec_local.at[1])
+    for t in range(8, count + 7):
+        tick(t)
+        if t < 13:
+            i = t - 8
+            vec_ops[i].wait_recv()
+            sums[i + 1] = sums[i] + sums[6 + i]
+            if i < 4:
+                vec_ops[i + 1].start()
+    vec_store = pltpu.make_async_copy(sums.at[5], vec_ref, vec_local.at[0])
     vec_store.start()
     vec_store.wait()
-    for op in vec_ops:
+    for op in (result_copy, attn_copy, one_copy, *vec_ops):
         op.wait_send()
-    for k in range(count):
-        for stage in stages:
-            ops[stage, k].wait_send()
-        ops["store", k].wait()
-
-
-def reduce(*args):
+    swap(0, lambda copy: copy.wait())
+    swap(1, lambda copy: copy.wait())
+    tick(count + 7)
+
+
+def backward(*args):
     bf16, f32 = jnp.bfloat16, jnp.float32
-    shape = jax.ShapeDtypeStruct
-    vec = args[-1]
-    count = 12
-    square = shape((EDGE, 2 * EDGE), bf16)
+    rows, width = args[0].shape
+    both = 2 * rows
+    outs = [
+        ((rows, width), bf16),
+        ((rows, width), bf16),
+        ((4 * EDGE, width), bf16),
+        ((EDGE, 8 * EDGE), bf16),
+        ((EDGE, width), bf16),
+        ((EDGE, width), bf16),
+        ((EDGE, width), bf16),
+        ((EDGE, width), bf16),
+        ((24, EDGE), f32),
+    ]
+    scratch = [
+        ((both, 4 * EDGE), bf16),
+        ((both, 4 * EDGE), bf16),
+        ((both, width), bf16),
+        ((both, width), bf16),
+        ((both, width), bf16),
+        ((4 * EDGE, width), bf16),
+        ((width, 4 * EDGE), bf16),
+        ((rows, width), f32),
+        ((2, rows, width), bf16),
+        ((2, rows, width), bf16),
+        ((rows, width), f32),
+        ((EDGE // HDIM, 1, both), f32),
+        ((2, 16, EDGE), f32),
+        ((8, 128), f32),
+        ((both, 128), f32),
+        ((both, 128), f32),
+        ((8, EDGE, EDGE), bf16),
+        ((4, EDGE, EDGE), bf16),
+        ((2, EDGE // 2, EDGE), bf16),
+        ((2, EDGE // 4, EDGE), bf16),
+        ((2, EDGE // 8, EDGE), bf16),
+        ((5, EDGE, EDGE), bf16),
+        ((11, 24, EDGE), f32),
+    ]
+    dma = pltpu.SemaphoreType.DMA
     return pl.pallas_call(
-        reduce_kernel,
+        backward_kernel,
         in_specs=[ANY] * len(args),
-        out_specs=[ANY] * 7,
-        out_shape=[
-            shape((4 * EDGE, 2 * EDGE), bf16),
-            shape((EDGE, 8 * EDGE), bf16),
-            square,
-            square,
-            square,
-            square,
-            shape(vec.shape, f32),
-        ],
-        scratch_shapes=[
-            pltpu.VMEM((count, EDGE, EDGE), bf16),
-            pltpu.VMEM((count, EDGE, EDGE), bf16),
-            pltpu.VMEM((count, EDGE // 2, EDGE), bf16),
-            pltpu.VMEM((count, EDGE // 4, EDGE), bf16),
-            pltpu.VMEM((count, EDGE // 8, EDGE), bf16),
-            pltpu.VMEM((count, EDGE, EDGE), bf16),
-            pltpu.VMEM((6,) + vec.shape, f32),
-            pltpu.VMEM((5,) + vec.shape, f32),
-            pltpu.SemaphoreType.DMA((8, count)),
-            pltpu.SemaphoreType.DMA((8, count)),
-            pltpu.SemaphoreType.DMA((count,)),
-            pltpu.SemaphoreType.DMA((count,)),
-            pltpu.SemaphoreType.DMA((5,)),
-            pltpu.SemaphoreType.DMA((5,)),
-            pltpu.SemaphoreType.DMA((2,)),
-        ],
+        out_specs=[ANY] * len(outs),
+        out_shape=[jax.ShapeDtypeStruct(*out) for out in outs],
+        scratch_shapes=[pltpu.VMEM(*array) for array in scratch]
+        + [dma((8, 12)), dma((8, 12)), dma((12,)), dma((20,)), dma((4,)), dma((4,))]
+        + [dma((2,)), dma((2,)), dma((2,)), dma((5,)), dma((5,)), dma((1,))],
         compiler_params=pltpu.CompilerParams(
-            collective_id=1, has_side_effects=True, vmem_limit_bytes=56 * 1024 * 1024
+            collective_id=1, has_side_effects=True, vmem_limit_bytes=64 * 1024 * 1024
         ),
-        name="reduce",
+        name="backward",
     )(*args)
-
-
-def attend_back_kernel(q_ref, k_ref, v_ref, total_ref, grad_ref, dq_ref, dk_ref, dv_ref, dk_acc, dv_acc):
-    f32, bf16 = jnp.float32, jnp.bfloat16
-    rows, lanes = q_ref.shape
-    lane = lax.broadcasted_iota(jnp.int32, (1, lanes), 1)
-    keys = k_ref[...]
-    keys_t = keys.T
-    values = v_ref[...]
-    nt = (((1,), (1,)), ((), ()))
-    for block in range(rows // Q_BLOCK):
-        part = pl.ds(block * Q_BLOCK, Q_BLOCK)
-        queries = q_ref[part, :] * jnp.asarray(0.125, bf16)
-        grads = grad_ref[part, :]
-        outs = []
-        key_part = None
-        value_part = None
-        for head in range(2):
-            own = (lane // HDIM) == head
-            q_own = jnp.where(own, queries, jnp.zeros_like(queries))
-            g_own = jnp.where(own, grads, jnp.zeros_like(grads))
-            scores = lax.dot_general(keys, q_own, nt, preferred_element_type=f32)
-            probs = jnp.exp(scores - total_ref[head, :, part])
-            grad_probs = lax.dot_general(values, g_own, nt, preferred_element_type=f32)
-            delta = jnp.sum(probs * grad_probs, axis=0, keepdims=True)
-            grad_scores = (probs * (grad_probs - delta)).astype(bf16)
-            one_value = jnp.dot(probs.astype(bf16), g_own, preferred_element_type=f32)
-            one_key = jnp.dot(grad_scores, q_own, preferred_element_type=f32)
-            value_part = one_value if head == 0 else value_part + one_value
-            key_part = one_key if head == 0 else key_part + one_key
-            outs.append(
-                jnp.dot(
-                    keys_t[head * HDIM : (head + 1) * HDIM, :],
-                    grad_scores,
-                    preferred_element_type=f32,
-                )
-            )
-        dq_ref[part, :] = (jnp.concatenate(outs, axis=0) * 0.125).T.astype(bf16)
-        if block == 0:
-            dk_acc[...] = key_part
-            dv_acc[...] = value_part
-        else:
-            dk_acc[...] += key_part
-            dv_acc[...] += value_part
-    dk_ref[...] = dk_acc[...].astype(bf16)
-    dv_ref[...] = dv_acc[...].astype(bf16)
-
-
-def attend_back(qkv, total, grad_mixed):
-    rows, width = grad_mixed.shape
-    pairs = width // 128
-    macs = 5 * rows * rows * width
-    block = pl.BlockSpec((rows, 128), lambda p: (0, p))
-    return pl.pallas_call(
-        attend_back_kernel,
-        grid=(pairs,),
-        in_specs=[
-            block,
-            pl.BlockSpec((rows, 128), lambda p: (0, pairs + p)),
-            pl.BlockSpec((rows, 128), lambda p: (0, 2 * pairs + p)),
-            pl.BlockSpec((2, 1, rows), lambda p: (p, 0, 0)),
-            block,
-        ],
-        out_specs=[block] * 3,
-        out_shape=[jax.ShapeDtypeStruct((rows, width), jnp.bfloat16)] * 3,
-        scratch_shapes=[pltpu.VMEM((rows, 128), jnp.float32)] * 2,
-        compiler_params=pltpu.CompilerParams(vmem_limit_bytes=VMEM),
-        cost_estimate=pl.CostEstimate(
-            flops=8 * macs, bytes_accessed=14 * rows * width, transcendentals=macs // 320
-        ),
-        name="attend_back",
-    )(qkv, qkv, qkv, total, grad_mixed)
 
 
 def tuned(
@@ -998,34 +1205,12 @@
 ):
     f32, bf16 = jnp.float32, jnp.bfloat16
     x = lax.axis_index("seq")
-    core = lax.axis_index("cell") % 2
-    swapped = x != core
-    rows, width = tokens.shape[1:]
-    hidden_width = up_weight.shape[1] // 2
-    head_width = width // 2
+    head_width = tokens.shape[2] // 2
 
     vectors = (first_gain, first_bias, query_bias, value_bias, output_bias, second_gain, second_bias, down_bias)
     vectors = jnp.concatenate([jnp.stack(vectors), up_bias.reshape(4, -1), jnp.zeros((4, head_width), bf16)])
     cell_weight = jnp.broadcast_to(jnp.sqrt(query_counts.astype(f32) / 1000.0), (8, 128))
-    (
-        own,
-        own_grad,
-        cell_weight,
-        vectors,
-        qkv_weight,
-        out_weight,
-        up_all,
-        down_all,
-        normed_one,
-        qkv,
-        mixed,
-        log_total,
-        middle,
-        normed_two,
-        hidden,
-        slope,
-        grad_ffn,
-    ) = forward(
+    state = forward(
         tokens[0],
         out_grad[0],
         cell_weight,
@@ -1037,87 +1222,27 @@
         up_weight,
         down_weight,
     )
-    gain_one, gain_two, d_bias = (vectors[:, i].reshape(-1) for i in (0, 5, 7))
-    standard_one, inverse_one = standardize(own.astype(f32))
-    standard_two, inverse_two = standardize(middle)
-
-    grad_result = own_grad.astype(f32) * cell_weight[:1, :1]
-
-    def weight_sum(left, right):
-        give = weight_grad(half_of(left, 1 - x, 1), right).astype(bf16)
-        keep = weight_grad(half_of(left, x, 1), right).astype(bf16)
-        return give, keep
-
-    sum_down = weight_sum(hidden, grad_ffn)
-    grad_up = (matmul_right_t(grad_ffn, down_all) * slope.astype(f32)).astype(bf16)
-    sum_up = weight_sum(normed_two, grad_up)
-    partial = matmul_right_t(grad_up, up_all)
-    grad_normed_two = partial[:rows] + across(partial[rows:].astype(bf16), CORE_BIT).astype(f32)
-    grad_middle = grad_result + standardize_back(grad_normed_two, standard_two, inverse_two, gain_two)
-    grad_attn_own = grad_middle.astype(bf16)
-    grad_attn = jnp.concatenate([grad_attn_own, across(grad_attn_own, CORE_BIT)])
-    sum_out = weight_sum(mixed, half_of(grad_attn, core, 1))
-
-    partial = matmul(hidden, down_all)
-    result = middle + partial[:rows] + across(partial[rows:].astype(bf16), CORE_BIT).astype(f32) + d_bias
-    result = result.astype(bf16)
-    result = jnp.where(swapped, across_diagonal(result), result)
-
-    grad_mixed = matmul_right_t(grad_attn, half_of(out_weight, core)).astype(bf16)
-    grad_qkv = jnp.concatenate(attend_back(qkv, log_total, grad_mixed), axis=1)
-    sum_qkv = weight_sum(normed_one, grad_qkv)
-    partial = matmul_right_t(grad_qkv, qkv_weight)
-    grad_normed_one = partial[:rows] + across(partial[rows:].astype(bf16), CORE_BIT).astype(f32)
-    input_grad = grad_middle + standardize_back(grad_normed_one, standard_one, inverse_one, gain_one)
-    input_grad = input_grad.astype(bf16)
-    input_grad = jnp.where(swapped, across_diagonal(input_grad), input_grad)
-
-    def at_core(value):
-        zero = jnp.zeros_like(value)
-        return jnp.concatenate([jnp.where(core == 0, value, zero), jnp.where(core == 0, zero, value)], axis=-1)
-
-    qkv_sum = column_sum(grad_qkv).reshape(3, head_width)
-    up_sum = at_core(column_sum(grad_up).reshape(2, 1, -1)).reshape(-1)
-    sums = [
-        jnp.sum(grad_normed_one * standard_one, axis=0),
-        jnp.sum(grad_normed_one, axis=0),
-        at_core(qkv_sum[0]),
-        at_core(qkv_sum[2]),
-        column_sum(grad_attn_own),
-        jnp.sum(grad_normed_two * standard_two, axis=0),
-        jnp.sum(grad_normed_two, axis=0),
-        column_sum(grad_ffn[:rows]),
-        up_sum,
-    ]
-    sizes = [value.shape[0] for value in sums]
-    packed = jnp.concatenate(sums)
-    packed = jnp.pad(packed, (0, -packed.shape[0] % 8192)).reshape(-1, 1024)
-    down_sum, up_sum, out_sum, *qkv_sum, packed = reduce(*sum_down, *sum_up, *sum_out, *sum_qkv, packed)
-    packed = packed.reshape(-1)
-    sums = []
-    for size in sizes:
-        sums.append(half_of(packed[:size], x))
-        packed = packed[size:]
-    s_gain_one, s_bias_one, s_q_bias, s_v_bias, s_o_bias, s_gain_two, s_bias_two, s_d_bias, s_u_bias = sums
-
+    result, input_grad, down, up, out, query, key, value, sums = backward(*state)
+    short = lax.dynamic_index_in_dim(sums[:16].reshape(8, 2, head_width), x, 1, keepdims=False)
+    up_sum = lax.dynamic_slice_in_dim(sums, 16 + 4 * x, 4, 0).reshape(-1)
     return (
         result[None],
         input_grad[None],
-        s_gain_one,
-        s_bias_one,
-        qkv_sum[0].astype(f32),
-        s_q_bias,
-        qkv_sum[1].astype(f32),
-        qkv_sum[2].astype(f32),
-        s_v_bias,
-        out_sum.astype(f32),
-        s_o_bias,
-        s_gain_two,
-        s_bias_two,
-        up_sum.astype(f32),
-        s_u_bias,
-        down_sum.astype(f32),
-        s_d_bias,
+        short[0],
+        short[1],
+        query.astype(f32),
+        short[2],
+        key.astype(f32),
+        value.astype(f32),
+        short[3],
+        out.astype(f32),
+        short[4],
+        short[5],
+        short[6],
+        up.astype(f32),
+        up_sum,
+        down.astype(f32),
+        short[7],
     )
 
 

time: 664 us -> 525 us (0.79)
  matrix products: 91.5 us -> 0 us
  other arithmetic: 43.3 us -> 24.2 us
  local copies, waits for them, and re-layouts: 23.2 us -> 10.3 us
  starting transfers between devices: 9.18 us -> 0 us
    dot_general x13 -> x0, matrix products: 91.5 us -> none  [the longest x8 52 us: weight_grad(): jnp.einsum('ti,to->io', left, right, preferred_element_type=jnp.float32)]
    reduce_sum x9 -> x0, other arithmetic: 13.9 us -> none  [the longest x3 5.87 us: column_sum(): return jnp.sum(values.astype(jnp.float32), axis=0)]
    ppermute x6 -> x0, starting transfers between devices: 9.18 us -> none  [the longest x4 7.7 us: across(): return lax.ppermute(value, BOTH, [(i, i ^ bit) for i in range(count)])]
    pallas_call x2 -> x1, Pallas kernels: 331 us -> 327 us  [backward(): pl.pallas_call(backward_kernel, in_specs=[ANY] * len(args), out_specs=[AN...]
    convert_element_type x7 -> x6, other arithmetic: 24.9 us -> 23.5 us  [the longest x1 9.74 us: tuned(): up.astype(f32)]
  transfers between devices with their start and end apart: 6 -> 0, of which waited for: 0 -> 0; matrix products, arithmetic and copies ran while one was open for 18% -> 0% of each run, Pallas kernels for 51% -> 0%
where the time goes in v4:
time: 525 us; the launch traced here: 517 us
  Pallas kernels  480 us (91%)
  other arithmetic  24.2 us (5%)
  local copies, waits for them, and re-layouts  10.3 us (2%)
    pallas_call x1, Pallas kernels, backward(): pl.pallas_call(backward_kernel, in_specs=[ANY] * len(args), out_specs=[AN...  327 us
    pallas_call x1, Pallas kernels, forward(): pl.pallas_call(forward_kernel, in_specs=[ANY] * len(args), out_specs=[ANY...  154 us

profile of v4, /device:TPU:0, one launch (start us, length us, event | category | flops | bytes accessed | tf_op | source)
XLA Modules:
  0.0 516.6 jit_solution(1193234738711073506)
XLA Ops:
  0.7 0.7 reshape.60
  1.4 0.7 stack.24
  2.0 0.7 stack.25
  2.7 0.7 stack.26
  3.4 0.7 stack.27
  4.1 0.7 stack.28
  4.8 0.7 stack.29
  5.5 0.7 stack.30
  6.2 0.7 stack.31
  6.9 0.1 concatenate.3
  6.9 0.6 convert_element_type.25.vectors
  8.2 0.6 broadcast_in_dim.14.cell_weight
  8.8 153.5 %forward.1 = (bf16[512,1280]{1,0:T(8,128)(2,1)}, bf16[512,1280]{1,0:T(8,128)(2,1)}, f32[8,128]{1,0:T(8,128)}, f32[2,16,640]{2,1,0:T(8,128)}, bf16[1280,1920]{1,0...) custom-call(bf16[512,1280]{1,0:T(8,128)(2,1)} %bitcast.5, ...), custom_call_target="tpu_custom_call" | custom-call | tf_op jit(solution)/shard_map/forward/pallas_call | solution.py:721
  162.4 326.7 %backward.1 = (bf16[512,1280]{1,0:T(8,128)(2,1)}, bf16[512,1280]{1,0:T(8,128)(2,1)}, bf16[2560,1280]{1,0:T(8,128)(2,1)}, bf16[640,5120]{1,0:T(8,128)(2,1)}, bf16...) custom-call(bf16[512,1280]{1,0:T(8,128)(2,1)} %get-tuple-element.43., ...), custom_call_target="tpu_custom_call" | custom-call | tf_op jit(solution)/shard_map/backward/pallas_call | solution.py:1171
  489.1 0.0 copy-start
  489.1 9.7 %convert_element_type.30 = f32[640,5120]{1,0:T(8,128)} convert(bf16[640,5120]{1,0:T(8,128)(2,1)} %get-tuple-element.67) | non-fusion elementwise | flops 3276800 | bytes 19660800 | tf_op jit(solution)/shard_map/convert_element_type | solution.py:1242
  498.9 0.0 copy-done
  498.9 6.0 %convert_element_type.31 = f32[2560,1280]{1,0:T(8,128)} convert(bf16[2560,1280]{1,0:T(8,128)(2,1)S(1)} %copy-done) | non-fusion elementwise | flops 3276800 | bytes 19660800 | tf_op jit(solution)/shard_map/convert_element_type | solution.py:1244
  504.8 0.0 copy-done.4
  504.8 2.0 convert_element_type.26
  506.8 0.0 copy-done.3
  506.8 2.0 convert_element_type.27
  508.8 0.0 copy-done.2
  508.8 2.0 convert_element_type.28
  510.7 0.0 copy-done.1
  510.7 2.0 convert_element_type.29
  512.7 0.0 copy-done.7
  512.7 0.7 dynamic-slice_reduce_fusion
  513.4 0.6 reshape.62
  514.0 0.0 copy-done.6
  514.0 1.1 copy.38
  515.1 1.1 copy.39
  (12 shorter events, 0.1 us)
Async XLA Ops:
  489.1 9.8 %copy-start = (bf16[2560,1280]{1,0:T(8,128)(2,1)S(1)}, bf16[2560,1280]{1,0:T(8,128)(2,1)}, u32[]{:S(2)}) copy-start(bf16[2560,1280]{1,0:T(8,128)(2,1)} %get-tuple-element.68) | copy-start | bytes 19660804
  498.9 6.0 %copy-start.4 = (bf16[640,1280]{1,0:T(8,128)(2,1)S(1)}, bf16[640,1280]{1,0:T(8,128)(2,1)}, u32[]{:S(2)}) copy-start(bf16[640,1280]{1,0:T(8,128)(2,1)} %get-tuple-element.63) | copy-start | bytes 4915204
  504.8 2.0 copy-start.3
  506.8 2.0 copy-start.2
  508.8 2.0 copy-start.1
  510.7 2.0 copy-start.7
  510.7 3.3 copy-start.6
  512.7 2.4 copy-start.5

commit v5 on v4

--- a/solution.py
+++ b/solution.py
@@ -357,6 +357,8 @@
 MESH = pl.DeviceIdType.MESH
 ANY = pl.BlockSpec(memory_space=pl.ANY)
 EDGE = 640
+WIDE = 256
+RING = 10
 
 
 class Spot:
@@ -467,33 +469,59 @@
         swap(i, lambda c: c.wait(), lambda c: c.wait())
 
     chunks = []
-    for i, ref in enumerate((wq, wk, wv)):
-        chunks.append((ref.at[:, cols(core * EDGE, EDGE)], qkv_w, EDGE, 0, i * EDGE))
-    for i in range(4):
-        start = (i // 2) * 4 * EDGE + core * 2 * EDGE + (i % 2) * EDGE
-        chunks.append((wup.at[:, cols(start, EDGE)], up_w, EDGE, 0, i * EDGE))
-    for i in range(4):
-        source = wdown.at[rows_at(core * 2 * EDGE + (i // 2) * EDGE, EDGE), pl.ds((i % 2) * EDGE, EDGE)]
-        chunks.append((source, down_w, 2 * EDGE, (i // 2) * EDGE, (i % 2) * EDGE))
+    for start in range(0, 3 * EDGE, WIDE):
+        width_now = min(WIDE, 3 * EDGE - start)
+        parts = []
+        for i, ref in enumerate((wq, wk, wv)):
+            low, high = max(start, i * EDGE), min(start + width_now, (i + 1) * EDGE)
+            if low < high:
+                parts.append((ref.at[:, cols(core * EDGE + low - i * EDGE, high - low)], low))
+        chunks.append((parts, qkv_w, EDGE, 0, start, width_now))
+    for start in range(0, 4 * EDGE, WIDE):
+        part = start // (2 * EDGE) * 2 * EDGE + start + core * 2 * EDGE
+        chunks.append(([(wup.at[:, cols(part, WIDE)], start)], up_w, EDGE, 0, start, WIDE))
+    for start in range(0, 2 * EDGE, WIDE):
+        source = wdown.at[rows_at(core * 2 * EDGE, EDGE), pl.ds(start, WIDE)]
+        chunks.append(([(source, start)], down_w, 2 * EDGE, 0, start, WIDE))
     count = len(chunks)
     eighth = EDGE // 8
     place = at.y * 4 + at.low * 2 + at.high
 
-    def region(k, half, start, size):
-        _, ref, stride, row, column = chunks[k]
-        return ref.at[rows_at(half * stride + row + start * eighth, size * eighth), pl.ds(column, EDGE)]
+    def region(k, half, start, size, column=None, width=None):
+        _, ref, stride, row, first, most = chunks[k]
+        column, width = (first, most) if column is None else (column, width)
+        return ref.at[rows_at(half * stride + row + start * eighth, size * eighth), pl.ds(column, width)]
 
     ops = {}
     for k, chunk in enumerate(chunks):
-        ops["x", k] = at.send(
-            "x", chunk[0].at[rows_at(place * eighth, eighth)], region(k, x, place, 1), send_sems.at[0, k], recv_sems.at[0, k]
-        )
+        ops["x", k] = [
+            at.send(
+                "x",
+                source.at[rows_at(place * eighth, eighth)],
+                region(k, x, place, 1, column, source.shape[1]),
+                send_sems.at[4 * j, k],
+                recv_sems.at[4 * j, k],
+            )
+            for j, (source, column) in enumerate(chunk[0])
+        ]
         for s, (name, start, size) in enumerate(
             (("high", place, 1), ("low", at.y * 4 + at.low * 2, 2), ("y", at.y * 4, 4))
         ):
             part = region(k, 1 - x, start, size)
-            ops[name, k] = at.send(name, part, part, send_sems.at[s + 1, k], recv_sems.at[s + 1, k])
-        ops["local", k] = pltpu.make_async_copy(chunk[0], region(k, x, 0, 8), local_sems.at[k])
+            ops[name, k] = [at.send(name, part, part, send_sems.at[s + 1, k], recv_sems.at[s + 1, k])]
+    direct = []
+    for i, start in enumerate(range(0, 2 * EDGE, WIDE)):
+        source = wdown.at[rows_at(core * 2 * EDGE + EDGE, EDGE), pl.ds(start, WIDE)]
+        target = down_w.at[rows_at(x * 2 * EDGE + EDGE, EDGE), pl.ds(start, WIDE)]
+        direct.append(at.send("x", source, target, send_sems.at[5, i], recv_sems.at[5, i]))
+    owns = []
+    mine = rows_at(x * EDGE, EDGE)
+    for i, ref in enumerate((wq, wk, wv)):
+        owns.append((ref.at[:, cols(core * EDGE, EDGE)], qkv_w.at[mine, pl.ds(i * EDGE, EDGE)]))
+    for i in range(2):
+        owns.append((wup.at[:, cols((2 * i + core) * 2 * EDGE, 2 * EDGE)], up_w.at[mine, pl.ds(i * 2 * EDGE, 2 * EDGE)]))
+    owns.append((wdown.at[rows_at(core * 2 * EDGE, 2 * EDGE)], down_w.at[rows_at(x * 2 * EDGE, 2 * EDGE)]))
+    owns = [pltpu.make_async_copy(source, target, local_sems.at[i]) for i, (source, target) in enumerate(owns)]
     half = EDGE // 2
     out_x = at.send(
         "x", wo.at[rows_at(core * half, half)], out_w.at[rows_at(x * EDGE + core * half, half)], side_send.at[4], side_recv.at[4]
@@ -526,37 +554,44 @@
         outs.append(copy)
         return copy
 
-    issue = {
-        0: [ops["x", 3], ops["x", 4]],
-        1: [ops["x", 5], ops["x", 6]],
-        2: [out_x, out_local, ops["local", 3], ops["local", 4], ops["local", 5], ops["local", 6]],
-        3: [ops["x", 7], ops["x", 8]],
-        4: [ops["x", 9], ops["x", 10], ops["local", 7], ops["local", 8], ops["local", 9], ops["local", 10]],
-    }
+    stages = ("x", "high", "low", "y")
+
+    def begin(name, k):
+        for op in ops[name, k]:
+            op.start()
 
     def tick(t):
-        for op in issue.get(t, ()):
-            op.start()
-        if t == 5:
-            swap_start(2)
-        for before, name, after in ((3, "y", None), (2, "low", "y"), (1, "high", "low"), (0, "x", "high")):
-            k = t - before
+        for s, name in enumerate(stages):
+            k = t - s
             if 0 <= k < count:
-                ops[name, k].wait_recv()
-                if after:
-                    ops[after, k].start()
-        if t == 6:
+                for op in ops[name, k]:
+                    op.wait_recv()
+                if s < 3:
+                    begin(stages[s + 1], k)
+        if t + 3 < count:
+            begin("x", t + 3)
+        if t == 3:
+            out_x.start()
+        if t == 8:
             out_x.wait_recv()
             out_core.start()
-
-    for k in range(3):
-        ops["x", k].start()
+        if t % 2 and 5 <= t < 5 + 2 * len(direct):
+            direct[(t - 5) // 2].start()
+        if t == 14:
+            swap_start(2)
+        if t in (1, 2, 4):
+            for op in {1: (out_local,), 2: owns[3:5], 4: owns[5:]}[t]:
+                op.start()
+
+    begin("x", 0)
+    begin("x", 1)
+    begin("x", 2)
     vec_x.start()
     swap_start(0)
     swap_start(1)
     vec_local.start()
-    for k in range(3):
-        ops["local", k].start()
+    for op in owns[:3]:
+        op.start()
     tick(0)
     tick(1)
     vec_x.wait_recv()
@@ -581,13 +616,15 @@
 
     normed_one_core.start()
     tick(2)
+    tick(3)
     put(tok, own_out)
     normed_one_core.wait_recv()
     put(normed_one, normed_one_out)
 
     for i in range(3):
-        tick(3 + i)
-        ops["local", i].wait()
+        for t in ((4, 5), (6, 7), (8, 9, 10))[i]:
+            tick(t)
+        owns[i].wait()
         lanes = pl.ds(i * EDGE, EDGE)
         bias = 0.0 if i == 1 else vec[core, 2 + i // 2 : 3 + i // 2, :]
 
@@ -604,18 +641,16 @@
     def _(pair):
         attend_pair(qkv, mixed, totals, pair, core * EDGE)
 
-        @pl.when(pair == 1)
-        def _():
-            tick(6)
-
-        @pl.when(pair == 3)
-        def _():
-            tick(7)
+        for i in range(5):
+
+            @pl.when(pair == i)
+            def _():
+                tick(11 + i)
 
     mixed_core[0].start()
     mixed_core[1].start()
     put(totals, total_out)
-    tick(8)
+    tick(16)
     out_local.wait()
     out_core.wait_recv()
     mixed_core[1].wait_recv()
@@ -634,12 +669,13 @@
     put(out_w, out_w_out)
     put(mixed, mixed_out)
     put(middle, middle_out)
-    tick(9)
+    tick(17)
     normed_two_core.wait_recv()
     put(normed_two, normed_two_out)
     waits = {}
     for i in range(4):
-        ops["local", 3 + i].wait()
+        if i % 2 == 0:
+            owns[3 + i // 2].wait()
         slot = i % 2
         if i >= 2:
             for copy in waits[slot]:
@@ -674,16 +710,19 @@
             put(grad, grad_out)
             put(scale, weight_out)
             put(vec, vectors_out)
-        tick(10 + i)
+        for t in ((18,), (19, 20), (21, 22), (23, 24, 25))[i]:
+            tick(t)
     put(up_w, up_w_out)
     ffn_core.wait_recv()
     put(ffn, ffn_out)
-    for k in range(7, count):
-        ops["local", k].wait()
+    owns[5].wait()
+    for op in direct:
+        op.wait()
     put(down_w, down_w_out)
     for k in range(count):
-        for name in ("x", "high", "low", "y"):
-            ops[name, k].wait_send()
+        for name in stages:
+            for op in ops[name, k]:
+                op.wait_send()
     for op in (out_x, out_core, vec_x, normed_one_core, *mixed_core, normed_two_core, ffn_core):
         op.wait_send()
     for copy in outs:
@@ -723,7 +762,7 @@
         in_specs=[ANY] * len(args),
         out_specs=[ANY] * len(arrays),
         out_shape=[shape(*array) for array in arrays],
-        scratch_shapes=scratch + [dma((4, 11)), dma((4, 11)), dma((11,)), dma((11,)), dma((11,)), dma((5,)), dma((24,))],
+        scratch_shapes=scratch + [dma((6, 23)), dma((6, 23)), dma((6,)), dma((11,)), dma((11,)), dma((5,)), dma((24,))],
         compiler_params=pltpu.CompilerParams(
             collective_id=0, has_side_effects=True, vmem_limit_bytes=60 * 1024 * 1024
         ),
@@ -810,17 +849,30 @@
     at.meet(("x", "core", "diagonal", "y", "low", "high"))
 
     chunks = []
-    for i in range(4):
-        target = down_ref.at[rows_at(core * 2 * EDGE + (i // 2) * EDGE, EDGE), pl.ds((i % 2) * EDGE, EDGE)]
-        chunks.append((wide, 2 * EDGE, (i // 2) * EDGE, ffn_buf, (i % 2) * EDGE, target))
-    for i in range(4):
-        target = up_ref.at[:, cols((i // 2) * 4 * EDGE + core * 2 * EDGE + (i % 2) * EDGE, EDGE)]
-        chunks.append((normed, EDGE, 0, grad_up, i * EDGE, target))
-    mine = cols(core * EDGE, EDGE)
+    for i in range(2):
+        for start in range(0, 2 * EDGE, WIDE):
+            target = down_ref.at[rows_at(core * 2 * EDGE + i * EDGE, EDGE), pl.ds(start, WIDE)]
+            chunks.append([(wide, 2 * EDGE, i * EDGE, ffn_buf, start, WIDE, target)])
+    for start in range(0, 4 * EDGE, WIDE):
+        target = up_ref.at[:, cols(start // (2 * EDGE) * 2 * EDGE + start + core * 2 * EDGE, WIDE)]
+        chunks.append([(normed, EDGE, 0, grad_up, start, WIDE, target)])
     mixed_rows = pl.ds(EDGE, both)
-    chunks.append((down_buf.at[mixed_rows], EDGE, 0, ffn_buf, core * EDGE, out_ref.at[:, mine]))
-    for i, ref in enumerate((q_ref, k_ref, v_ref)):
-        chunks.append((normed, EDGE, 0, wide, i * EDGE, ref.at[:, mine]))
+
+    def out_part(start, width):
+        target = out_ref.at[:, cols(core * EDGE + start, width)]
+        return (down_buf.at[mixed_rows], EDGE, 0, ffn_buf, core * EDGE + start, width, target)
+
+    last = EDGE % WIDE
+    chunks += [[out_part(start, WIDE)] for start in range(0, EDGE - last, WIDE)]
+    for start in range(0, 3 * EDGE, WIDE):
+        parts = []
+        for i, ref in enumerate((q_ref, k_ref, v_ref)):
+            first, end = max(start, i * EDGE), min(start + WIDE, (i + 1) * EDGE)
+            if first < end:
+                target = ref.at[:, cols(core * EDGE + first - i * EDGE, end - first)]
+                parts.append((normed, EDGE, 0, wide, first, end - first, target))
+        chunks.append(parts)
+    chunks[-1].append(out_part(EDGE - last, last))
     count = len(chunks)
 
     half, quarter, eighth = EDGE // 2, EDGE // 4, EDGE // 8
@@ -828,84 +880,108 @@
     l0 = y0 + at.low * quarter
     h0 = l0 + at.high * eighth
     ops = {}
-    for k, chunk in enumerate(chunks):
-        acc, two, slot = k % 5, k % 2, k % 5
+    for k, parts in enumerate(chunks):
+        acc, four, slot, sem = k % 6, k % 4, k % 7, k % RING
         hops = (
-            ("x", "x", blocks.at[5 + k % 3], from_x.at[k % 4]),
-            ("y", "y", blocks.at[acc, rows_at((1 - at.y) * half, half)], from_y.at[two]),
-            ("low", "low", blocks.at[acc, rows_at(y0 + (1 - at.low) * quarter, quarter)], from_low.at[two]),
-            ("high", "high", blocks.at[acc, rows_at(l0 + (1 - at.high) * eighth, eighth)], from_high.at[two]),
+            ("x", "x", blocks.at[6 + k % 3], from_x.at[four]),
+            ("y", "y", blocks.at[acc, rows_at((1 - at.y) * half, half)], from_y.at[four]),
+            ("low", "low", blocks.at[acc, rows_at(y0 + (1 - at.low) * quarter, quarter)], from_low.at[four]),
+            ("high", "high", blocks.at[acc, rows_at(l0 + (1 - at.high) * eighth, eighth)], from_high.at[four]),
             ("all_high", "high", res.at[slot, rows_at(h0, eighth)], res.at[slot, rows_at(h0, eighth)]),
             ("all_low", "low", res.at[slot, rows_at(l0, quarter)], res.at[slot, rows_at(l0, quarter)]),
             ("all_y", "y", res.at[slot, rows_at(y0, half)], res.at[slot, rows_at(y0, half)]),
-            ("core", "core", res.at[slot], chunk[5]),
         )
         for s, (stage, name, source, goal) in enumerate(hops):
-            ops[stage, k] = at.send(name, source, goal, send_sems.at[s, k], recv_sems.at[s, k])
-        ops["store", k] = pltpu.make_async_copy(res.at[slot], chunk[5], store_sems.at[k])
+            ops[stage, k] = [at.send(name, source, goal, send_sems.at[s, sem], recv_sems.at[s, sem])]
+        ops["core", k] = []
+        ops["store", k] = []
+        start = 0
+        for s, part in enumerate(parts):
+            source = res.at[slot, :, pl.ds(start, part[5])]
+            ops["core", k].append(at.send("core", source, part[6], send_sems.at[7 + s, sem], recv_sems.at[7 + s, sem]))
+            ops["store", k].append(pltpu.make_async_copy(source, part[6], store_sems.at[s, sem]))
+            start += part[5]
+
+    def begin(stage, k):
+        for op in ops[stage, k]:
+            op.start()
+
+    def came(stage, k):
+        for op in ops[stage, k]:
+            op.wait_recv()
+
+    def left_here(stage, k):
+        for op in ops[stage, k]:
+            op.wait_send()
 
     def make(k):
-        left, stride, left_at, right, right_at, _ = chunks[k]
-
         @pl.loop(0, 2)
         def _(j):
             of = j * x + (1 - j) * (1 - x)
-            slot = j * (k % 5) + (1 - j) * (5 + k % 3)
-            lanes = right_at if isinstance(right_at, int) else pl.multiple_of(right_at, 128)
-            product = lax.dot_general(
-                left[:, cols(of * stride + left_at, EDGE)], right[:, pl.ds(lanes, EDGE)], tn, preferred_element_type=f32
-            )
-            blocks[slot] = product.astype(bf16)
-
-        ops["x", k].start()
+            slot = j * (k % 6) + (1 - j) * (6 + k % 3)
+            start = 0
+            for left, stride, left_at, right, right_at, width_now, _ in chunks[k]:
+                lanes = right_at if isinstance(right_at, int) else pl.multiple_of(right_at, 128)
+                product = lax.dot_general(
+                    left[:, cols(of * stride + left_at, EDGE)],
+                    right[:, pl.ds(lanes, width_now)],
+                    tn,
+                    preferred_element_type=f32,
+                )
+                blocks[slot, :, start : start + width_now] = product.astype(bf16)
+                start += width_now
+
+        begin("x", k)
 
     def add(k, start, size, other, goal, goal_slot):
         @pl.loop(0, size // 80)
         def _(i):
             here = rows_at(start + i * 80, 80)
             there = rows_at(i * 80, 80)
-            total = blocks[k % 5, here, :].astype(f32) + other[there, :].astype(f32)
+            total = blocks[k % 6, here, :].astype(f32) + other[there, :].astype(f32)
             goal[goal_slot, here, :] = total.astype(bf16)
 
     def tick(t):
+        k = t
+        if 0 <= k < count:
+            came("x", k)
+            add(k, 0, EDGE, from_x.at[k % 4], blocks, k % 6)
+            begin("y", k)
+            if k >= 1:
+                left_here("x", k - 1)
+            if k + 2 < count:
+                make(k + 2)
+        k = t - 1
+        if 0 <= k < count:
+            came("y", k)
+            add(k, y0, half, from_y.at[k % 4], blocks, k % 6)
+            begin("low", k)
+        k = t - 2
+        if 0 <= k < count:
+            came("low", k)
+            add(k, l0, quarter, from_low.at[k % 4], blocks, k % 6)
+            begin("high", k)
+        k = t - 3
+        if 0 <= k < count:
+            came("high", k)
+            add(k, h0, eighth, from_high.at[k % 4], res, k % 7)
+            begin("all_high", k)
+            for stage in ("y", "low", "high"):
+                left_here(stage, k)
+        for before, stage, after in ((4, "all_high", "all_low"), (5, "all_low", "all_y"), (6, "all_y", "core")):
+            k = t - before
+            if 0 <= k < count:
+                came(stage, k)
+                begin(after, k)
+                if after == "core":
+                    begin("store", k)
         k = t - 7
         if 0 <= k < count:
-            ops["core", k].wait_recv()
+            came("core", k)
             for stage in ("all_high", "all_low", "all_y", "core"):
-                ops[stage, k].wait_send()
-            ops["store", k].wait()
-        for before, stage, after in ((6, "all_y", "core"), (5, "all_low", "all_y"), (4, "all_high", "all_low")):
-            k = t - before
-            if 0 <= k < count:
-                ops[stage, k].wait_recv()
-                ops[after, k].start()
-                if after == "core":
-                    ops["store", k].start()
-        k = t - 3
-        if 0 <= k < count:
-            ops["high", k].wait_recv()
-            add(k, h0, eighth, from_high.at[k % 2], res, k % 5)
-            ops["all_high", k].start()
-            for stage in ("y", "low", "high"):
-                ops[stage, k].wait_send()
-        k = t - 2
-        if 0 <= k < count:
-            ops["low", k].wait_recv()
-            add(k, l0, quarter, from_low.at[k % 2], blocks, k % 5)
-            ops["high", k].start()
-        k = t - 1
-        if 0 <= k < count:
-            ops["y", k].wait_recv()
-            add(k, y0, half, from_y.at[k % 2], blocks, k % 5)
-            ops["low", k].start()
-        k = t
-        if 0 <= k < count:
-            ops["x", k].wait_recv()
-            add(k, 0, EDGE, from_x.at[k % 4], blocks, k % 5)
-            ops["y", k].start()
-            ops["x", k].wait_send()
-            if k + 2 < count:
-                make(k + 2)
+                left_here(stage, k)
+            for op in ops["store", k]:
+                op.wait()
 
     def core_copy(i, source, target):
         return at.send("core", source, target, core_send.at[i], core_recv.at[i])
@@ -974,10 +1050,11 @@
 
         if i < 2:
             load("slope%d" % (i + 2), *slopes[i + 2])
+        if i == 1:
+            loads["normed_two"].wait()
+        tick(i)
     load("own_grad", own_grad, pair_buf.at[top])
     load("own", own, pair_buf.at[bottom])
-    loads["normed_two"].wait()
-    tick(0)
     loads["up_w"].wait()
 
     @pl.loop(0, rows // 256)
@@ -986,19 +1063,22 @@
         given[0, rows_at(r * 256, 256), :] = value.astype(bf16)
 
     two_copy.start()
+    tick(4)
 
     @pl.loop(0, rows // 256)
     def _(r):
         value = lax.dot_general(grad_up[rows_at(r * 256, 256), :], up_buf[...], nt, preferred_element_type=f32)
         part_buf[rows_at(r * 256, 256), :] = value
 
-    tick(1)
+    tick(5)
 
     @pl.loop(0, rows // 256)
     def _(r):
         value = jnp.dot(wide[rows_at(rows + r * 256, 256), :], down_buf[...], preferred_element_type=f32)
         given[1, rows_at(r * 256, 256), :] = value.astype(bf16)
 
+    tick(6)
+    tick(7)
     result_copy.start()
     two_copy.wait_recv()
     for name in ("middle", "vectors", "scale", "own_grad", "totals"):
@@ -1019,6 +1099,7 @@
     load("out_w", out_w.at[rows_at(core * EDGE, EDGE)], down_buf.at[pl.ds(0, EDGE)])
     load("qkv_w", qkv_w, up_buf.at[:, pl.ds(0, 3 * EDGE)])
     weight = scale[0:1, 0:1]
+    tick(8)
 
     @pl.loop(0, rows // 32)
     def _(r):
@@ -1036,7 +1117,7 @@
 
     attn_copy.start()
     two_copy.wait_send()
-    tick(2)
+    tick(9)
     loads["out_w"].wait()
     attn_copy.wait_recv()
 
@@ -1047,23 +1128,17 @@
         wide[here, pl.ds(3 * EDGE, EDGE)] = value.astype(bf16)
 
     loads["qkv"].wait()
+    tick(10)
 
     @pl.loop(0, EDGE // 128)
     def _(pair):
         attend_back_pair(wide, tot, keys_acc, values_acc, pair)
-
-        @pl.when(pair == 0)
-        def _():
-            tick(3)
-
-        @pl.when(pair == 2)
-        def _():
-            tick(4)
-
-    tick(5)
-    load("normed_one", normed_one, normed)
-    loads["mixed"].wait()
-    tick(6)
+        for i in range(5):
+
+            @pl.when(pair == i)
+            def _():
+                tick(11 + i)
+
     loads["qkv_w"].wait()
     weights = pl.ds(0, 3 * EDGE)
 
@@ -1075,14 +1150,17 @@
         given[0, rows_at(r * 256, 256), :] = value.astype(bf16)
 
     one_copy.start()
-    loads["normed_one"].wait()
-    tick(7)
+    tick(16)
+    tick(17)
+    load("normed_one", normed_one, normed)
+    loads["mixed"].wait()
 
     @pl.loop(0, rows // 256)
     def _(r):
         value = lax.dot_general(wide[rows_at(r * 256, 256), weights], up_buf[:, weights], nt, preferred_element_type=f32)
         part_buf[rows_at(r * 256, 256), :] = value
 
+    tick(18)
     one_copy.wait_recv()
     loads["own"].wait()
 
@@ -1097,6 +1175,8 @@
         taken[0, here, :] = (mid[here, :] + back).astype(bf16)
 
     swap(1, lambda copy: copy.start())
+    tick(19)
+    loads["normed_one"].wait()
 
     @pl.loop(0, both // 128)
     def _(r):
@@ -1109,10 +1189,10 @@
     names = ("x", "core", "y", "low", "high")
     vec_ops = [at.send(name, sums.at[i], sums.at[6 + i], vec_send.at[i], vec_recv.at[i]) for i, name in enumerate(names)]
     vec_ops[0].start()
-    for t in range(8, count + 7):
+    for t in range(20, count + 7):
         tick(t)
-        if t < 13:
-            i = t - 8
+        if t < 25:
+            i = t - 20
             vec_ops[i].wait_recv()
             sums[i + 1] = sums[i] + sums[6 + i]
             if i < 4:
@@ -1124,7 +1204,7 @@
         op.wait_send()
     swap(0, lambda copy: copy.wait())
     swap(1, lambda copy: copy.wait())
-    tick(count + 7)
+    left_here("x", count - 1)
 
 
 def backward(*args):
@@ -1159,12 +1239,12 @@
         ((8, 128), f32),
         ((both, 128), f32),
         ((both, 128), f32),
-        ((8, EDGE, EDGE), bf16),
-        ((4, EDGE, EDGE), bf16),
-        ((2, EDGE // 2, EDGE), bf16),
-        ((2, EDGE // 4, EDGE), bf16),
-        ((2, EDGE // 8, EDGE), bf16),
-        ((5, EDGE, EDGE), bf16),
+        ((9, EDGE, WIDE), bf16),
+        ((4, EDGE, WIDE), bf16),
+        ((4, EDGE // 2, WIDE), bf16),
+        ((4, EDGE // 4, WIDE), bf16),
+        ((4, EDGE // 8, WIDE), bf16),
+        ((7, EDGE, WIDE), bf16),
         ((11, 24, EDGE), f32),
     ]
     dma = pltpu.SemaphoreType.DMA
@@ -1174,7 +1254,7 @@
         out_specs=[ANY] * len(outs),
         out_shape=[jax.ShapeDtypeStruct(*out) for out in outs],
         scratch_shapes=[pltpu.VMEM(*array) for array in scratch]
-        + [dma((8, 12)), dma((8, 12)), dma((12,)), dma((20,)), dma((4,)), dma((4,))]
+        + [dma((9, RING)), dma((9, RING)), dma((2, RING)), dma((20,)), dma((4,)), dma((4,))]
         + [dma((2,)), dma((2,)), dma((2,)), dma((5,)), dma((5,)), dma((1,))],
         compiler_params=pltpu.CompilerParams(
             collective_id=1, has_side_effects=True, vmem_limit_bytes=64 * 1024 * 1024

time: 525 us -> 477 us (0.909)
  Pallas kernels: 480 us -> 432 us
    pallas_call x1, Pallas kernels: 327 us -> 287 us  [backward(): pl.pallas_call(backward_kernel, in_specs=[ANY] * len(args), out_specs=[AN...]
    pallas_call x1, Pallas kernels: 154 us -> 145 us  [forward(): pl.pallas_call(forward_kernel, in_specs=[ANY] * len(args), out_specs=[ANY...]
where the time goes in v5:
time: 477 us; the launch traced here: 468 us
  Pallas kernels  432 us (91%)
  other arithmetic  24.2 us (5%)
  local copies, waits for them, and re-layouts  10.3 us (2%)
    pallas_call x1, Pallas kernels, backward(): pl.pallas_call(backward_kernel, in_specs=[ANY] * len(args), out_specs=[AN...  287 us
    pallas_call x1, Pallas kernels, forward(): pl.pallas_call(forward_kernel, in_specs=[ANY] * len(args), out_specs=[ANY...  145 us
    convert_element_type x1, other arithmetic, tuned(): up.astype(f32)  9.74 us

profile of v5, /device:TPU:0, one launch (start us, length us, event | category | flops | bytes accessed | tf_op | source)
XLA Modules:
  0.0 467.7 jit_solution(2536019693920893681)
XLA Ops:
  0.7 0.7 reshape.60
  1.4 0.7 stack.24
  2.0 0.7 stack.25
  2.7 0.7 stack.26
  3.4 0.7 stack.27
  4.1 0.7 stack.28
  4.8 0.7 stack.29
  5.5 0.7 stack.30
  6.2 0.7 stack.31
  6.9 0.1 concatenate.3
  6.9 0.6 convert_element_type.25.vectors
  8.2 0.6 broadcast_in_dim.14.cell_weight
  8.8 145.0 %forward.1 = (bf16[512,1280]{1,0:T(8,128)(2,1)}, bf16[512,1280]{1,0:T(8,128)(2,1)}, f32[8,128]{1,0:T(8,128)}, f32[2,16,640]{2,1,0:T(8,128)}, bf16[1280,1920]{1,0...) custom-call(bf16[512,1280]{1,0:T(8,128)(2,1)} %bitcast.5, ...), custom_call_target="tpu_custom_call" | custom-call | tf_op jit(solution)/shard_map/forward/pallas_call | solution.py:760
  153.8 286.6 %backward.1 = (bf16[512,1280]{1,0:T(8,128)(2,1)}, bf16[512,1280]{1,0:T(8,128)(2,1)}, bf16[2560,1280]{1,0:T(8,128)(2,1)}, bf16[640,5120]{1,0:T(8,128)(2,1)}, bf16...) custom-call(bf16[512,1280]{1,0:T(8,128)(2,1)} %get-tuple-element.43., ...), custom_call_target="tpu_custom_call" | custom-call | tf_op jit(solution)/shard_map/backward/pallas_call | solution.py:1251
  440.4 0.0 copy-start
  440.4 9.7 %convert_element_type.30 = f32[640,5120]{1,0:T(8,128)} convert(bf16[640,5120]{1,0:T(8,128)(2,1)} %get-tuple-element.67) | non-fusion elementwise | flops 3276800 | bytes 19660800 | tf_op jit(solution)/shard_map/convert_element_type | solution.py:1322
  450.1 0.0 copy-done
  450.1 6.0 %convert_element_type.31 = f32[2560,1280]{1,0:T(8,128)} convert(bf16[2560,1280]{1,0:T(8,128)(2,1)S(1)} %copy-done) | non-fusion elementwise | flops 3276800 | bytes 19660800 | tf_op jit(solution)/shard_map/convert_element_type | solution.py:1324
  456.1 0.0 copy-done.4
  456.1 2.0 convert_element_type.26
  458.1 0.0 copy-done.3
  458.1 2.0 convert_element_type.27
  460.1 0.0 copy-done.2
  460.1 2.0 convert_element_type.28
  462.0 0.0 copy-done.1
  462.0 2.0 convert_element_type.29
  464.0 0.0 copy-done.7
  464.0 0.7 dynamic-slice_reduce_fusion
  464.7 0.6 reshape.62
  465.3 0.0 copy-done.6
  465.3 1.1 copy.38
  466.4 1.1 copy.39
  (12 shorter events, 0.1 us)
Async XLA Ops:
  440.4 9.8 %copy-start = (bf16[2560,1280]{1,0:T(8,128)(2,1)S(1)}, bf16[2560,1280]{1,0:T(8,128)(2,1)}, u32[]{:S(2)}) copy-start(bf16[2560,1280]{1,0:T(8,128)(2,1)} %get-tuple-element.68) | copy-start | bytes 19660804
  450.1 6.0 %copy-start.4 = (bf16[640,1280]{1,0:T(8,128)(2,1)S(1)}, bf16[640,1280]{1,0:T(8,128)(2,1)}, u32[]{:S(2)}) copy-start(bf16[640,1280]{1,0:T(8,128)(2,1)} %get-tuple-element.63) | copy-start | bytes 4915204
  456.1 2.0 copy-start.3
  458.1 2.0 copy-start.2
  460.1 2.0 copy-start.1
  462.0 2.0 copy-start.7
  462.0 3.3 copy-start.6
  464.0 2.4 copy-start.5

commit v6 on v5

--- a/solution.py
+++ b/solution.py
@@ -351,7 +351,7 @@
     )
 
 
-Q_BLOCK = 512
+Q_BLOCK = 256
 
 
 MESH = pl.DeviceIdType.MESH
@@ -434,19 +434,70 @@
         mixed[part, cols(base + here, 128)] = jnp.concatenate(outs, axis=0).T.astype(bf16)
 
 
-def forward_kernel(
-    tokens, out_grad, cell_weight, vectors, wq, wk, wv, wo, wup, wdown,
-    own_out, grad_out, weight_out, vectors_out, qkv_w_out, out_w_out, up_w_out, down_w_out,
-    normed_one_out, qkv_out, mixed_out, total_out, middle_out, normed_two_out, hidden_out, slope_out, ffn_out,
-    tok, grad, scale, vec, qkv_w, out_w, up_w, down_w,
-    normed_one, qkv, mixed, totals, middle, normed_two, hidden, slope, ffn,
-    send_sems, recv_sems, local_sems, side_send, side_recv, side_local, out_sems,
+def attend_back_pair(qkv, totals, keys_acc, values_acc, pair):
+    f32, bf16 = jnp.float32, jnp.bfloat16
+    rows = qkv.shape[0]
+    size = Q_BLOCK
+    lane = lax.broadcasted_iota(jnp.int32, (1, 128), 1)
+    here, key_lanes, value_lanes, grad_lanes = (cols(i * EDGE + pair * 128, 128) for i in range(4))
+    keys = qkv[:, key_lanes]
+    keys_t = keys.T
+    nt = (((1,), (1,)), ((), ()))
+    keys_acc[...] = jnp.zeros_like(keys_acc)
+    values_acc[...] = jnp.zeros_like(values_acc)
+
+    @pl.loop(0, rows // size)
+    def _(block):
+        part = rows_at(block * size, size)
+        queries = qkv[part, here] * jnp.asarray(0.125, bf16)
+        grads = qkv[part, grad_lanes]
+        values = qkv[:, value_lanes]
+        outs = []
+        key_part = value_part = 0.0
+        for head in range(2):
+            own = (lane // HDIM) == head
+            q_own = jnp.where(own, queries, jnp.zeros_like(queries))
+            g_own = jnp.where(own, grads, jnp.zeros_like(grads))
+            scores = lax.dot_general(keys, q_own, nt, preferred_element_type=f32)
+            probs = jnp.exp(scores - totals[2 * pair + head, :, cols(block * size, size)])
+            grad_probs = lax.dot_general(values, g_own, nt, preferred_element_type=f32)
+            delta = jnp.sum(probs * grad_probs, axis=0, keepdims=True)
+            grad_scores = (probs * (grad_probs - delta)).astype(bf16)
+            value_part += jnp.dot(probs.astype(bf16), g_own, preferred_element_type=f32)
+            key_part += jnp.dot(grad_scores, q_own, preferred_element_type=f32)
+            outs.append(jnp.dot(keys_t[head * HDIM : (head + 1) * HDIM, :], grad_scores, preferred_element_type=f32))
+        qkv[part, here] = (jnp.concatenate(outs, axis=0) * 0.125).T.astype(bf16)
+        keys_acc[...] += key_part
+        values_acc[...] += value_part
+
+    qkv[:, key_lanes] = keys_acc[...].astype(bf16)
+    qkv[:, value_lanes] = values_acc[...].astype(bf16)
+
+
+def layer_kernel(
+    tokens, out_grad, counts, wq, wk, wv, wo, wup, wdown, v0, v1, v2, v3, v4, v5, v6, v7, v8,
+    result_ref, input_ref, down_ref, up_ref, out_ref, q_ref, k_ref, v_ref, vec_ref, normed_spill, qkv_spill, mixed_spill,
+    pair, scale, vec, qkv_w, out_w, up_w, down_w, normed, wide, grad_up, ffn, mid, partial_sum, taken, given, tot,
+    keys_acc, values_acc, blocks, from_x, from_y, from_low, from_high, res, sums,
+    cell_weight, vectors, send_sems, recv_sems, local_sems, side_send, side_recv, side_local, out_sems,
+    sum_send, sum_recv, store_sems, load_sems, swap_send, swap_recv, swap_local, vec_send, vec_recv, vec_store_sem,
 ):
     f32, bf16 = jnp.float32, jnp.bfloat16
     at = Spot()
     x, core = at.x, at.core
-    rows = tok.shape[0]
-    width = tok.shape[1]
+    rows, width = tokens.shape
+    both = 2 * rows
+    top, bottom = pl.ds(0, rows), pl.ds(rows, rows)
+    grad, tok = pair.at[top], pair.at[bottom]
+    nt = (((1,), (1,)), ((), ()))
+    tn = (((0,), (0,)), ((), ()))
+    sums[0] = jnp.zeros(sums.shape[1:], f32)
+    for i, ref in enumerate((v0, v1, v2, v3, v4, v5, v6, v7)):
+        vectors[i : i + 1, :] = ref[...].astype(f32).reshape(1, EDGE)
+    for i in range(4):
+        vectors[8 + i : 9 + i, :] = v8[i * EDGE : (i + 1) * EDGE].astype(f32).reshape(1, EDGE)
+    vectors[12:16, :] = jnp.zeros((4, EDGE), f32)
+    cell_weight[...] = jnp.sqrt(jnp.full(cell_weight.shape, counts[0], jnp.int32).astype(f32) / 1000.0)
     at.meet(("x", "core", "diagonal", "y", "low", "high"))
 
     side = [(tokens, tok), (cell_weight, scale), (out_grad, grad)]
@@ -531,45 +582,40 @@
     out_local = pltpu.make_async_copy(wo, out_w.at[rows_at(x * EDGE, EDGE)], side_local.at[4])
     vec_x = at.send("x", vectors, vec.at[x], side_send.at[3], side_recv.at[3])
     vec_local = pltpu.make_async_copy(vectors, vec.at[x], side_local.at[3])
-    top, bottom = pl.ds(0, rows), pl.ds(rows, rows)
-
     def core_copy(i, source, target):
         return at.send("core", source, target, side_send.at[i], side_recv.at[i])
 
-    normed_one_core = core_copy(6, normed_one.at[top], normed_one.at[bottom])
+    normed_one_core = core_copy(6, normed.at[top], normed.at[bottom])
     heads = cols(core * EDGE, EDGE)
     mixed_core = [
-        core_copy(7, mixed.at[top, heads], mixed.at[bottom, heads]),
-        core_copy(8, mixed.at[bottom, heads], mixed.at[top, heads]),
+        core_copy(7, ffn.at[top, heads], ffn.at[bottom, heads]),
+        core_copy(8, ffn.at[bottom, heads], ffn.at[top, heads]),
     ]
-    normed_two_core = core_copy(9, normed_two.at[top], normed_two.at[bottom])
+    normed_two_core = core_copy(9, normed.at[top], normed.at[bottom])
     ffn_core = core_copy(10, ffn.at[top], ffn.at[bottom])
 
-    outs = []
-    early = []
-
-    def put(source, target):
-        copy = pltpu.make_async_copy(source, target, out_sems.at[len(outs)])
-        copy.start()
-        outs.append(copy)
-        return copy
+    spills = {}
+
+    def put(name, source, target):
+        spills[name] = pltpu.make_async_copy(source, target, out_sems.at[len(spills)])
+        spills[name].start()
 
     stages = ("x", "high", "low", "y")
 
-    def begin(name, k):
+    def fetch(name, k):
         for op in ops[name, k]:
             op.start()
 
-    def tick(t):
+    def bring(t):
         for s, name in enumerate(stages):
             k = t - s
             if 0 <= k < count:
                 for op in ops[name, k]:
                     op.wait_recv()
                 if s < 3:
-                    begin(stages[s + 1], k)
+                    fetch(stages[s + 1], k)
         if t + 3 < count:
-            begin("x", t + 3)
+            fetch("x", t + 3)
         if t == 3:
             out_x.start()
         if t == 8:
@@ -583,17 +629,17 @@
             for op in {1: (out_local,), 2: owns[3:5], 4: owns[5:]}[t]:
                 op.start()
 
-    begin("x", 0)
-    begin("x", 1)
-    begin("x", 2)
+    fetch("x", 0)
+    fetch("x", 1)
+    fetch("x", 2)
     vec_x.start()
     swap_start(0)
     swap_start(1)
     vec_local.start()
     for op in owns[:3]:
         op.start()
-    tick(0)
-    tick(1)
+    bring(0)
+    bring(1)
     vec_x.wait_recv()
     vec_local.wait()
 
@@ -612,18 +658,17 @@
     @pl.loop(0, rows // 64)
     def _(i):
         here = rows_at(i * 64, 64)
-        normed_one[here, :] = norm(tok[here, :].astype(f32), gain_one, bias_one)
+        normed[here, :] = norm(tok[here, :].astype(f32), gain_one, bias_one)
 
     normed_one_core.start()
-    tick(2)
-    tick(3)
-    put(tok, own_out)
+    bring(2)
+    bring(3)
     normed_one_core.wait_recv()
-    put(normed_one, normed_one_out)
+    put("normed_one", normed, normed_spill)
 
     for i in range(3):
         for t in ((4, 5), (6, 7), (8, 9, 10))[i]:
-            tick(t)
+            bring(t)
         owns[i].wait()
         lanes = pl.ds(i * EDGE, EDGE)
         bias = 0.0 if i == 1 else vec[core, 2 + i // 2 : 3 + i // 2, :]
@@ -631,72 +676,64 @@
         @pl.loop(0, 2 * rows // 256)
         def _(r):
             here = rows_at(r * 256, 256)
-            value = jnp.dot(normed_one[here, :], qkv_w[:, lanes], preferred_element_type=f32)
-            qkv[here, lanes] = (value + bias).astype(bf16)
-
-    put(qkv, qkv_out)
-    put(qkv_w, qkv_w_out)
+            value = jnp.dot(normed[here, :], qkv_w[:, lanes], preferred_element_type=f32)
+            wide[here, lanes] = (value + bias).astype(bf16)
+
+    put("qkv", wide.at[:, pl.ds(0, 3 * EDGE)], qkv_spill)
 
     @pl.loop(0, EDGE // 128)
-    def _(pair):
-        attend_pair(qkv, mixed, totals, pair, core * EDGE)
+    def _(two):
+        attend_pair(wide, ffn, tot, two, core * EDGE)
 
         for i in range(5):
 
-            @pl.when(pair == i)
+            @pl.when(two == i)
             def _():
-                tick(11 + i)
-
+                bring(11 + i)
+
+    spills["normed_one"].wait()
+    normed_one_core.wait_send()
     mixed_core[0].start()
     mixed_core[1].start()
-    put(totals, total_out)
-    tick(16)
+    bring(16)
     out_local.wait()
     out_core.wait_recv()
     mixed_core[1].wait_recv()
+    mixed_core[0].wait_recv()
+    put("mixed", ffn, mixed_spill)
     gain_two, bias_two, out_bias = vector(5), vector(6), vector(4)
 
     @pl.loop(0, rows // 128)
     def _(r):
         here = rows_at(r * 128, 128)
-        value = jnp.dot(mixed[here, :], out_w[...], preferred_element_type=f32)
+        value = jnp.dot(ffn[here, :], out_w[...], preferred_element_type=f32)
         value = tok[here, :].astype(f32) + value + out_bias
-        middle[here, :] = value
-        normed_two[here, :] = norm(value, gain_two, bias_two)
-
+        mid[here, :] = value
+        normed[here, :] = norm(value, gain_two, bias_two)
+
+    spills["mixed"].wait()
+    spills["qkv"].wait()
+    for op in mixed_core:
+        op.wait_send()
     normed_two_core.start()
-    mixed_core[0].wait_recv()
-    put(out_w, out_w_out)
-    put(mixed, mixed_out)
-    put(middle, middle_out)
-    tick(17)
+    bring(17)
     normed_two_core.wait_recv()
-    put(normed_two, normed_two_out)
-    waits = {}
+    up_bias = jnp.concatenate([vec[h, pl.ds(8 + core * 2 + i, 1), :] for h in range(2) for i in range(2)], axis=1)
     for i in range(4):
         if i % 2 == 0:
             owns[3 + i // 2].wait()
-        slot = i % 2
-        if i >= 2:
-            for copy in waits[slot]:
-                copy.wait()
-                early.append(copy)
         lanes = pl.ds(i * EDGE, EDGE)
-        bias = vec[i // 2, pl.ds(8 + core * 2 + i % 2, 1), :]
-
-        @pl.loop(0, 2 * rows // 128)
+        bias = up_bias[:, i * EDGE : (i + 1) * EDGE]
+
+        @pl.loop(0, both // 128)
         def _(r):
             here = rows_at(r * 128, 128)
-            up = jnp.dot(normed_two[here, :], up_w[:, lanes], preferred_element_type=f32) + bias
+            up = jnp.dot(normed[here, :], up_w[:, lanes], preferred_element_type=f32) + bias
             cdf = 0.5 * (1.0 + lax.erf(up * 0.7071067811865476))
-            hidden[slot, here, :] = (up * cdf).astype(bf16)
-            slope[slot, here, :] = (cdf + up * jnp.exp(-0.5 * up * up) * 0.3989422804014327).astype(bf16)
-
-        waits[slot] = (
-            put(hidden.at[slot], hidden_out.at[:, lanes]),
-            put(slope.at[slot], slope_out.at[:, lanes]),
-        )
-        if i == 1:
+            wide[here, lanes] = (up * cdf).astype(bf16)
+            grad_up[here, lanes] = (cdf + up * jnp.exp(-0.5 * up * up) * 0.3989422804014327).astype(bf16)
+
+        if i == 0:
             swap_wait(1)
             swap_wait(2)
             weight = scale[0:1, 0:1]
@@ -707,163 +744,26 @@
                 ffn[here, :] = (grad[here, :].astype(f32) * weight).astype(bf16)
 
             ffn_core.start()
-            put(grad, grad_out)
-            put(scale, weight_out)
-            put(vec, vectors_out)
-        for t in ((18,), (19, 20), (21, 22), (23, 24, 25))[i]:
-            tick(t)
-    put(up_w, up_w_out)
+        for t in ((18,), (19, 20), (21,), (22,))[i]:
+            bring(t)
     ffn_core.wait_recv()
-    put(ffn, ffn_out)
-    owns[5].wait()
-    for op in direct:
-        op.wait()
-    put(down_w, down_w_out)
-    for k in range(count):
-        for name in stages:
-            for op in ops[name, k]:
-                op.wait_send()
-    for op in (out_x, out_core, vec_x, normed_one_core, *mixed_core, normed_two_core, ffn_core):
-        op.wait_send()
-    for copy in outs:
-        if not any(copy is other for other in early):
-            copy.wait()
-
-
-def forward(*args):
-    bf16, f32 = jnp.bfloat16, jnp.float32
-    shape = jax.ShapeDtypeStruct
-    rows, width = args[0].shape
-    both = 2 * rows
-    arrays = [
-        ((rows, width), bf16),
-        ((rows, width), bf16),
-        (args[2].shape, f32),
-        ((2,) + args[3].shape, f32),
-        ((width, 3 * EDGE), bf16),
-        ((width, width), bf16),
-        ((width, 4 * EDGE), bf16),
-        ((4 * EDGE, width), bf16),
-        ((both, width), bf16),
-        ((both, 3 * EDGE), bf16),
-        ((both, width), bf16),
-        ((EDGE // HDIM, 1, both), f32),
-        ((rows, width), f32),
-        ((both, width), bf16),
-        ((both, 4 * EDGE), bf16),
-        ((both, 4 * EDGE), bf16),
-        ((both, width), bf16),
-    ]
-    scratch = [pltpu.VMEM(*array) for array in arrays]
-    scratch[14] = scratch[15] = pltpu.VMEM((2, both, EDGE), bf16)
-    dma = pltpu.SemaphoreType.DMA
-    return pl.pallas_call(
-        forward_kernel,
-        in_specs=[ANY] * len(args),
-        out_specs=[ANY] * len(arrays),
-        out_shape=[shape(*array) for array in arrays],
-        scratch_shapes=scratch + [dma((6, 23)), dma((6, 23)), dma((6,)), dma((11,)), dma((11,)), dma((5,)), dma((24,))],
-        compiler_params=pltpu.CompilerParams(
-            collective_id=0, has_side_effects=True, vmem_limit_bytes=60 * 1024 * 1024
-        ),
-        name="forward",
-    )(*args)
-
-
-def attend_back_pair(qkv, totals, keys_acc, values_acc, pair):
-    f32, bf16 = jnp.float32, jnp.bfloat16
-    rows = qkv.shape[0]
-    size = Q_BLOCK // 2
-    lane = lax.broadcasted_iota(jnp.int32, (1, 128), 1)
-    here, key_lanes, value_lanes, grad_lanes = (cols(i * EDGE + pair * 128, 128) for i in range(4))
-    keys = qkv[:, key_lanes]
-    keys_t = keys.T
-    nt = (((1,), (1,)), ((), ()))
-    keys_acc[...] = jnp.zeros_like(keys_acc)
-    values_acc[...] = jnp.zeros_like(values_acc)
-
-    @pl.loop(0, rows // size)
-    def _(block):
-        part = rows_at(block * size, size)
-        queries = qkv[part, here] * jnp.asarray(0.125, bf16)
-        grads = qkv[part, grad_lanes]
-        values = qkv[:, value_lanes]
-        outs = []
-        key_part = value_part = 0.0
-        for head in range(2):
-            own = (lane // HDIM) == head
-            q_own = jnp.where(own, queries, jnp.zeros_like(queries))
-            g_own = jnp.where(own, grads, jnp.zeros_like(grads))
-            scores = lax.dot_general(keys, q_own, nt, preferred_element_type=f32)
-            probs = jnp.exp(scores - totals[2 * pair + head, :, cols(block * size, size)])
-            grad_probs = lax.dot_general(values, g_own, nt, preferred_element_type=f32)
-            delta = jnp.sum(probs * grad_probs, axis=0, keepdims=True)
-            grad_scores = (probs * (grad_probs - delta)).astype(bf16)
-            value_part += jnp.dot(probs.astype(bf16), g_own, preferred_element_type=f32)
-            key_part += jnp.dot(grad_scores, q_own, preferred_element_type=f32)
-            outs.append(jnp.dot(keys_t[head * HDIM : (head + 1) * HDIM, :], grad_scores, preferred_element_type=f32))
-        qkv[part, here] = (jnp.concatenate(outs, axis=0) * 0.125).T.astype(bf16)
-        keys_acc[...] += key_part
-        values_acc[...] += value_part
-
-    qkv[:, key_lanes] = keys_acc[...].astype(bf16)
-    qkv[:, value_lanes] = values_acc[...].astype(bf16)
-
-
-def backward_kernel(
-    own, own_grad, cell_weight, vectors, qkv_w, out_w, up_w, down_w,
-    normed_one, qkv, mixed, totals, middle, normed_two, hidden, slope, ffn,
-    result_ref, input_ref, down_ref, up_ref, out_ref, q_ref, k_ref, v_ref, vec_ref,
-    wide, grad_up, normed, pair_buf, ffn_buf, down_buf, up_buf, part_buf, taken, given, mid, tot, vec, scale, keys_acc, values_acc,
-    blocks, from_x, from_y, from_low, from_high, res, sums,
-    send_sems, recv_sems, store_sems, load_sems, core_send, core_recv, swap_send, swap_recv, swap_local, vec_send, vec_recv, vec_local,
-):
-    f32, bf16 = jnp.float32, jnp.bfloat16
-    at = Spot()
-    x, core = at.x, at.core
-    rows, width = own.shape
-    both = 2 * rows
-    top, bottom = pl.ds(0, rows), pl.ds(rows, rows)
-    nt = (((1,), (1,)), ((), ()))
-    tn = (((0,), (0,)), ((), ()))
-    loads = {}
-
-    def load(name, source, target):
-        copy = pltpu.make_async_copy(source, target, load_sems.at[len(loads)])
-        copy.start()
-        loads[name] = copy
-
-    load("hidden", hidden, wide)
-    load("ffn", ffn, ffn_buf)
-    load("down_w", down_w, down_buf)
-    slopes = [(slope.at[:, pl.ds(i * EDGE, EDGE)], pair_buf.at[:, pl.ds((i % 2) * EDGE, EDGE)]) for i in range(4)]
-    load("slope0", *slopes[0])
-    load("slope1", *slopes[1])
-    load("up_w", up_w, up_buf)
-    load("normed_two", normed_two, normed)
-    load("middle", middle, mid)
-    load("vectors", vectors, vec)
-    load("scale", cell_weight, scale)
-    load("totals", totals, tot)
-    sums[0] = jnp.zeros(sums.shape[1:], f32)
-    at.meet(("x", "core", "diagonal", "y", "low", "high"))
-
-    chunks = []
+
+    pieces = []
     for i in range(2):
         for start in range(0, 2 * EDGE, WIDE):
             target = down_ref.at[rows_at(core * 2 * EDGE + i * EDGE, EDGE), pl.ds(start, WIDE)]
-            chunks.append([(wide, 2 * EDGE, i * EDGE, ffn_buf, start, WIDE, target)])
+            pieces.append([(wide, 2 * EDGE, i * EDGE, ffn, start, WIDE, target)])
     for start in range(0, 4 * EDGE, WIDE):
         target = up_ref.at[:, cols(start // (2 * EDGE) * 2 * EDGE + start + core * 2 * EDGE, WIDE)]
-        chunks.append([(normed, EDGE, 0, grad_up, start, WIDE, target)])
+        pieces.append([(normed, EDGE, 0, grad_up, start, WIDE, target)])
     mixed_rows = pl.ds(EDGE, both)
 
     def out_part(start, width):
         target = out_ref.at[:, cols(core * EDGE + start, width)]
-        return (down_buf.at[mixed_rows], EDGE, 0, ffn_buf, core * EDGE + start, width, target)
+        return (down_w.at[mixed_rows], EDGE, 0, ffn, core * EDGE + start, width, target)
 
     last = EDGE % WIDE
-    chunks += [[out_part(start, WIDE)] for start in range(0, EDGE - last, WIDE)]
+    pieces += [[out_part(start, WIDE)] for start in range(0, EDGE - last, WIDE)]
     for start in range(0, 3 * EDGE, WIDE):
         parts = []
         for i, ref in enumerate((q_ref, k_ref, v_ref)):
@@ -871,16 +771,16 @@
             if first < end:
                 target = ref.at[:, cols(core * EDGE + first - i * EDGE, end - first)]
                 parts.append((normed, EDGE, 0, wide, first, end - first, target))
-        chunks.append(parts)
-    chunks[-1].append(out_part(EDGE - last, last))
-    count = len(chunks)
+        pieces.append(parts)
+    pieces[-1].append(out_part(EDGE - last, last))
+    total_count = len(pieces)
 
     half, quarter, eighth = EDGE // 2, EDGE // 4, EDGE // 8
     y0 = at.y * half
     l0 = y0 + at.low * quarter
     h0 = l0 + at.high * eighth
-    ops = {}
-    for k, parts in enumerate(chunks):
+    sum_ops = {}
+    for k, parts in enumerate(pieces):
         acc, four, slot, sem = k % 6, k % 4, k % 7, k % RING
         hops = (
             ("x", "x", blocks.at[6 + k % 3], from_x.at[four]),
@@ -892,26 +792,26 @@
             ("all_y", "y", res.at[slot, rows_at(y0, half)], res.at[slot, rows_at(y0, half)]),
         )
         for s, (stage, name, source, goal) in enumerate(hops):
-            ops[stage, k] = [at.send(name, source, goal, send_sems.at[s, sem], recv_sems.at[s, sem])]
-        ops["core", k] = []
-        ops["store", k] = []
+            sum_ops[stage, k] = [at.send(name, source, goal, sum_send.at[s, sem], sum_recv.at[s, sem])]
+        sum_ops["core", k] = []
+        sum_ops["store", k] = []
         start = 0
         for s, part in enumerate(parts):
             source = res.at[slot, :, pl.ds(start, part[5])]
-            ops["core", k].append(at.send("core", source, part[6], send_sems.at[7 + s, sem], recv_sems.at[7 + s, sem]))
-            ops["store", k].append(pltpu.make_async_copy(source, part[6], store_sems.at[s, sem]))
+            sum_ops["core", k].append(at.send("core", source, part[6], sum_send.at[7 + s, sem], sum_recv.at[7 + s, sem]))
+            sum_ops["store", k].append(pltpu.make_async_copy(source, part[6], store_sems.at[s, sem]))
             start += part[5]
 
     def begin(stage, k):
-        for op in ops[stage, k]:
+        for op in sum_ops[stage, k]:
             op.start()
 
     def came(stage, k):
-        for op in ops[stage, k]:
+        for op in sum_ops[stage, k]:
             op.wait_recv()
 
     def left_here(stage, k):
-        for op in ops[stage, k]:
+        for op in sum_ops[stage, k]:
             op.wait_send()
 
     def make(k):
@@ -920,7 +820,7 @@
             of = j * x + (1 - j) * (1 - x)
             slot = j * (k % 6) + (1 - j) * (6 + k % 3)
             start = 0
-            for left, stride, left_at, right, right_at, width_now, _ in chunks[k]:
+            for left, stride, left_at, right, right_at, width_now, _ in pieces[k]:
                 lanes = right_at if isinstance(right_at, int) else pl.multiple_of(right_at, 128)
                 product = lax.dot_general(
                     left[:, cols(of * stride + left_at, EDGE)],
@@ -943,26 +843,26 @@
 
     def tick(t):
         k = t
-        if 0 <= k < count:
+        if 0 <= k < total_count:
             came("x", k)
             add(k, 0, EDGE, from_x.at[k % 4], blocks, k % 6)
             begin("y", k)
             if k >= 1:
                 left_here("x", k - 1)
-            if k + 2 < count:
+            if k + 2 < total_count:
                 make(k + 2)
         k = t - 1
-        if 0 <= k < count:
+        if 0 <= k < total_count:
             came("y", k)
             add(k, y0, half, from_y.at[k % 4], blocks, k % 6)
             begin("low", k)
         k = t - 2
-        if 0 <= k < count:
+        if 0 <= k < total_count:
             came("low", k)
             add(k, l0, quarter, from_low.at[k % 4], blocks, k % 6)
             begin("high", k)
         k = t - 3
-        if 0 <= k < count:
+        if 0 <= k < total_count:
             came("high", k)
             add(k, h0, eighth, from_high.at[k % 4], res, k % 7)
             begin("all_high", k)
@@ -970,26 +870,23 @@
                 left_here(stage, k)
         for before, stage, after in ((4, "all_high", "all_low"), (5, "all_low", "all_y"), (6, "all_y", "core")):
             k = t - before
-            if 0 <= k < count:
+            if 0 <= k < total_count:
                 came(stage, k)
                 begin(after, k)
                 if after == "core":
                     begin("store", k)
         k = t - 7
-        if 0 <= k < count:
+        if 0 <= k < total_count:
             came("core", k)
             for stage in ("all_high", "all_low", "all_y", "core"):
                 left_here(stage, k)
-            for op in ops["store", k]:
+            for op in sum_ops["store", k]:
                 op.wait()
 
-    def core_copy(i, source, target):
-        return at.send("core", source, target, core_send.at[i], core_recv.at[i])
-
-    two_copy = core_copy(0, given.at[0], taken.at[0])
-    result_copy = core_copy(1, given.at[1], taken.at[1])
-    attn_copy = core_copy(2, ffn_buf.at[top], ffn_buf.at[bottom])
-    one_copy = core_copy(3, given.at[0], taken.at[0])
+    two_copy = core_copy(11, given.at[0], taken.at[0])
+    result_copy = core_copy(12, given.at[1], taken.at[1])
+    attn_copy = core_copy(13, ffn.at[top], ffn.at[bottom])
+    one_copy = core_copy(14, given.at[0], taken.at[0])
     swaps = []
     for i, target in enumerate((result_ref, input_ref)):
         source = taken.at[1 - i]
@@ -1000,7 +897,7 @@
             )
         )
 
-    def swap(i, act):
+    def swap_back(i, act):
         @pl.when(x != core)
         def _():
             act(swaps[i][0])
@@ -1008,9 +905,6 @@
         @pl.when(x == core)
         def _():
             act(swaps[i][1])
-
-    def vector(i):
-        return jnp.concatenate([vec[0, i : i + 1, :], vec[1, i : i + 1, :]], axis=1)
 
     def add_vector(i, value):
         total = jnp.sum(value, axis=0, keepdims=True)
@@ -1030,36 +924,37 @@
         )
         return standard, back
 
-    loads["hidden"].wait()
-    loads["ffn"].wait()
     make(0)
     make(1)
-    loads["down_w"].wait()
+    for t in (23, 24, 25):
+        bring(t)
+    owns[5].wait()
+    for op in direct:
+        op.wait()
+    normed_two_core.wait_send()
+    loads = {}
+
+    def load(name, source, target):
+        loads[name] = pltpu.make_async_copy(source, target, load_sems.at[len(loads)])
+        loads[name].start()
+
     for i in range(4):
-        loads["slope%d" % i].wait()
         lanes = pl.ds(i * EDGE, EDGE)
-        row = pl.ds(16 + (i // 2) * 4 + core * 2 + i % 2, 1)
+        row = pl.ds(16 + 2 * (core * 2 + i % 2) + i // 2, 1)
 
         @pl.loop(0, both // 256)
         def _(r):
             here = rows_at(r * 256, 256)
-            value = lax.dot_general(ffn_buf[here, :], down_buf[lanes, :], nt, preferred_element_type=f32)
-            value = (value * pair_buf[here, pl.ds((i % 2) * EDGE, EDGE)].astype(f32)).astype(bf16)
+            value = lax.dot_general(ffn[here, :], down_w[lanes, :], nt, preferred_element_type=f32)
+            value = (value * grad_up[here, lanes].astype(f32)).astype(bf16)
             grad_up[here, lanes] = value
             sums[0, row, :] += jnp.sum(value.astype(f32), axis=0, keepdims=True)
 
-        if i < 2:
-            load("slope%d" % (i + 2), *slopes[i + 2])
-        if i == 1:
-            loads["normed_two"].wait()
         tick(i)
-    load("own_grad", own_grad, pair_buf.at[top])
-    load("own", own, pair_buf.at[bottom])
-    loads["up_w"].wait()
 
     @pl.loop(0, rows // 256)
     def _(r):
-        value = lax.dot_general(grad_up[rows_at(rows + r * 256, 256), :], up_buf[...], nt, preferred_element_type=f32)
+        value = lax.dot_general(grad_up[rows_at(rows + r * 256, 256), :], up_w[...], nt, preferred_element_type=f32)
         given[0, rows_at(r * 256, 256), :] = value.astype(bf16)
 
     two_copy.start()
@@ -1067,114 +962,113 @@
 
     @pl.loop(0, rows // 256)
     def _(r):
-        value = lax.dot_general(grad_up[rows_at(r * 256, 256), :], up_buf[...], nt, preferred_element_type=f32)
-        part_buf[rows_at(r * 256, 256), :] = value
+        value = lax.dot_general(grad_up[rows_at(r * 256, 256), :], up_w[...], nt, preferred_element_type=f32)
+        partial_sum[rows_at(r * 256, 256), :] = value
 
     tick(5)
 
     @pl.loop(0, rows // 256)
     def _(r):
-        value = jnp.dot(wide[rows_at(rows + r * 256, 256), :], down_buf[...], preferred_element_type=f32)
+        value = jnp.dot(wide[rows_at(rows + r * 256, 256), :], down_w[...], preferred_element_type=f32)
         given[1, rows_at(r * 256, 256), :] = value.astype(bf16)
 
     tick(6)
     tick(7)
     result_copy.start()
     two_copy.wait_recv()
-    for name in ("middle", "vectors", "scale", "own_grad", "totals"):
-        loads[name].wait()
     result_copy.wait_recv()
-    down_bias, gain_two, gain_one = vector(7), vector(5), vector(0)
+    down_bias = vector(7)
 
     @pl.loop(0, rows // 128)
     def _(r):
         here = rows_at(r * 128, 128)
-        value = jnp.dot(wide[here, :], down_buf[...], preferred_element_type=f32)
+        value = jnp.dot(wide[here, :], down_w[...], preferred_element_type=f32)
         value = mid[here, :] + value + taken[1, here, :].astype(f32) + down_bias
         taken[1, here, :] = value.astype(bf16)
 
-    swap(0, lambda copy: copy.start())
-    load("qkv", qkv, wide.at[:, pl.ds(0, 3 * EDGE)])
-    load("mixed", mixed, down_buf.at[mixed_rows])
-    load("out_w", out_w.at[rows_at(core * EDGE, EDGE)], down_buf.at[pl.ds(0, EDGE)])
-    load("qkv_w", qkv_w, up_buf.at[:, pl.ds(0, 3 * EDGE)])
+    swap_back(0, lambda copy: copy.start())
+    for k in range(count):
+        for name in stages:
+            for op in ops[name, k]:
+                op.wait_send()
+    for op in (ffn_core, out_x, out_core, vec_x):
+        op.wait_send()
+    load("qkv", qkv_spill, wide.at[:, pl.ds(0, 3 * EDGE)])
+    load("mixed", mixed_spill, down_w.at[mixed_rows])
     weight = scale[0:1, 0:1]
     tick(8)
 
     @pl.loop(0, rows // 32)
     def _(r):
         here = rows_at(r * 32, 32)
-        add_vector(7, ffn_buf[here, :].astype(f32))
-        grad_normed = part_buf[here, :] + taken[0, here, :].astype(f32)
+        add_vector(7, ffn[here, :].astype(f32))
+        grad_normed = partial_sum[here, :] + taken[0, here, :].astype(f32)
         standard, back = norm_back(mid[here, :], grad_normed, gain_two)
         add_vector(5, grad_normed * standard)
         add_vector(6, grad_normed)
-        value = pair_buf[here, :].astype(f32) * weight + back
+        value = pair[here, :].astype(f32) * weight + back
         mid[here, :] = value
         value = value.astype(bf16)
-        ffn_buf[here, :] = value
+        ffn[here, :] = value
         add_vector(4, value.astype(f32))
 
     attn_copy.start()
     two_copy.wait_send()
     tick(9)
-    loads["out_w"].wait()
     attn_copy.wait_recv()
 
     @pl.loop(0, both // 256)
     def _(r):
         here = rows_at(r * 256, 256)
-        value = lax.dot_general(ffn_buf[here, :], down_buf[0:EDGE, :], nt, preferred_element_type=f32)
+        value = lax.dot_general(ffn[here, :], out_w[rows_at(core * EDGE, EDGE), :], nt, preferred_element_type=f32)
         wide[here, pl.ds(3 * EDGE, EDGE)] = value.astype(bf16)
 
     loads["qkv"].wait()
     tick(10)
 
     @pl.loop(0, EDGE // 128)
-    def _(pair):
-        attend_back_pair(wide, tot, keys_acc, values_acc, pair)
+    def _(two):
+        attend_back_pair(wide, tot, keys_acc, values_acc, two)
         for i in range(5):
 
-            @pl.when(pair == i)
+            @pl.when(two == i)
             def _():
                 tick(11 + i)
 
-    loads["qkv_w"].wait()
     weights = pl.ds(0, 3 * EDGE)
 
     @pl.loop(0, rows // 256)
     def _(r):
         value = lax.dot_general(
-            wide[rows_at(rows + r * 256, 256), weights], up_buf[:, weights], nt, preferred_element_type=f32
+            wide[rows_at(rows + r * 256, 256), weights], qkv_w[...], nt, preferred_element_type=f32
         )
         given[0, rows_at(r * 256, 256), :] = value.astype(bf16)
 
     one_copy.start()
     tick(16)
     tick(17)
-    load("normed_one", normed_one, normed)
+    load("normed_one", normed_spill, normed)
     loads["mixed"].wait()
 
     @pl.loop(0, rows // 256)
     def _(r):
-        value = lax.dot_general(wide[rows_at(r * 256, 256), weights], up_buf[:, weights], nt, preferred_element_type=f32)
-        part_buf[rows_at(r * 256, 256), :] = value
+        value = lax.dot_general(wide[rows_at(r * 256, 256), weights], qkv_w[...], nt, preferred_element_type=f32)
+        partial_sum[rows_at(r * 256, 256), :] = value
 
     tick(18)
     one_copy.wait_recv()
-    loads["own"].wait()
 
     @pl.loop(0, rows // 32)
     def _(r):
         here = rows_at(r * 32, 32)
-        tok = pair_buf[rows_at(rows + r * 32, 32), :].astype(f32)
-        grad_normed = part_buf[here, :] + taken[0, here, :].astype(f32)
+        tok = pair[rows_at(rows + r * 32, 32), :].astype(f32)
+        grad_normed = partial_sum[here, :] + taken[0, here, :].astype(f32)
         standard, back = norm_back(tok, grad_normed, gain_one)
         add_vector(0, grad_normed * standard)
         add_vector(1, grad_normed)
         taken[0, here, :] = (mid[here, :] + back).astype(bf16)
 
-    swap(1, lambda copy: copy.start())
+    swap_back(1, lambda copy: copy.start())
     tick(19)
     loads["normed_one"].wait()
 
@@ -1189,7 +1083,7 @@
     names = ("x", "core", "y", "low", "high")
     vec_ops = [at.send(name, sums.at[i], sums.at[6 + i], vec_send.at[i], vec_recv.at[i]) for i, name in enumerate(names)]
     vec_ops[0].start()
-    for t in range(20, count + 7):
+    for t in range(20, total_count + 7):
         tick(t)
         if t < 25:
             i = t - 20
@@ -1197,17 +1091,17 @@
             sums[i + 1] = sums[i] + sums[6 + i]
             if i < 4:
                 vec_ops[i + 1].start()
-    vec_store = pltpu.make_async_copy(sums.at[5], vec_ref, vec_local.at[0])
+    vec_store = pltpu.make_async_copy(sums.at[5], vec_ref, vec_store_sem.at[0])
     vec_store.start()
     vec_store.wait()
     for op in (result_copy, attn_copy, one_copy, *vec_ops):
         op.wait_send()
-    swap(0, lambda copy: copy.wait())
-    swap(1, lambda copy: copy.wait())
-    left_here("x", count - 1)
-
-
-def backward(*args):
+    swap_back(0, lambda copy: copy.wait())
+    swap_back(1, lambda copy: copy.wait())
+    left_here("x", total_count - 1)
+
+
+def layer(*args):
     bf16, f32 = jnp.bfloat16, jnp.float32
     rows, width = args[0].shape
     both = 2 * rows
@@ -1221,22 +1115,27 @@
         ((EDGE, width), bf16),
         ((EDGE, width), bf16),
         ((24, EDGE), f32),
+        ((both, width), bf16),
+        ((both, 3 * EDGE), bf16),
+        ((both, width), bf16),
     ]
     scratch = [
+        ((both, width), bf16),
+        ((8, 128), f32),
+        ((2, 16, EDGE), f32),
+        ((width, 3 * EDGE), bf16),
+        ((width, width), bf16),
+        ((width, 4 * EDGE), bf16),
+        ((4 * EDGE, width), bf16),
+        ((both, width), bf16),
         ((both, 4 * EDGE), bf16),
         ((both, 4 * EDGE), bf16),
         ((both, width), bf16),
-        ((both, width), bf16),
-        ((both, width), bf16),
-        ((4 * EDGE, width), bf16),
-        ((width, 4 * EDGE), bf16),
+        ((rows, width), f32),
         ((rows, width), f32),
         ((2, rows, width), bf16),
         ((2, rows, width), bf16),
-        ((rows, width), f32),
         ((EDGE // HDIM, 1, both), f32),
-        ((2, 16, EDGE), f32),
-        ((8, 128), f32),
         ((both, 128), f32),
         ((both, 128), f32),
         ((9, EDGE, WIDE), bf16),
@@ -1246,21 +1145,44 @@
         ((4, EDGE // 8, WIDE), bf16),
         ((7, EDGE, WIDE), bf16),
         ((11, 24, EDGE), f32),
+        ((8, 128), f32),
+        ((16, EDGE), f32),
     ]
     dma = pltpu.SemaphoreType.DMA
+    sizes = [(6, 23), (6, 23), (6,), (15,), (15,), (5,), (3,), (9, RING), (9, RING), (2, RING), (3,)]
+    sizes += [(2,), (2,), (2,), (5,), (5,), (1,)]
     return pl.pallas_call(
-        backward_kernel,
-        in_specs=[ANY] * len(args),
+        layer_kernel,
+        in_specs=[ANY] * 2 + [pl.BlockSpec(memory_space=pltpu.SMEM)] + [ANY] * 6 + [pl.BlockSpec(memory_space=pltpu.VMEM)] * 9,
         out_specs=[ANY] * len(outs),
         out_shape=[jax.ShapeDtypeStruct(*out) for out in outs],
-        scratch_shapes=[pltpu.VMEM(*array) for array in scratch]
-        + [dma((9, RING)), dma((9, RING)), dma((2, RING)), dma((20,)), dma((4,)), dma((4,))]
-        + [dma((2,)), dma((2,)), dma((2,)), dma((5,)), dma((5,)), dma((1,))],
+        scratch_shapes=[pltpu.VMEM(*array) for array in scratch] + [dma(size) for size in sizes],
         compiler_params=pltpu.CompilerParams(
-            collective_id=1, has_side_effects=True, vmem_limit_bytes=64 * 1024 * 1024
+            collective_id=0, has_side_effects=True, vmem_limit_bytes=64 * 1024 * 1024
         ),
-        name="backward",
+        name="layer",
     )(*args)
+
+
+def widen_kernel(*refs):
+    half = len(refs) // 2
+    for source, target in zip(refs[:half], refs[half:]):
+        target[...] = source[...].astype(target.dtype)
+
+
+def widen(*arrays):
+    steps = 8
+    specs = [pl.BlockSpec((a.shape[0] // steps, a.shape[1]), lambda i: (i, 0)) for a in arrays]
+    types = [jnp.float32] * (len(arrays) - 2) + [jnp.bfloat16] * 2
+    return pl.pallas_call(
+        widen_kernel,
+        grid=(steps,),
+        in_specs=specs,
+        out_specs=specs,
+        out_shape=[jax.ShapeDtypeStruct(a.shape, kind) for a, kind in zip(arrays, types)],
+        compiler_params=pltpu.CompilerParams(vmem_limit_bytes=64 * 1024 * 1024),
+        name="widen",
+    )(*arrays)
 
 
 def tuned(
@@ -1287,42 +1209,47 @@
     x = lax.axis_index("seq")
     head_width = tokens.shape[2] // 2
 
-    vectors = (first_gain, first_bias, query_bias, value_bias, output_bias, second_gain, second_bias, down_bias)
-    vectors = jnp.concatenate([jnp.stack(vectors), up_bias.reshape(4, -1), jnp.zeros((4, head_width), bf16)])
-    cell_weight = jnp.broadcast_to(jnp.sqrt(query_counts.astype(f32) / 1000.0), (8, 128))
-    state = forward(
+    result, input_grad, down, up, out, query, key, value, sums, *_ = layer(
         tokens[0],
         out_grad[0],
-        cell_weight,
-        vectors.astype(f32),
+        query_counts,
         query_weight,
         key_weight,
         value_weight,
         output_weight,
         up_weight,
         down_weight,
-    )
-    result, input_grad, down, up, out, query, key, value, sums = backward(*state)
-    short = lax.dynamic_index_in_dim(sums[:16].reshape(8, 2, head_width), x, 1, keepdims=False)
-    up_sum = lax.dynamic_slice_in_dim(sums, 16 + 4 * x, 4, 0).reshape(-1)
+        first_gain,
+        first_bias,
+        query_bias,
+        value_bias,
+        output_bias,
+        second_gain,
+        second_bias,
+        down_bias,
+        up_bias,
+    )
+    out, query, key, value, up, down, result, input_grad = widen(out, query, key, value, up, down, result, input_grad)
+    sums = lax.dynamic_index_in_dim(sums.reshape(12, 2, head_width), x, 1, keepdims=False)
+    up_sum = sums[8:].reshape(-1)
     return (
         result[None],
         input_grad[None],
-        short[0],
-        short[1],
-        query.astype(f32),
-        short[2],
-        key.astype(f32),
-        value.astype(f32),
-        short[3],
-        out.astype(f32),
-        short[4],
-        short[5],
-        short[6],
-        up.astype(f32),
+        sums[0],
+        sums[1],
+        query,
+        sums[2],
+        key,
+        value,
+        sums[3],
+        out,
+        sums[4],
+        sums[5],
+        sums[6],
+        up,
         up_sum,
-        down.astype(f32),
-        short[7],
+        down,
+        sums[7],
     )
 
 

time: 477 us -> 453 us (0.950)
  other arithmetic: 24.2 us -> 0 us
  Pallas kernels: 432 us -> 441 us
  local copies, waits for them, and re-layouts: 10.3 us -> 2.19 us
    convert_element_type x7 -> x0, other arithmetic: 24.2 us -> none  [the longest x1 9.74 us: tuned(): up.astype(f32)]
    pallas_call x2, Pallas kernels: 432 us -> 441 us  [the longest x1 418 us: layer(): pl.pallas_call(layer_kernel, in_specs=[ANY] * 2 + [pl.BlockSpec(memory_sp...]
    another operation x8 -> x0, local copies, waits for them, and re-layouts: 5.48 us -> none  [tuned(): jnp.stack(vectors)]
where the time goes in v6:
time: 453 us; the launch traced here: 445 us
  Pallas kernels  441 us (97%)
    pallas_call x1, Pallas kernels, layer(): pl.pallas_call(layer_kernel, in_specs=[ANY] * 2 + [pl.BlockSpec(memory_sp...  418 us
    pallas_call x1, Pallas kernels, widen(): pl.pallas_call(widen_kernel, grid=(steps,), in_specs=specs, out_specs=spe...  22.6 us

profile of v6, /device:TPU:0, one launch (start us, length us, event | category | flops | bytes accessed | tf_op | source)
XLA Modules:
  0.0 444.7 jit_solution(7594120973848432299)
XLA Ops:
  1.3 418.1 %layer.1 = (bf16[512,1280]{1,0:T(8,128)(2,1)}, bf16[512,1280]{1,0:T(8,128)(2,1)}, bf16[2560,1280]{1,0:T(8,128)(2,1)}, bf16[640,5120]{1,0:T(8,128)(2,1)}, bf16[64...) custom-call(bf16[512,1280]{1,0:T(8,128)(2,1)} %bitcast.4, ...), custom_call_target="tpu_custom_call" | custom-call | tf_op jit(solution)/shard_map/layer/pallas_call | solution.py:1154
  419.4 0.9 reshape.58
  420.3 0.7 dynamic-slice_reduce_fusion.1
  421.0 0.6 reshape.59
  421.6 22.6 %widen.1 = (f32[640,1280]{1,0:T(8,128)}, f32[640,1280]{1,0:T(8,128)}, f32[640,1280]{1,0:T(8,128)}, f32[640,1280]{1,0:T(8,128)}, f32[640,5120]{1,0:T(8,128)}, /*i...) custom-call(bf16[640,1280]{1,0:T(8,128)(2,1)} %get-tuple-element.34.refs_0_, ...), custom_call_target="tpu_custom_call" | custom-call | tf_op jit(solution)/shard_map/widen/pallas_call | solution.py:1177
  (1 shorter events, 0.0 us)

commit v7 on v6

--- a/solution.py
+++ b/solution.py
@@ -1171,7 +1171,7 @@
 
 
 def widen(*arrays):
-    steps = 8
+    steps = 4
     specs = [pl.BlockSpec((a.shape[0] // steps, a.shape[1]), lambda i: (i, 0)) for a in arrays]
     types = [jnp.float32] * (len(arrays) - 2) + [jnp.bfloat16] * 2
     return pl.pallas_call(

time: 453 us -> 451 us (level)
  no operation moved by 1% of the time
where the time goes in v7:
time: 451 us; the launch traced here: 442 us
  Pallas kernels  438 us (97%)
    pallas_call x1, Pallas kernels, layer(): pl.pallas_call(layer_kernel, in_specs=[ANY] * 2 + [pl.BlockSpec(memory_sp...  418 us
    pallas_call x1, Pallas kernels, widen(): pl.pallas_call(widen_kernel, grid=(steps,), in_specs=specs, out_specs=spe...  20 us

profile of v7, /device:TPU:0, one launch (start us, length us, event | category | flops | bytes accessed | tf_op | source)
XLA Modules:
  0.0 442.0 jit_solution(18394480457088021293)
XLA Ops:
  1.3 418.1 %layer.1 = (bf16[512,1280]{1,0:T(8,128)(2,1)}, bf16[512,1280]{1,0:T(8,128)(2,1)}, bf16[2560,1280]{1,0:T(8,128)(2,1)}, bf16[640,5120]{1,0:T(8,128)(2,1)}, bf16[64...) custom-call(bf16[512,1280]{1,0:T(8,128)(2,1)} %bitcast.4, ...), custom_call_target="tpu_custom_call" | custom-call | tf_op jit(solution)/shard_map/layer/pallas_call | solution.py:1154
  419.4 0.9 reshape.58
  420.3 0.7 dynamic-slice_reduce_fusion.1
  421.0 0.6 reshape.59
  421.6 20.0 %widen.1 = (f32[640,1280]{1,0:T(8,128)}, f32[640,1280]{1,0:T(8,128)}, f32[640,1280]{1,0:T(8,128)}, f32[640,1280]{1,0:T(8,128)}, f32[640,5120]{1,0:T(8,128)}, /*i...) custom-call(bf16[640,1280]{1,0:T(8,128)(2,1)} %get-tuple-element.34.refs_0_, ...), custom_call_target="tpu_custom_call" | custom-call | tf_op jit(solution)/shard_map/widen/pallas_call | solution.py:1177
  (1 shorter events, 0.0 us)

commit v8 on v7

--- a/solution.py
+++ b/solution.py
@@ -614,8 +614,8 @@
                     op.wait_recv()
                 if s < 3:
                     fetch(stages[s + 1], k)
-        if t + 3 < count:
-            fetch("x", t + 3)
+        for k in range(8 + 5 * t, min(count, 13 + 5 * t)):
+            fetch("x", k)
         if t == 3:
             out_x.start()
         if t == 8:
@@ -629,9 +629,8 @@
             for op in {1: (out_local,), 2: owns[3:5], 4: owns[5:]}[t]:
                 op.start()
 
-    fetch("x", 0)
-    fetch("x", 1)
-    fetch("x", 2)
+    for k in range(8):
+        fetch("x", k)
     vec_x.start()
     swap_start(0)
     swap_start(1)

time: 451 us -> 464 us (1.029)
  Pallas kernels: 438 us -> 451 us
    pallas_call x1, Pallas kernels: 418 us -> 431 us  [layer(): pl.pallas_call(layer_kernel, in_specs=[ANY] * 2 + [pl.BlockSpec(memory_sp...]
where the time goes in v8:
time: 464 us; the launch traced here: 455 us
  Pallas kernels  451 us (97%)
    pallas_call x1, Pallas kernels, layer(): pl.pallas_call(layer_kernel, in_specs=[ANY] * 2 + [pl.BlockSpec(memory_sp...  431 us
    pallas_call x1, Pallas kernels, widen(): pl.pallas_call(widen_kernel, grid=(steps,), in_specs=specs, out_specs=spe...  20 us

profile of v8, /device:TPU:0, one launch (start us, length us, event | category | flops | bytes accessed | tf_op | source)
XLA Modules:
  0.0 455.0 jit_solution(8315420500912744269)
XLA Ops:
  1.3 431.0 %layer.1 = (bf16[512,1280]{1,0:T(8,128)(2,1)}, bf16[512,1280]{1,0:T(8,128)(2,1)}, bf16[2560,1280]{1,0:T(8,128)(2,1)}, bf16[640,5120]{1,0:T(8,128)(2,1)}, bf16[64...) custom-call(bf16[512,1280]{1,0:T(8,128)(2,1)} %bitcast.4, ...), custom_call_target="tpu_custom_call" | custom-call | tf_op jit(solution)/shard_map/layer/pallas_call | solution.py:1153
  432.3 0.9 reshape.58
  433.3 0.7 dynamic-slice_reduce_fusion.1
  433.9 0.6 reshape.59
  434.5 20.0 %widen.1 = (f32[640,1280]{1,0:T(8,128)}, f32[640,1280]{1,0:T(8,128)}, f32[640,1280]{1,0:T(8,128)}, f32[640,1280]{1,0:T(8,128)}, f32[640,5120]{1,0:T(8,128)}, /*i...) custom-call(bf16[640,1280]{1,0:T(8,128)(2,1)} %get-tuple-element.34.refs_0_, ...), custom_call_target="tpu_custom_call" | custom-call | tf_op jit(solution)/shard_map/widen/pallas_call | solution.py:1176
  (1 shorter events, 0.0 us)
